TPU v7x, 32 devices: a whole 2x2x4 slice. The times are simulated.
32 devices in a mesh: groups: 2 (over x), cells: 16 (over z, y, core).
Axes of the slice: x: 2, y: 2, z: 4, core: 2. Of those that a mesh axis runs over, the one named last changes fastest.
Arguments:
- basis: bfloat16 [512, 64, 8, 128], P(None, ('groups', 'cells')), parts along dimension 1, may hold values from -6 to 6
- face_speed: float32 [2, 3, 64, 8, 128], P(None, None, ('groups', 'cells')), parts along dimension 2, may hold values from 0.1 to 2
- face_diffusion: float32 [2, 3, 64, 8, 128], P(None, None, ('groups', 'cells')), parts along dimension 2, may hold values from 0.05 to 1
- upwind_flag: int32 [2, 3, 64, 8, 128], P(None, None, ('groups', 'cells')), parts along dimension 2, may hold values 0 or 1
- reaction: float32 [2, 64, 8, 128], P(None, ('groups', 'cells')), parts along dimension 1, may hold values from -2 to 2
- sample_cell: int32 [32, 16, 2], P(('groups', 'cells')), parts along dimension 0, may hold values from 0 to 2047
- sample_count: int32 [32, 16], P(('groups', 'cells')), parts along dimension 0, may hold values from 1 to 2, as said below
Outputs:
- galerkin: float32 [1024, 2, 128], P(('groups', 'cells')), parts along dimension 0
- sample_rows: bfloat16 [32, 16, 2, 9, 128], P(('groups', 'cells')), parts along dimension 0
There are 2 independent parts, one for each index of `groups`. A program takes and returns all parts, laid end to end along the dimension named above; each array names one. Nothing has to cross between parts.
Inputs may be any that keep to these rules, and one draw needn't show every extreme that they name: `sample_count`: in every draw some owner receives 2 live slots from every holding device.
All inputs are finite; a program needn't handle non-finite values. No bound on the sum of `upwind_flag` on one device may be relied on, other than what follows from the above.
Results may differ from a plain program's by a relative error of at most 0.0025.
Values may be sent and summed in bfloat16 or wider, within the bound.
No kernel may reach another device: no remote copies, remote signals or barrier semaphores. Data moves between devices by JAX's collectives and lax.ppermute only.
A program may use at most 64 MiB of HBM per device.

v0:
```python
import jax
import jax.numpy as jnp
from jax import lax
from jax.sharding import PartitionSpec as P

MB = 128


def with_halo(value, sides, width):
    for axis, dim in sides:
        size, length = (lax.axis_size(axis), value.shape[dim])
        up = [(i, (i + 1) % size) for i in range(size - 1)]
        down = [(j, i) for i, j in up]
        last = lax.slice_in_dim(value, length - width, length, axis=dim)
        first = lax.slice_in_dim(value, 0, width, axis=dim)
        before = lax.ppermute(last, axis, up)
        after = lax.ppermute(first, axis, down)
        value = jnp.concatenate([before, value, after], axis=dim)
    return value


def from_behind(value, axis, by):
    size = lax.axis_size(axis)
    pairs = [(i, i + by) for i in range(size) if 0 <= i + by < size]
    return lax.ppermute(value, axis, pairs)


def high_flux(state, neighbour, speed_face, diff_face, upwind_face):
    forward = upwind_face == 1
    signed = jnp.where(forward, speed_face, -speed_face)
    upstream = jnp.where(forward, state, neighbour)
    return signed * upstream - diff_face * (neighbour - state)


def next_cells(state, axis_pos):
    zero_layer = jnp.zeros_like(lax.slice_in_dim(state, 0, 1, axis=axis_pos))
    upper_part = lax.slice_in_dim(state, 1, state.shape[axis_pos], axis=axis_pos)
    return jnp.concatenate([upper_part, zero_layer], axis=axis_pos)


def lower_faces(fluxes, axis_pos):
    zero_layer = jnp.zeros_like(lax.slice_in_dim(fluxes, 0, 1, axis=axis_pos))
    lower_part = lax.slice_in_dim(fluxes, 0, fluxes.shape[axis_pos] - 1, axis=axis_pos)
    return jnp.concatenate([zero_layer, lower_part], axis=axis_pos)


def shards(basis, face_speed, face_diffusion, upwind_flag, reaction, sample_cell, sample_count):
    modes = basis.shape[0]
    layers, width_y, width_z = (basis.shape[1], basis.shape[2], basis.shape[3])
    params = face_speed.shape[0]
    devices = lax.axis_size("cells")
    slab_cells = layers * width_y * width_z
    block_bf = basis[:MB]
    rimmed = with_halo(block_bf, (("cells", 1),), 1)
    rimmed_f = rimmed.astype(jnp.float32)
    state = rimmed_f[:, 1:-1]
    upper_x = []
    for param in range(params):
        upper_x.append(
            high_flux(
                state,
                rimmed_f[:, 2:],
                face_speed[param, 0],
                face_diffusion[param, 0],
                upwind_flag[param, 0],
            )
        )
    last_flag = upwind_flag[:, 0, -1] == 1
    last_speed = face_speed[:, 0, -1]
    signed_last = jnp.where(last_flag, last_speed, -last_speed)
    signed_prev, diff_prev = from_behind((signed_last, face_diffusion[:, 0, -1]), "cells", 1)
    below = rimmed_f[:, 0]
    above = rimmed_f[:, 1]
    first_faces = []
    for param in range(params):
        upstream = jnp.where(signed_prev[param] > 0, below, above)
        first_faces.append(signed_prev[param] * upstream - diff_prev[param] * (above - below))
    applied_list = []
    for param in range(params):
        upper = upper_x[param]
        lower = jnp.concatenate([first_faces[param][:, None], upper[:, :-1]], axis=1)
        result = reaction[param] * state + (upper - lower)
        for axis_d in range(1, 3):
            neighbour = next_cells(state, axis_d + 1)
            upper_d = high_flux(
                state,
                neighbour,
                face_speed[param, axis_d],
                face_diffusion[param, axis_d],
                upwind_flag[param, axis_d],
            )
            result = result + (upper_d - lower_faces(upper_d, axis_d + 1))
        applied_list.append(result.astype(jnp.bfloat16))
    volume = 1.0 / (layers * devices * width_y * width_z)
    basis_flat = basis.reshape(modes, slab_cells)
    applied_flat = jnp.stack(applied_list).reshape(params * MB, slab_cells)
    own_rows = modes // devices
    terms = lax.dot_general(
        basis_flat, applied_flat, (((1,), (1,)), ((), ())), preferred_element_type=jnp.float32
    )
    summed = lax.psum(terms.reshape(modes, params, MB), "cells")
    mine = lax.dynamic_slice_in_dim(summed, lax.axis_index("cells") * own_rows, own_rows, 0)
    galerkin = volume * mine
    local_cell = sample_cell[0]
    x_cell = local_cell // (width_y * width_z)
    y_cell = local_cell // width_z % width_y
    z_cell = local_cell % width_z
    padded = jnp.pad(rimmed, ((0, 0), (0, 0), (1, 1), (1, 1)))
    offsets = [(0, 0, 0), (-1, 0, 0), (1, 0, 0), (0, -1, 0), (0, 1, 0), (0, 0, -1), (0, 0, 1)]
    rows_list = [applied[:, x_cell, y_cell, z_cell] for applied in applied_list]
    for shift_x, shift_y, shift_z in offsets:
        rows_list.append(
            padded[:, x_cell + 1 + shift_x, y_cell + 1 + shift_y, z_cell + 1 + shift_z]
        )
    stacked = jnp.transpose(jnp.stack(rows_list), (2, 3, 0, 1))
    slots = lax.broadcasted_iota(jnp.int32, local_cell.shape, 1)
    live = slots < sample_count[0][:, None]
    payload = jnp.where(live[:, :, None, None], stacked, jnp.zeros_like(stacked))
    received = lax.all_to_all(payload, "cells", split_axis=0, concat_axis=0, tiled=True)
    return (galerkin, received[None])


def solution(mesh):
    return jax.shard_map(
        shards,
        mesh=mesh,
        in_specs=(
            P(None, ("groups", "cells"), None, None),
            P(None, None, ("groups", "cells"), None, None),
            P(None, None, ("groups", "cells"), None, None),
            P(None, None, ("groups", "cells"), None, None),
            P(None, ("groups", "cells"), None, None),
            P(("groups", "cells"), None, None),
            P(("groups", "cells"), None),
        ),
        out_specs=(
            P(("groups", "cells"), None, None),
            P(("groups", "cells"), None, None, None, None),
        ),
        check_vma=False,
    )
```

profile of v0, /device:TPU:0, one launch (start us, length us, event | category | flops | bytes accessed | tf_op | source)
XLA Modules:
  0.0 157.0 jit_solution(11013117581368692537)
XLA Ops:
  7.3 0.7 slice_bitcast_fusion.6
  8.0 2.3 %collective-permute-start.3 = (f32[2,8,128]{2,1,0:T(8,128)S(1)}, f32[2,8,128]{2,1,0:T(8,128)S(1)}, u32[]{:S(2)}, u32[]{:S(2)}) collective-permute-start(f32[2,8,128]{2,1,0:T(8,128)S(1)} %slice_bitcast_fusion.6), channel_id=1, source_target_pairs={{0,1},{1,2},{2,3},{3,4},{4,5},{5,6},{6,7},{7,8},{8,9},{9,10},{10,1... | collective-permute-start | bytes 24584 | tf_op jit(solution)/shard_map/ppermute | solution.py:25
  10.4 1.5 negate_select_fusion.4
  11.8 4.5 %collective-permute-start.2 = (f32[2,8,128]{2,1,0:T(8,128)S(1)}, f32[2,8,128]{2,1,0:T(8,128)S(1)}, u32[]{:S(2)}, u32[]{:S(2)}) collective-permute-start(f32[2,8,128]{2,1,0:T(8,128)S(1)} %get-tuple-element.36), channel_id=1, source_target_pairs={{0,1},{1,2},{2,3},{3,4},{4,5},{5,6},{6,7},{7,8},{8,9},{9,10},{10,1... | collective-permute-start | bytes 24584 | tf_op jit(solution)/shard_map/ppermute | solution.py:25
  16.4 1.1 fusion.68
  17.4 0.2 copy.52
  17.7 1.3 collective-permute-start.1
  19.0 0.2 copy.50
  19.2 3.0 %collective-permute-start = (bf16[128,1,8,128]{0,3,2,1:T(8,128)(2,1)S(1)}, bf16[128,1,8,128]{0,3,2,1:T(8,128)(2,1)S(1)}, u32[]{:S(2)}, u32[]{:S(2)}) collective-permute-start(bf16[128,1,8,128]{0,3,2,1:T(8,128)(2,1)S(1)} %copy.50), channel_id=1, source_target_pairs={{0,1},{1,2},{2,3},{3,4},{4,5},{5,6},{6,7},{7,8},{8,9},{9,10},{10,1... | collective-permute-start | bytes 786440 | tf_op jit(solution)/shard_map/ppermute | solution.py:16
  22.3 0.6 slice_bitcast_fusion.5
  23.0 0.6 slice_bitcast_fusion.8
  23.6 0.7 iota_compare_fusion
  24.3 0.1 copy.48
  24.3 0.1 reshape.593
  24.4 0.1 copy.46
  24.5 0.1 reshape.587
  24.6 0.1 copy.40
  24.7 0.1 reshape.569
  24.8 0.1 copy.42
  24.9 0.1 reshape.575
  25.0 0.1 copy.44
  25.1 0.1 reshape.581
  25.1 0.1 copy.36
  25.2 0.1 reshape.557
  25.3 0.1 copy.35
  25.4 0.1 reshape.545
  25.5 0.1 copy.38
  25.6 0.1 reshape.563
  25.7 0.5 copy.51
  26.2 0.6 slice_bitcast_fusion.12
  26.8 0.6 broadcast_compare_fusion.1
  27.4 0.6 slice_bitcast_fusion.11
  28.0 0.2 pad_maximum_fusion
  28.2 1.0 slice.211
  29.2 1.1 slice.213
  30.2 0.8 copy.54
  31.1 0.5 pad.10.clone
  31.5 0.8 gather_fusion.8
  32.3 0.8 gather_fusion.7
  33.1 0.8 gather_fusion.6
  33.8 0.8 gather_fusion.5
  34.6 0.8 gather_fusion.4
  35.3 0.8 gather_fusion.3
  36.1 0.8 gather_fusion.2
  36.9 5.8 %multiply_subtract_fusion.2 = (f32[128,2,8,128]{0,3,2,1:T(8,128)S(1)}, f32[128,2,8,128]{0,3,2,1:T(8,128)S(1)}, f32[128,2,8,128]{0,3,2,1:T(8,128)S(1)}) fusion(f32[128,2,8,127]{0,3,2,1:T(8,128)} %slice.213, f32[128,4,8,128]{0,3,2,1:T(8,128)S(1)} %get-tuple-element.31, f32[2,8,128]{2,1,0:T(8,128)} %get-tuple-element.45, ...), kind=kLoop, calls=%fused_computation.33 | loop fusion | flops 3670016 | bytes 6338560 | tf_op jit(solution)/shard_map/sub | solution.py:32
  42.9 2.8 %fusion.4 = (f32[128,2,8,128]{0,3,2,1:T(8,128)S(1)}, f32[128,2,8,128]{0,3,2,1:T(8,128)S(1)}, f32[128,2,8,128]{0,3,2,1:T(8,128)S(1)}) fusion(f32[128,2,7,128]{0,3,2,1:T(8,128)S(1)} %copy-done, f32[128,4,8,128]{0,3,2,1:T(8,128)S(1)} %get-tuple-element.31, f32[2,8,128]{2,1,0:T(8,128)S(1)} %get-tuple-element.43, f32[2,8,128]{2,1,0:T(8,128)S(1)} %get-tuple-element.6, ...), kind=kLoop, calls=%fused_computation.16 | loop fusion | flops 3670016 | bytes 6215680 | tf_op jit(solution)/shard_map/sub | solution.py:32
  45.7 0.1 slice.212
  45.8 0.1 slice.218
  45.9 0.4 copy-done.6
  46.4 1.0 multiply_subtract_fusion.5
  47.4 1.7 %fusion.10 = (bf16[128,2,8,128]{0,3,2,1:T(8,128)(2,1)S(1)}, bf16[128,2,8,128]{0,3,2,1:T(8,128)(2,1)S(1)}) fusion(f32[128,2,8,128]{0,3,2,1:T(8,128)S(1)} %get-tuple-element.25, f32[128,1,8,128]{0,3,2,1:T(8,128)S(1)} %slice.210, f32[128,1,8,128]{0,3,2,1:T(8,128)S(1)} %get-tuple-element.26, f32[128,2,8,128]{0,3,2,1:T(8,128)S(1)} %get-tuple-element.18, ...), kind=kLoop, calls=%fused_computation.24 | loop fusion | flops 4718592 | bytes 14417920 | tf_op jit(solution)/shard_map/convert_element_type | solution.py:93
  49.2 0.8 gather_fusion
  49.9 0.8 gather_fusion.1
  50.7 0.1 pad_maximum_fusion.1
  50.8 1.0 copy.33
  51.8 0.5 reshape.542
  52.3 2.4 %fusion = f32[256,512]{1,0:T(8,128)S(1)} fusion(bf16[256,2048]{1,0:T(8,128)(2,1)S(1)} %reshape.542, bf16[64,8,16,128]{3,2,1,0:T(8,128)(2,1)} %bitcast.186), kind=kOutput, calls=%fused_computation.9 | convolution fusion | flops 536870912 | bytes 3670016 | tf_op jit(solution)/shard_map/dot_general | solution.py:98
  54.7 1.0 copy.34
  55.9 0.8 fusion.15
  56.7 6.7 %all-to-all-start = ((bf16[16,2,9,128]{3,1,2,0:T(2,128)(2,1)}), bf16[16,2,9,128]{3,1,2,0:T(2,128)(2,1)S(1)}, u32[]{:S(2)}, u32[]{:S(2)}) async-start(bf16[16,2,9,128]{3,1,2,0:T(2,128)(2,1)} %fusion.15), calls=%async_computation | async-start | bytes 147456 | tf_op jit(solution)/shard_map/all_to_all | solution.py:119
  63.4 7.2 %all-to-all-done = bf16[16,2,9,128]{3,1,2,0:T(2,128)(2,1)S(1)} async-done(((bf16[16,2,9,128]{3,1,2,0:T(2,128)(2,1)}), bf16[16,2,9,128]{3,1,2,0:T(2,128)(2,1)S(1)}, u32[]{:S(2)}, u32[]{:S(2)}) %all-to-all-start) | async-done | bytes 73760 | tf_op jit(solution)/shard_map/all_to_all | solution.py:119
  70.6 77.5 %all-reduce.9.cloned.1.call-done = f32[512,2,128]{2,1,0:T(2,128)} async-done(((f32[512,2,128]{2,1,0:T(2,128)}), f32[512,2,128]{2,1,0:T(2,128)}) %all-reduce.9.cloned.1.call-update) | async-done | bytes 524304 | tf_op jit(solution)/shard_map/psum | solution.py:101
  148.1 1.4 dynamic-slice_multiply_fusion
  149.5 0.6 copy.70
  (60 shorter events, 0.4 us)
Async XLA Ops:
  7.2 15.1 %copy-start.1 = (f32[2,3,2,8,128]{4,3,2,1,0:T(8,128)S(1)}, f32[2,3,2,8,128]{4,3,2,1,0:T(8,128)}, u32[]{:S(2)}) copy-start(f32[2,3,2,8,128]{4,3,2,1,0:T(8,128)} %param.9) | copy-start | bytes 147460
  7.2 18.5 %slice-start = ((bf16[512,2,8,128]{3,2,1,0:T(8,128)(2,1)}), bf16[128,2,8,128]{3,2,1,0:T(8,128)(2,1)S(1)}, s32[]{:S(2)}) async-start(bf16[512,2,8,128]{3,2,1,0:T(8,128)(2,1)} %param.7), calls=%async_computation.2 | async-start | bytes 1048576 | tf_op jit(solution)/shard_map/slice | solution.py:53
  7.2 15.7 %copy-start.18 = (s32[1,16,2]{1,2,0:T(2,128)S(1)}, s32[1,16,2]{1,2,0:T(2,128)}, u32[]{:S(2)}) copy-start(s32[1,16,2]{1,2,0:T(2,128)} %param.12) | copy-start | bytes 388
  7.2 15.8 %copy-start.10 = (f32[2,2,8,128]{3,2,1,0:T(8,128)S(1)}, f32[2,2,8,128]{3,2,1,0:T(8,128)}, u32[]{:S(2)}) copy-start(f32[2,2,8,128]{3,2,1,0:T(8,128)} %param.11) | copy-start | bytes 49156
  7.2 16.4 %copy-start.19 = (s32[1,16]{1,0:T(1,128)S(1)}, s32[1,16]{1,0:T(1,128)}, u32[]{:S(2)}) copy-start(s32[1,16]{1,0:T(1,128)} %param.13) | copy-start | bytes 196
  7.2 140.9 %all-reduce.9.cloned.1.call-start = ((), (), s32[]{:S(2)}) async-start(), calls=%async_computation.1 | async-start | bytes 1048576 | tf_op jit(solution)/shard_map/psum | solution.py:101
  8.0 19.3 %collective-permute-start.3 = (f32[2,8,128]{2,1,0:T(8,128)S(1)}, f32[2,8,128]{2,1,0:T(8,128)S(1)}, u32[]{:S(2)}, u32[]{:S(2)}) collective-permute-start(f32[2,8,128]{2,1,0:T(8,128)S(1)} %slice_bitcast_fusion.6), channel_id=1, source_target_pairs={{0,1},{1,2},{2,3},{3,4},{4,5},{5,6},{6,7},{7,8},{8,9},{9,10},{10,1... | collective-permute-start | bytes 24584 | tf_op jit(solution)/shard_map/ppermute | solution.py:25
  11.8 14.3 %collective-permute-start.2 = (f32[2,8,128]{2,1,0:T(8,128)S(1)}, f32[2,8,128]{2,1,0:T(8,128)S(1)}, u32[]{:S(2)}, u32[]{:S(2)}) collective-permute-start(f32[2,8,128]{2,1,0:T(8,128)S(1)} %get-tuple-element.36), channel_id=1, source_target_pairs={{0,1},{1,2},{2,3},{3,4},{4,5},{5,6},{6,7},{7,8},{8,9},{9,10},{10,1... | collective-permute-start | bytes 24584 | tf_op jit(solution)/shard_map/ppermute | solution.py:25
  17.7 10.3 %collective-permute-start.1 = (bf16[128,1,8,128]{0,3,2,1:T(8,128)(2,1)S(1)}, bf16[128,1,8,128]{0,3,2,1:T(8,128)(2,1)S(1)}, u32[]{:S(2)}, u32[]{:S(2)}) collective-permute-start(bf16[128,1,8,128]{0,3,2,1:T(8,128)(2,1)S(1)} %copy.52), channel_id=1, source_target_pairs={{1,0},{2,1},{3,2},{4,3},{5,4},{6,5},{7,6},{8,7},{9,8},{10,9},{11,1... | collective-permute-start | bytes 786440 | tf_op jit(solution)/shard_map/ppermute | solution.py:17
  19.2 8.7 %collective-permute-start = (bf16[128,1,8,128]{0,3,2,1:T(8,128)(2,1)S(1)}, bf16[128,1,8,128]{0,3,2,1:T(8,128)(2,1)S(1)}, u32[]{:S(2)}, u32[]{:S(2)}) collective-permute-start(bf16[128,1,8,128]{0,3,2,1:T(8,128)(2,1)S(1)} %copy.50), channel_id=1, source_target_pairs={{0,1},{1,2},{2,3},{3,4},{4,5},{5,6},{6,7},{7,8},{8,9},{9,10},{10,1... | collective-permute-start | bytes 786440 | tf_op jit(solution)/shard_map/ppermute | solution.py:16
  36.1 0.8 copy-start.14
  36.9 5.9 %copy-start = (f32[128,2,7,128]{0,3,2,1:T(8,128)S(1)}, f32[128,2,7,128]{0,3,2,1:T(8,128)}, u32[]{:S(2)}) copy-start(f32[128,2,7,128]{0,3,2,1:T(8,128)} %slice.211) | copy-start | bytes 2752516
  36.9 5.9 %copy-start.2 = (f32[2,8,128]{2,1,0:T(8,128)S(1)}, f32[2,8,128]{2,1,0:T(8,128)}, u32[]{:S(2)}) copy-start(f32[2,8,128]{2,1,0:T(8,128)} %get-tuple-element.44) | copy-start | bytes 24580
  36.9 5.9 %copy-start.3 = (f32[2,8,128]{2,1,0:T(8,128)S(1)}, f32[2,8,128]{2,1,0:T(8,128)}, u32[]{:S(2)}) copy-start(f32[2,8,128]{2,1,0:T(8,128)} %get-tuple-element.48) | copy-start | bytes 24580
  36.9 5.9 %copy-start.11 = (pred[2,8,128]{2,1,0:T(8,128)(4,1)S(1)}, pred[2,8,128]{2,1,0:T(8,128)(4,1)}, u32[]{:S(2)}) copy-start(pred[2,8,128]{2,1,0:T(8,128)(4,1)} %get-tuple-element.7) | copy-start | bytes 6148
  36.9 5.9 %copy-start.12 = (pred[2,8,128]{2,1,0:T(8,128)(4,1)S(1)}, pred[2,8,128]{2,1,0:T(8,128)(4,1)}, u32[]{:S(2)}) copy-start(pred[2,8,128]{2,1,0:T(8,128)(4,1)} %get-tuple-element.33) | copy-start | bytes 6148
  36.9 5.9 %copy-start.13 = (pred[2,8,128]{2,1,0:T(8,128)(4,1)S(1)}, pred[2,8,128]{2,1,0:T(8,128)(4,1)}, u32[]{:S(2)}) copy-start(pred[2,8,128]{2,1,0:T(8,128)(4,1)} %get-tuple-element.42) | copy-start | bytes 6148
  45.7 0.7 copy-start.6
  45.7 0.7 copy-start.7
  45.7 0.7 copy-start.8
  45.7 0.7 copy-start.9
  45.7 0.7 copy-start.16
  45.7 0.7 copy-start.17
  45.8 1.6 %copy-start.4 = (f32[2,8,128]{2,1,0:T(8,128)S(1)}, f32[2,8,128]{2,1,0:T(8,128)}, u32[]{:S(2)}) copy-start(f32[2,8,128]{2,1,0:T(8,128)} %get-tuple-element.49) | copy-start | bytes 24580
  45.8 1.6 %copy-start.5 = (f32[2,8,128]{2,1,0:T(8,128)S(1)}, f32[2,8,128]{2,1,0:T(8,128)}, u32[]{:S(2)}) copy-start(f32[2,8,128]{2,1,0:T(8,128)} %get-tuple-element.50) | copy-start | bytes 24580
  52.3 3.6 %copy-start.15 = (pred[16,2]{1,0:T(8,128)(4,1)S(1)}, pred[16,2]{1,0:T(8,128)(4,1)}, u32[]{:S(2)}) copy-start(pred[16,2]{1,0:T(8,128)(4,1)} %iota_compare_fusion) | copy-start | bytes 100
  56.7 13.9 %all-to-all-start = ((bf16[16,2,9,128]{3,1,2,0:T(2,128)(2,1)}), bf16[16,2,9,128]{3,1,2,0:T(2,128)(2,1)S(1)}, u32[]{:S(2)}, u32[]{:S(2)}) async-start(bf16[16,2,9,128]{3,1,2,0:T(2,128)(2,1)} %fusion.15), calls=%async_computation | async-start | bytes 147456 | tf_op jit(solution)/shard_map/all_to_all | solution.py:119
Sparse Core Ops, SparseCore 0:
  55.8 92.2 all-reduce.8
where the time goes:
time: 158 us; the launch traced here: 157 us
  waiting for transfers between devices  84.7 us (54%)
  local copies, waits for them, and re-layouts  20.8 us (13%)
  starting transfers between devices  17.9 us (11%)
  other arithmetic  16.5 us (10%)
  between operations  14.6 us (9%)
  matrix products  2.38 us (2%)
    psum x1, waiting for transfers between devices, shards(): summed = lax.psum(terms.reshape(modes, params, MB), 'cells')  77.5 us
    sub x2, other arithmetic, high_flux(): return signed * upstream - diff_face * (neighbour - state)  8.59 us
    all_to_all x1, waiting for transfers between devices, shards(): lax.all_to_all(payload, 'cells', split_axis=0, concat_axis=0, tiled=True)  7.21 us
    ppermute x2, starting transfers between devices, from_behind(): return lax.ppermute(value, axis, pairs)  6.87 us
    all_to_all x1, starting transfers between devices, shards(): lax.all_to_all(payload, 'cells', split_axis=0, concat_axis=0, tiled=True)  6.67 us
    gather x7, local copies, waits for them, and re-layouts, shards(): padded[:, x_cell + 1 + shift_x, y_cell + 1 + shift_y, z_cell + 1 + shift_z]  5.31 us
  transfers between devices with their start and end apart: 6, of which 2 were waited for; matrix products, arithmetic and copies ran while one was open for 6% of the time, Pallas kernels for 0%

commit v1 on v0

v1 whole, which is shorter than its diff:
```python
import functools

import jax
import jax.numpy as jnp
import numpy as np
from jax import lax
from jax.experimental import pallas as pl
from jax.experimental.pallas import tpu as pltpu
from jax.sharding import PartitionSpec as P

MB = 128
SPLITS = 3
BF16 = jnp.bfloat16
F32 = jnp.float32
OFFSETS = 7


def round_up(value, multiple):
    return -(-value // multiple) * multiple


def nt_dot(left, right):
    return lax.dot_general(left, right, (((1,), (1,)), ((), ())), preferred_element_type=F32)


def exact_parts(value):
    parts = []
    for _ in range(SPLITS):
        head = lax.reduce_precision(value, 8, 7)
        parts.append(head.astype(BF16))
        value = value - head
    return parts


def main_kernel(
    dims,
    odd_ref,
    basis_ref,
    inner_ref,
    outer_ref,
    speed_ref,
    diff_ref,
    flag_ref,
    react_ref,
    cell_ref,
    row_from_ref,
    payload_ref,
    coef_ref,
    prev_ref,
    halo_ref,
    applied_ref,
):
    params, layers, width_y, width_z, devices, own, slots, pad = dims
    plane = width_y * width_z
    cells = layers * plane
    odd = odd_ref[0] == 1

    halo_ref[0] = jnp.where(odd, inner_ref[:MB], outer_ref[:MB])
    halo_ref[1] = jnp.where(odd, outer_ref[:MB], inner_ref[:MB])
    tail = jnp.where(odd, inner_ref[MB:], outer_ref[MB:]).astype(F32)
    count = 2 * params
    prev = tail[:count]
    for part in range(1, SPLITS):
        prev = prev + tail[part * count : (part + 1) * count]
    signed_prev, diff_prev = prev[:params], prev[params:]
    prev_ref[:params] = jnp.maximum(signed_prev, 0.0) + diff_prev
    prev_ref[params:] = jnp.minimum(signed_prev, 0.0) - diff_prev

    y_at = lax.broadcasted_iota(jnp.int32, (width_y, width_z), 0)
    z_at = lax.broadcasted_iota(jnp.int32, (width_y, width_z), 1)
    for param in range(params):
        uppers, nexts = [], []
        for layer in range(layers):
            up_d, next_d = [], []
            for axis_d in range(3):
                forward = flag_ref[param, axis_d, layer] == 1
                speed = speed_ref[param, axis_d, layer]
                diff = diff_ref[param, axis_d, layer]
                up_d.append(jnp.where(forward, speed, 0.0) + diff)
                next_d.append(jnp.where(forward, 0.0, -speed) - diff)
            uppers.append(up_d)
            nexts.append(next_d)
        for layer in range(layers):
            diag = react_ref[param, layer]
            diag = diag + uppers[layer][0] + uppers[layer][1] + uppers[layer][2]
            if layer > 0:
                diag = diag - nexts[layer - 1][0]
                coef_ref[param, layer, 2] = -uppers[layer - 1][0]
            coef_ref[param, layer, 1] = nexts[layer][0]
            for axis_d, at, shift_axis, size in ((1, y_at, 0, width_y), (2, z_at, 1, width_z)):
                up, following = uppers[layer][axis_d], nexts[layer][axis_d]
                low_up = jnp.where(at == 0, 0.0, pltpu.roll(up, 1, shift_axis))
                low_next = jnp.where(at == 0, 0.0, pltpu.roll(following, 1, shift_axis))
                diag = diag - low_next
                coef_ref[param, layer, 1 + 2 * axis_d] = jnp.where(at == size - 1, 0.0, following)
                coef_ref[param, layer, 2 + 2 * axis_d] = -low_up
            coef_ref[param, layer, 0] = diag

    def tile(layer, y):
        lanes = slice(y * width_z, (y + 1) * width_z)
        if layer < 0:
            return halo_ref[0, :, lanes]
        if layer >= layers:
            return halo_ref[1, :, lanes]
        start = layer * plane + y * width_z
        return basis_ref[:MB, start : start + width_z]

    for layer in range(layers):
        for y in range(width_y):
            start = layer * plane + y * width_z
            state = tile(layer, y).astype(F32)
            terms = [state, tile(layer + 1, y).astype(F32), tile(layer - 1, y).astype(F32)]
            which = [0, 1, 2]
            if y < width_y - 1:
                terms.append(tile(layer, y + 1).astype(F32))
                which.append(3)
            if y > 0:
                terms.append(tile(layer, y - 1).astype(F32))
                which.append(4)
            terms.append(pltpu.roll(state, width_z - 1, 1))
            terms.append(pltpu.roll(state, 1, 1))
            which += [5, 6]
            for param in range(params):
                total = None
                for at, term in zip(which, terms):
                    if at == 2 and layer == 0:
                        coef = -prev_ref[param : param + 1, y * width_z : (y + 1) * width_z]
                    else:
                        coef = coef_ref[param, layer, at, y : y + 1, :]
                    if at == 0 and layer == 0:
                        coef = coef - prev_ref[params + param : params + param + 1, y * width_z : (y + 1) * width_z]
                    product = coef * term
                    total = product if total is None else total + product
                applied_ref[param * MB : (param + 1) * MB, start : start + width_z] = total.astype(BF16)

    sums = nt_dot(basis_ref[...], applied_ref[...]).astype(BF16)
    for owner in range(devices):
        for param in range(params):
            payload_ref[owner, param * own : (param + 1) * own, :] = sums[
                owner * own : (owner + 1) * own, param * MB : (param + 1) * MB
            ]

    samples = devices * slots
    lanes = lax.broadcasted_iota(jnp.int32, (1, width_z), 1)

    def picked(targets, place):
        return jnp.where(targets - place * width_z == lanes, 1.0, 0.0).astype(BF16)

    center = cell_ref[0 * samples : 1 * samples]
    inside = cell_ref[: 5 * samples]
    below = cell_ref[5 * samples : 6 * samples]
    above = cell_ref[6 * samples : 7 * samples]
    got_in = jnp.zeros((5 * samples, MB), F32)
    got_below = jnp.zeros((samples, MB), F32)
    got_above = jnp.zeros((samples, MB), F32)
    got_applied = jnp.zeros((samples, params * MB), F32)
    for layer in range(-1, layers + 1):
        for y in range(width_y):
            place = layer * width_y + y
            block = tile(layer, y)
            if 0 <= layer < layers:
                got_in = got_in + nt_dot(picked(inside, place), block)
                got_applied = got_applied + nt_dot(
                    picked(center, place), applied_ref[:, place * width_z : (place + 1) * width_z]
                )
            if layer < layers - 1:
                got_below = got_below + nt_dot(picked(below, place), block)
            if layer > 0:
                got_above = got_above + nt_dot(picked(above, place), block)
    pieces = [got_applied[:, param * MB : (param + 1) * MB] for param in range(params)]
    pieces += [got_in[:samples], got_below, got_above, got_in[samples:]]
    gathered = jnp.concatenate(pieces, axis=0).astype(BF16)
    columns = lax.broadcasted_iota(jnp.int32, (1, gathered.shape[0]), 1)
    order = jnp.where(row_from_ref[...] == columns, 1.0, 0.0).astype(BF16)
    ordered = jnp.dot(order, gathered, preferred_element_type=F32).astype(BF16)
    for owner in range(devices):
        payload_ref[owner, params * own :, :] = ordered[owner * pad : (owner + 1) * pad]


def shards(basis, face_speed, face_diffusion, upwind_flag, reaction, sample_cell, sample_count):
    modes, layers, width_y, width_z = basis.shape
    params = face_speed.shape[0]
    devices = lax.axis_size("cells")
    slots = sample_cell.shape[2]
    plane = width_y * width_z
    cells = layers * plane
    own = modes // devices
    rows = params + OFFSETS
    me = lax.axis_index("cells")
    odd = me % 2

    block = basis[:MB].reshape(MB, cells)
    first, last = block[:, :plane], block[:, cells - plane :]
    last_speed = face_speed[:, 0, -1]
    signed = jnp.where(upwind_flag[:, 0, -1] == 1, last_speed, -last_speed)
    faces = jnp.concatenate([signed, face_diffusion[:, 0, -1]], axis=0).reshape(2 * params, plane)
    tail = jnp.concatenate(exact_parts(faces), axis=0)
    tail = jnp.pad(tail, ((0, round_up(tail.shape[0], 16) - tail.shape[0]), (0, 0)))
    to_inner = jnp.concatenate([jnp.where(odd == 1, first, last), tail], axis=0)
    to_outer = jnp.concatenate([jnp.where(odd == 1, last, first), tail], axis=0)
    inner_pairs = [(i, i ^ 1) for i in range(devices)]
    outer_pairs = []
    for i in range(1, devices - 1, 2):
        outer_pairs += [(i, i + 1), (i + 1, i)]
    inner = lax.ppermute(to_inner, "cells", inner_pairs)
    outer = lax.ppermute(to_outer, "cells", outer_pairs)

    flat = sample_cell[0].reshape(devices * slots, 1)
    slot_at = lax.broadcasted_iota(jnp.int32, (devices, slots), 1)
    live = (slot_at < sample_count[0][:, None]).reshape(devices * slots, 1)
    y_at = flat // width_z % width_y
    z_at = flat % width_z
    nowhere = -(4 * cells)

    def target(shift, ok):
        return jnp.where(live & ok, flat + shift, nowhere)

    anywhere = live
    targets = jnp.concatenate(
        [
            target(0, anywhere),
            target(-width_z, y_at > 0),
            target(width_z, y_at < width_y - 1),
            target(-1, z_at > 0),
            target(1, z_at < width_z - 1),
            target(-plane, anywhere),
            target(plane, anywhere),
        ],
        axis=0,
    )

    samples = devices * slots
    pad = round_up(slots * rows, 8)
    row_from = np.full((devices, pad), -1, np.int32)
    for owner in range(devices):
        for slot in range(slots):
            for row in range(rows):
                row_from[owner, row * slots + slot] = row * samples + owner * slots + slot
    dims = (params, layers, width_y, width_z, devices, own, slots, pad)
    vmem = pl.BlockSpec(memory_space=pltpu.VMEM)
    payload = pl.pallas_call(
        functools.partial(main_kernel, dims),
        out_shape=jax.ShapeDtypeStruct((devices, params * own + pad, MB), BF16),
        in_specs=[pl.BlockSpec(memory_space=pltpu.SMEM)] + [vmem] * 9,
        out_specs=vmem,
        scratch_shapes=[
            pltpu.VMEM((params, layers, OFFSETS, width_y, width_z), F32),
            pltpu.VMEM((2 * params, plane), F32),
            pltpu.VMEM((2, MB, plane), BF16),
            pltpu.VMEM((params * MB, cells), BF16),
        ],
        compiler_params=pltpu.CompilerParams(vmem_limit_bytes=40 * 1024 * 1024),
        name="project",
    )(
        odd.reshape(1).astype(jnp.int32),
        basis.reshape(modes, cells),
        inner,
        outer,
        face_speed,
        face_diffusion,
        upwind_flag,
        reaction,
        targets,
        jnp.asarray(row_from.reshape(-1, 1)),
    )
    received = lax.all_to_all(payload, "cells", split_axis=0, concat_axis=0, tiled=True)
    volume = 1.0 / (layers * devices * width_y * width_z)
    summed = jnp.sum(received[:, : params * own].astype(F32), axis=0) * volume
    galerkin = jnp.transpose(summed.reshape(params, own, MB), (1, 0, 2))
    sampled = received[:, params * own : params * own + slots * rows].reshape(devices, rows, slots, MB)
    return (galerkin, jnp.transpose(sampled, (0, 2, 1, 3))[None])


def solution(mesh):
    return jax.shard_map(
        shards,
        mesh=mesh,
        in_specs=(
            P(None, ("groups", "cells"), None, None),
            P(None, None, ("groups", "cells"), None, None),
            P(None, None, ("groups", "cells"), None, None),
            P(None, None, ("groups", "cells"), None, None),
            P(None, ("groups", "cells"), None, None),
            P(("groups", "cells"), None, None),
            P(("groups", "cells"), None),
        ),
        out_specs=(
            P(("groups", "cells"), None, None),
            P(("groups", "cells"), None, None, None, None),
        ),
        check_vma=False,
    )
```

time: 158 us -> 38.5 us (0.24)
  waiting for transfers between devices: 84.7 us -> 0.01 us
  blocking collectives: 0 us -> 22.4 us
  other arithmetic: 16.5 us -> 0.99 us
  local copies, waits for them, and re-layouts: 20.8 us -> 5.51 us
  between operations: 14.6 us -> 0.85 us
  starting transfers between devices: 17.9 us -> 5.06 us
  Pallas kernels: 0 us -> 3.36 us
  matrix products: 2.38 us -> 0 us
    psum x1 -> x0, waiting for transfers between devices: 77.5 us -> none  [shards(): summed = lax.psum(terms.reshape(modes, params, MB), 'cells')]
    all_to_all x0 -> x1, blocking collectives: none -> 22.4 us  [shards(): lax.all_to_all(payload, 'cells', split_axis=0, concat_axis=0, tiled=True)]
    sub x3 -> x0, other arithmetic: 9.61 us -> none  [the longest x2 8.59 us: high_flux(): return signed * upstream - diff_face * (neighbour - state)]
    all_to_all x1 -> x0, waiting for transfers between devices: 7.21 us -> none  [shards(): lax.all_to_all(payload, 'cells', split_axis=0, concat_axis=0, tiled=True)]
    gather x9 -> x0, local copies, waits for them, and re-layouts: 6.83 us -> none  [the longest x7 5.31 us: shards(): padded[:, x_cell + 1 + shift_x, y_cell + 1 + shift_y, z_cell + 1 + shift_z]]
    all_to_all x1 -> x0, starting transfers between devices: 6.67 us -> none  [shards(): lax.all_to_all(payload, 'cells', split_axis=0, concat_axis=0, tiled=True)]
    ppermute x4 -> x2, starting transfers between devices: 11.2 us -> 5.06 us  [the longest x1 4.38 us: shards(): inner = lax.ppermute(to_inner, 'cells', inner_pairs)]
    pallas_call x0 -> x1, Pallas kernels: none -> 3.36 us  [shards(): pl.pallas_call(functools.partial(main_kernel, dims), out_shape=jax.ShapeD...]
  transfers between devices with their start and end apart: 6 -> 2, of which waited for: 2 -> 0; matrix products, arithmetic and copies ran while one was open for 6% -> 3% of each run, Pallas kernels for 0% -> 0%
where the time goes in v1:
time: 38.5 us; the launch traced here: 38.2 us
  blocking collectives  22.4 us (58%)
  local copies, waits for them, and re-layouts  5.51 us (14%)
  starting transfers between devices  5.06 us (13%)
  Pallas kernels  3.36 us (9%)
  other arithmetic  0.99 us (3%)
  between operations  0.85 us (2%)
    all_to_all x1, blocking collectives, shards(): lax.all_to_all(payload, 'cells', split_axis=0, concat_axis=0, tiled=True)  22.4 us
    ppermute x1, starting transfers between devices, shards(): inner = lax.ppermute(to_inner, 'cells', inner_pairs)  4.38 us
    unnamed x24, local copies, waits for them, and re-layouts  3.85 us
    pallas_call x1, Pallas kernels, shards(): pl.pallas_call(functools.partial(main_kernel, dims), out_shape=jax.ShapeD...  3.36 us
    slice x1, local copies, waits for them, and re-layouts, shards(): block = basis[:MB].reshape(MB, cells)  1.23 us
  transfers between devices with their start and end apart: 2, of which 0 were waited for; matrix products, arithmetic and copies ran while one was open for 3% of the time, Pallas kernels for 0%

profile of v1, /device:TPU:0, one launch (start us, length us, event | category | flops | bytes accessed | tf_op | source)
XLA Modules:
  0.0 38.2 jit_solution(12732116899618879696)
XLA Ops:
  0.6 0.7 %fusion.7 = pred[1,2,8,128]{3,2,1,0:T(8,128)(4,1)S(1)} fusion(s32[2,3,2,8,128]{4,3,2,1,0:T(8,128)} %flag_ref.1), kind=kLoop, calls=%fused_computation.27 | loop fusion | flops 2048 | bytes 10240
  1.3 0.7 %slice_bitcast_fusion.1 = f32[1,2,8,128]{3,2,1,0:T(8,128)S(1)} fusion(f32[2,3,2,8,128]{4,3,2,1,0:T(8,128)} %speed_ref.1), kind=kLoop, calls=%fused_computation.25 | loop fusion | bytes 16384
  2.0 0.7 %slice_bitcast_fusion = f32[1,2,8,128]{3,2,1,0:T(8,128)S(1)} fusion(f32[2,3,2,8,128]{4,3,2,1,0:T(8,128)} %diff_ref.1), kind=kLoop, calls=%fused_computation.24 | loop fusion | bytes 16384
  2.8 0.0 copy-start.7
  2.8 0.0 copy-start.6
  2.8 0.0 copy-start.5
  2.8 1.2 %slice.24 = bf16[128,2,8,128]{3,2,1,0:T(8,128)(2,1)S(1)} slice(bf16[512,2,8,128]{3,2,1,0:T(8,128)(2,1)} %param.8), slice={[0:128], [0:2], [0:8], [0:128]} | slice | bytes 1048576 | tf_op jit(solution)/shard_map/slice | solution.py:192
  4.0 0.1 copy.65
  4.3 0.7 %collective-permute-start.1 = (bf16[144,1024]{1,0:T(8,128)(2,1)S(1)}, bf16[144,1024]{1,0:T(8,128)(2,1)S(1)}, u32[]{:S(2)}, u32[]{:S(2)}) collective-permute-start(bf16[144,1024]{1,0:T(8,128)(2,1)S(1)} %get-tuple-element.10), channel_id=1, source_target_pairs={{1,2},{2,1},{3,4},{4,3},{5,6},{6,5},{7,8},{8,7},{9,10},{10,9},{11,... | collective-permute-start | bytes 884744 | tf_op jit(solution)/shard_map/ppermute | solution.py:206
  5.0 4.4 %collective-permute-start = (bf16[144,1024]{1,0:T(8,128)(2,1)S(1)}, bf16[144,1024]{1,0:T(8,128)(2,1)S(1)}, u32[]{:S(2)}, u32[]{:S(2)}) collective-permute-start(bf16[144,1024]{1,0:T(8,128)(2,1)S(1)} %get-tuple-element.11), channel_id=1, source_target_pairs={{0,1},{1,0},{2,3},{3,2},{4,5},{5,4},{6,7},{7,6},{8,9},{9,8},{10,11... | collective-permute-start | bytes 884744 | tf_op jit(solution)/shard_map/ppermute | solution.py:205
  9.4 0.0 copy-done.7
  9.4 0.1 iota_compare_fusion.1
  9.5 0.1 lt.93
  9.6 0.0 copy-done.6
  9.6 0.1 copy.49
  9.7 0.1 reshape_squeeze.3
  9.8 0.1 concatenate.23
  9.9 0.1 copy.50.cell_ref
  10.0 0.0 copy-done.5
  10.0 0.0 copy-start
  10.0 0.0 copy-start.1
  10.1 0.0 copy-start.2
  10.1 0.0 copy-start.3
  10.1 0.0 copy-start.4
  10.1 0.5 %copy.64 = bf16[64,8,16,128]{3,1,2,0:T(8,128)(2,1)S(1)} copy(bf16[64,8,16,128]{3,2,1,0:T(8,128)(2,1)S(1)} %bitcast.37) | data formatting | bytes 4194304
  10.6 0.0 collective-permute-done.1.outer_ref
  10.7 0.0 collective-permute-done.inner_ref
  10.7 0.3 copy-done
  11.0 0.0 copy-done.1
  11.0 0.0 copy-done.2
  11.0 0.0 copy-done.3
  11.0 0.0 copy-done.4
  11.0 3.4 %project.1 = bf16[16,88,128]{2,1,0:T(8,128)(2,1)S(1)} custom-call(s32[1]{0:T(128)} %bitcast.odd_ref, bf16[512,2048]{1,0:T(8,128)(2,1)S(1)} %bitcast.36, bf16[144,1024]{1,0:T(8,128)(2,1)S(1)} %collective-permute-done.inner_ref, bf16[144,1024]{1,0:T(8,128)(2,1)S(1)} %collective-permute-done.1.outer_ref, f32[2,3,2,8,128]{4,3,2,1,0:T(8,128)S(1)} %copy-done.3, ...), custom_call_target="tpu_custom_call" | custom-call | tf_op jit(solution)/shard_map/project/pallas_call | solution.py:241
  14.3 22.4 %all_to_all.5 = bf16[16,88,128]{2,1,0:T(8,128)(2,1)S(1)} all-to-all(bf16[16,88,128]{2,1,0:T(8,128)(2,1)S(1)} %project.1), channel_id=1, replica_groups=mesh['groups'=2,'cells'=16] {'cells'}, dimensions={0} | all-to-all | bytes 720896 | tf_op jit(solution)/shard_map/all_to_all | solution.py:266
  36.8 0.7 %copy.53 = bf16[1,16,2,9,128]{4,2,3,1,0:T(2,128)(2,1)} copy(bf16[1,16,2,9,128]{4,1,2,3,0:T(8,128)(2,1)S(1)} %bitcast.40) | data formatting | bytes 147456
  37.6 0.6 %copy.52 = f32[32,2,128]{2,1,0:T(2,128)} copy(f32[32,2,128]{2,0,1:T(8,128)S(1)} %bitcast.41) | data formatting | bytes 65536
  (12 shorter events, 0.2 us)
Async XLA Ops:
  2.8 6.6 %copy-start.7 = (s32[1,16]{1,0:T(1,128)S(1)}, s32[1,16]{1,0:T(1,128)}, u32[]{:S(2)}) copy-start(s32[1,16]{1,0:T(1,128)} %param.14) | copy-start | bytes 196
  2.8 6.8 %copy-start.6 = (s32[1,16,2]{1,2,0:T(2,128)S(1)}, s32[1,16,2]{1,2,0:T(2,128)}, u32[]{:S(2)}) copy-start(s32[1,16,2]{1,2,0:T(2,128)} %param.13) | copy-start | bytes 388
  2.8 7.3 %copy-start.5 = (bf16[512,2,8,128]{3,2,1,0:T(8,128)(2,1)S(1)}, bf16[512,2,8,128]{3,2,1,0:T(8,128)(2,1)}, u32[]{:S(2)}) copy-start(bf16[512,2,8,128]{3,2,1,0:T(8,128)(2,1)} %param.8) | copy-start | bytes 6291460
  4.3 6.3 %collective-permute-start.1 = (bf16[144,1024]{1,0:T(8,128)(2,1)S(1)}, bf16[144,1024]{1,0:T(8,128)(2,1)S(1)}, u32[]{:S(2)}, u32[]{:S(2)}) collective-permute-start(bf16[144,1024]{1,0:T(8,128)(2,1)S(1)} %get-tuple-element.10), channel_id=1, source_target_pairs={{1,2},{2,1},{3,4},{4,3},{5,6},{6,5},{7,8},{8,7},{9,10},{10,9},{11,... | collective-permute-start | bytes 884744 | tf_op jit(solution)/shard_map/ppermute | solution.py:206
  5.0 5.7 %collective-permute-start = (bf16[144,1024]{1,0:T(8,128)(2,1)S(1)}, bf16[144,1024]{1,0:T(8,128)(2,1)S(1)}, u32[]{:S(2)}, u32[]{:S(2)}) collective-permute-start(bf16[144,1024]{1,0:T(8,128)(2,1)S(1)} %get-tuple-element.11), channel_id=1, source_target_pairs={{0,1},{1,0},{2,3},{3,2},{4,5},{5,4},{6,7},{7,6},{8,9},{9,8},{10,11... | collective-permute-start | bytes 884744 | tf_op jit(solution)/shard_map/ppermute | solution.py:205
  10.0 0.9 %copy-start = (s32[384,1]{1,0:T(8,128)S(1)}, s32[384,1]{1,0:T(8,128)}, u32[]{:S(2)}) copy-start(s32[384,1]{1,0:T(8,128)} %constant.78.clone.row_from_ref) | copy-start | bytes 4612
  10.0 0.9 %copy-start.1 = (f32[2,3,2,8,128]{4,3,2,1,0:T(8,128)S(1)}, f32[2,3,2,8,128]{4,3,2,1,0:T(8,128)}, u32[]{:S(2)}) copy-start(f32[2,3,2,8,128]{4,3,2,1,0:T(8,128)} %diff_ref.1) | copy-start | bytes 147460
  10.1 0.9 %copy-start.2 = (s32[2,3,2,8,128]{4,3,2,1,0:T(8,128)S(1)}, s32[2,3,2,8,128]{4,3,2,1,0:T(8,128)}, u32[]{:S(2)}) copy-start(s32[2,3,2,8,128]{4,3,2,1,0:T(8,128)} %flag_ref.1) | copy-start | bytes 147460
  10.1 0.9 %copy-start.3 = (f32[2,3,2,8,128]{4,3,2,1,0:T(8,128)S(1)}, f32[2,3,2,8,128]{4,3,2,1,0:T(8,128)}, u32[]{:S(2)}) copy-start(f32[2,3,2,8,128]{4,3,2,1,0:T(8,128)} %speed_ref.1) | copy-start | bytes 147460
  10.1 0.9 %copy-start.4 = (f32[2,2,8,128]{3,2,1,0:T(8,128)S(1)}, f32[2,2,8,128]{3,2,1,0:T(8,128)}, u32[]{:S(2)}) copy-start(f32[2,2,8,128]{3,2,1,0:T(8,128)} %react_ref.1) | copy-start | bytes 49156

commit v2 on v1

v2 whole, which is shorter than its diff:
```python
import functools

import jax
import jax.numpy as jnp
import numpy as np
from jax import lax
from jax.experimental import pallas as pl
from jax.experimental.pallas import tpu as pltpu
from jax.sharding import PartitionSpec as P

MB = 128
SPLITS = 3
NARROW_STEPS = 3
BF16 = jnp.bfloat16
F32 = jnp.float32
I32 = jnp.int32
OFFSETS = 7
VMEM = pl.BlockSpec(memory_space=pltpu.VMEM)
SMEM = pl.BlockSpec(memory_space=pltpu.SMEM)
LIMIT = pltpu.CompilerParams(vmem_limit_bytes=40 * 1024 * 1024)


def nt_dot(left, right):
    return lax.dot_general(left, right, (((1,), (1,)), ((), ())), preferred_element_type=F32)


def picked(targets, start, count):
    lanes = lax.broadcasted_iota(I32, (1, count), 1) + start
    return jnp.where(targets == lanes, 1.0, 0.0).astype(BF16)


def halves(value):
    head = value.astype(BF16)
    return head, (value - head.astype(F32)).astype(BF16)


def pack_kernel(dims, odd_ref, flat_ref, speed_ref, diff_ref, flag_ref, inner_ref, outer_ref):
    params, layers, width_y, width_z, plane = dims
    odd = odd_ref[0]
    last = (layers - 1) * plane
    to_inner = pl.multiple_of((1 - odd) * last, width_z)
    to_outer = pl.multiple_of(odd * last, width_z)
    inner_ref[:MB] = flat_ref[:MB, pl.ds(to_inner, plane)]
    outer_ref[:MB] = flat_ref[:MB, pl.ds(to_outer, plane)]
    speed = speed_ref[:, 0, layers - 1].reshape(params * width_y, width_z)
    forward = flag_ref[:, 0, layers - 1].reshape(params * width_y, width_z) == 1
    signed = jnp.where(forward, speed, -speed)
    diff = diff_ref[:, 0, layers - 1].reshape(params * width_y, width_z)
    for ref in (inner_ref, outer_ref):
        ref[MB:] = jnp.zeros((params * width_y, plane), BF16)
    for at, value in enumerate((signed, diff)):
        for part in range(SPLITS):
            head = value.astype(BF16)
            value = value - head.astype(F32)
            lane = (at * SPLITS + part) * width_z
            inner_ref[MB:, lane : lane + width_z] = head
            outer_ref[MB:, lane : lane + width_z] = head


def local_kernel(
    dims,
    flat_ref,
    speed_ref,
    diff_ref,
    flag_ref,
    react_ref,
    cell_ref,
    acc_ref,
    edge_ref,
    in_ref,
    side_ref,
    center_ref,
    coef_ref,
):
    params, layers, width_y, width_z, plane, samples = dims
    y_at = lax.broadcasted_iota(I32, (width_y, width_z), 0)
    z_at = lax.broadcasted_iota(I32, (width_y, width_z), 1)
    for param in range(params):
        uppers, nexts = [], []
        for layer in range(layers):
            up_d, next_d = [], []
            for axis_d in range(3):
                forward = flag_ref[param, axis_d, layer] == 1
                speed = speed_ref[param, axis_d, layer]
                diff = diff_ref[param, axis_d, layer]
                up_d.append(jnp.where(forward, speed, 0.0) + diff)
                next_d.append(jnp.where(forward, 0.0, -speed) - diff)
            uppers.append(up_d)
            nexts.append(next_d)
        edge_ref[param] = nexts[layers - 1][0]
        for layer in range(layers):
            diag = react_ref[param, layer]
            diag = diag + uppers[layer][0] + uppers[layer][1] + uppers[layer][2]
            if layer > 0:
                diag = diag - nexts[layer - 1][0]
                coef_ref[param, layer, 2] = -uppers[layer - 1][0]
            coef_ref[param, layer, 1] = nexts[layer][0]
            for axis_d, at, shift_axis, size in ((1, y_at, 0, width_y), (2, z_at, 1, width_z)):
                up, following = uppers[layer][axis_d], nexts[layer][axis_d]
                low_up = jnp.where(at == 0, 0.0, pltpu.roll(up, 1, shift_axis))
                low_next = jnp.where(at == 0, 0.0, pltpu.roll(following, 1, shift_axis))
                diag = diag - low_next
                coef_ref[param, layer, 1 + 2 * axis_d] = jnp.where(at == size - 1, 0.0, following)
                coef_ref[param, layer, 2 + 2 * axis_d] = -low_up
            coef_ref[param, layer, 0] = diag

    def tile(layer, y):
        start = layer * plane + y * width_z
        return flat_ref[:MB, start : start + width_z].astype(F32)

    for layer in range(layers):
        for y in range(width_y):
            start = layer * plane + y * width_z
            state = tile(layer, y)
            terms = [(0, state), (5, pltpu.roll(state, width_z - 1, 1)), (6, pltpu.roll(state, 1, 1))]
            if layer < layers - 1:
                terms.append((1, tile(layer + 1, y)))
            if layer > 0:
                terms.append((2, tile(layer - 1, y)))
            if y < width_y - 1:
                terms.append((3, tile(layer, y + 1)))
            if y > 0:
                terms.append((4, tile(layer, y - 1)))
            for param in range(params):
                total = None
                for at, term in terms:
                    product = coef_ref[param, layer, at, y : y + 1, :] * term
                    total = product if total is None else total + product
                acc_ref[param * MB : (param + 1) * MB, start : start + width_z] = total

    cells = layers * plane
    block = flat_ref[:MB, :]
    inside = picked(cell_ref[: 5 * samples], 0, cells)
    center_ref[...] = inside[:samples]
    in_ref[...] = nt_dot(inside, block).astype(BF16)
    side_ref[:samples] = nt_dot(picked(cell_ref[5 * samples : 6 * samples], 0, cells), block).astype(BF16)
    side_ref[samples:] = nt_dot(picked(cell_ref[6 * samples :], 0, cells), block).astype(BF16)


def project_kernel(
    dims,
    odd_ref,
    dest_ref,
    flat_ref,
    inner_ref,
    outer_ref,
    acc_ref,
    edge_ref,
    in_ref,
    side_ref,
    center_ref,
    cell_ref,
    row_ref,
    keep_ref,
    keep_rows_ref,
    packet_ref,
    halo_ref,
    prev_ref,
    applied_ref,
    sums_ref,
):
    params, layers, width_y, width_z, plane, samples, devices, own = dims
    cells = layers * plane
    odd = odd_ref[0] == 1
    halo_ref[0] = jnp.where(odd, inner_ref[:MB], outer_ref[:MB])
    halo_ref[1] = jnp.where(odd, outer_ref[:MB], inner_ref[:MB])
    tail = jnp.where(odd, inner_ref[MB:], outer_ref[MB:]).astype(F32)
    faces = []
    for at in range(2):
        value = None
        for part in range(SPLITS):
            lane = (at * SPLITS + part) * width_z
            piece = tail[:, lane : lane + width_z]
            value = piece if value is None else value + piece
        faces.append(value)
    signed_prev, diff_prev = faces
    prev_ref[0] = -(jnp.maximum(signed_prev, 0.0) + diff_prev)
    prev_ref[1] = diff_prev - jnp.minimum(signed_prev, 0.0)

    for layer in range(layers):
        for y in range(width_y):
            start = layer * plane + y * width_z
            lanes = slice(y * width_z, (y + 1) * width_z)
            for param in range(params):
                modes = slice(param * MB, (param + 1) * MB)
                total = acc_ref[modes, start : start + width_z]
                row = param * width_y + y
                if layer == 0:
                    total = total + prev_ref[1, row : row + 1, :] * flat_ref[:MB, start : start + width_z].astype(F32)
                    total = total + prev_ref[0, row : row + 1, :] * halo_ref[0, :, lanes].astype(F32)
                if layer == layers - 1:
                    total = total + edge_ref[param, y : y + 1, :] * halo_ref[1, :, lanes].astype(F32)
                applied_ref[modes, start : start + width_z] = total.astype(BF16)

    sums = nt_dot(flat_ref[...], applied_ref[...])
    for param in range(params):
        sums_ref[pl.ds(param, sums.shape[0], stride=params), :] = sums[:, param * MB : (param + 1) * MB]
    size = own * params
    half = devices // 2
    for place in range(devices):
        start = pl.multiple_of(dest_ref[place] * size, size)
        terms = sums_ref[pl.ds(start, size), :]
        if place < half:
            keep_ref[place * size : (place + 1) * size] = terms
        else:
            head, rest = halves(terms)
            at = (place - half) * size
            packet_ref[at : at + size] = head
            packet_ref[half * size + at : half * size + at + size] = rest

    got_applied = nt_dot(center_ref[...], applied_ref[...]).astype(BF16)
    below = picked(cell_ref[5 * samples : 6 * samples], -plane, plane)
    above = picked(cell_ref[6 * samples :], cells, plane)
    got_below = nt_dot(below, halo_ref[0]).astype(BF16) + side_ref[:samples]
    got_above = nt_dot(above, halo_ref[1]).astype(BF16) + side_ref[samples:]
    pieces = [got_applied[:, param * MB : (param + 1) * MB] for param in range(params)]
    pieces += [in_ref[:samples], got_below, got_above, in_ref[samples:]]
    gathered = jnp.concatenate(pieces, axis=0)
    order = picked(row_ref[...], 0, gathered.shape[0])
    ordered = jnp.dot(order, gathered, preferred_element_type=F32).astype(BF16)
    count = ordered.shape[0] // 2
    keep_rows_ref[...] = ordered[:count]
    packet_ref[2 * half * size :] = ordered[count:]


def merge_kernel(wide_in, wide_out, keep_ref, keep_rows_ref, got_ref, shuffle_ref, keep_out, rows_out, packet_out):
    size = keep_ref.shape[0]
    half = size // 2
    total = keep_ref[...] + got_ref[:size].astype(F32)
    if wide_in:
        total = total + got_ref[size : 2 * size].astype(F32)
    keep_out[...] = total[:half]
    if wide_out:
        head, rest = halves(total[half:])
        packet_out[:half] = head
        packet_out[half : 2 * half] = rest
    else:
        packet_out[:half] = total[half:].astype(BF16)
    count = keep_rows_ref.shape[0]
    rows = jnp.concatenate([keep_rows_ref[...], got_ref[got_ref.shape[0] - count :]], axis=0)
    order = picked(shuffle_ref[...], 0, 2 * count)
    ordered = jnp.dot(order, rows, preferred_element_type=F32).astype(BF16)
    rows_out[...] = ordered[:count]
    packet_out[packet_out.shape[0] - count :] = ordered[count:]


def final_kernel(wide_in, volume, keep_ref, keep_rows_ref, got_ref, final_ref, sum_out, rows_out):
    size = keep_ref.shape[0]
    total = keep_ref[...] + got_ref[:size].astype(F32)
    if wide_in:
        total = total + got_ref[size : 2 * size].astype(F32)
    sum_out[...] = volume * total
    count = keep_rows_ref.shape[0]
    rows = jnp.concatenate([keep_rows_ref[...], got_ref[got_ref.shape[0] - count :]], axis=0)
    order = picked(final_ref[...], 0, 2 * count)
    rows_out[...] = jnp.dot(order, rows, preferred_element_type=F32).astype(BF16)


def shape(dims, dtype):
    return jax.ShapeDtypeStruct(dims, dtype)


def shards(basis, face_speed, face_diffusion, upwind_flag, reaction, sample_cell, sample_count):
    modes, layers, width_y, width_z = basis.shape
    params = face_speed.shape[0]
    devices = lax.axis_size("cells")
    slots = sample_cell.shape[2]
    plane = width_y * width_z
    cells = layers * plane
    own = modes // devices
    rows = params + OFFSETS
    samples = devices * slots
    me = lax.axis_index("cells")
    odd = (me % 2).astype(I32).reshape(1)
    steps = devices.bit_length() - 1

    flat = basis.reshape(modes, cells)
    tail = params * width_y
    halo = shape((MB + tail, plane), BF16)
    to_inner, to_outer = pl.pallas_call(
        functools.partial(pack_kernel, (params, layers, width_y, width_z, plane)),
        out_shape=(halo, halo),
        in_specs=[SMEM] + [VMEM] * 4,
        out_specs=(VMEM, VMEM),
        compiler_params=LIMIT,
        name="pack_halo",
    )(odd, flat, face_speed, face_diffusion, upwind_flag)
    inner_pairs = [(i, i ^ 1) for i in range(devices)]
    outer_pairs = []
    for i in range(1, devices - 1, 2):
        outer_pairs += [(i, i + 1), (i + 1, i)]
    outer = lax.ppermute(to_outer, "cells", outer_pairs)
    inner = lax.ppermute(to_inner, "cells", inner_pairs)

    cell = sample_cell[0].reshape(samples, 1)
    slot_at = lax.broadcasted_iota(I32, (devices, slots), 1)
    live = (slot_at < sample_count[0][:, None]).reshape(samples, 1)
    y_at = cell // width_z % width_y
    z_at = cell % width_z
    nowhere = -(4 * cells)

    def target(shift, ok):
        return jnp.where(live & ok, cell + shift, nowhere)

    targets = jnp.concatenate(
        [
            target(0, live),
            target(-width_z, y_at > 0),
            target(width_z, y_at < width_y - 1),
            target(-1, z_at > 0),
            target(1, z_at < width_z - 1),
            target(-plane, live),
            target(plane, live),
        ],
        axis=0,
    )

    block = slots * rows
    relative = np.zeros(devices, np.int32)
    came = np.zeros(devices, np.int32)
    shuffle = np.zeros((devices, block), np.int32)
    for place in range(devices):
        bits = [(place >> (steps - 1 - step)) & 1 for step in range(steps)]
        relative[place] = sum(bit << step for step, bit in enumerate(bits))
        came[relative[place]] = (bits[-1] << (steps - 1)) + (place >> 1)
        shuffle[place] = ((bits[-1] << (steps - 1)) + (place >> 1)) * block + np.arange(block)
    in_block = np.arange(block)
    by_row = (in_block // slots) * samples + in_block % slots
    dest = jnp.asarray(relative) ^ me
    row_from = (dest[:, None] * slots + jnp.asarray(by_row)[None]).reshape(-1, 1).astype(I32)
    source = jnp.asarray(came)[jnp.arange(devices) ^ me]
    final_from = (source[:, None] * block + jnp.asarray(in_block)[None]).reshape(-1, 1).astype(I32)
    shuffle = jnp.asarray(shuffle.reshape(-1, 1))

    acc, edge, got_in, got_side, center = pl.pallas_call(
        functools.partial(local_kernel, (params, layers, width_y, width_z, plane, samples)),
        out_shape=(
            shape((params * MB, cells), F32),
            shape((params, width_y, width_z), F32),
            shape((5 * samples, MB), BF16),
            shape((2 * samples, MB), BF16),
            shape((samples, cells), BF16),
        ),
        in_specs=[VMEM] * 6,
        out_specs=(VMEM,) * 5,
        scratch_shapes=[pltpu.VMEM((params, layers, OFFSETS, width_y, width_z), F32)],
        compiler_params=LIMIT,
        cost_estimate=pl.CostEstimate(flops=100_000_000, bytes_accessed=6_000_000, transcendentals=0),
        name="local_stencil",
    )(flat, face_speed, face_diffusion, upwind_flag, reaction, targets)

    size = own * params
    half = devices // 2
    count = half * block
    keep, keep_rows, packet = pl.pallas_call(
        functools.partial(project_kernel, (params, layers, width_y, width_z, plane, samples, devices, own)),
        out_shape=(
            shape((half * size, MB), F32),
            shape((count, MB), BF16),
            shape((2 * half * size + count, MB), BF16),
        ),
        in_specs=[SMEM] * 2 + [VMEM] * 10,
        out_specs=(VMEM,) * 3,
        scratch_shapes=[
            pltpu.VMEM((2, MB, plane), BF16),
            pltpu.VMEM((2, tail, width_z), F32),
            pltpu.VMEM((params * MB, cells), BF16),
            pltpu.VMEM((params * modes, MB), F32),
        ],
        compiler_params=LIMIT,
        name="project",
    )(odd, dest.astype(I32), flat, inner, outer, acc, edge, got_in, got_side, center, targets, row_from)

    wide = True
    for step in range(steps):
        got = lax.ppermute(packet, "cells", [(i, i ^ (1 << step)) for i in range(devices)])
        if step < steps - 1:
            next_wide = not 0 < step + 1 <= NARROW_STEPS
            half //= 2
            packet_rows = (2 if next_wide else 1) * half * size + count
            keep, keep_rows, packet = pl.pallas_call(
                functools.partial(merge_kernel, wide, next_wide),
                out_shape=(
                    shape((half * size, MB), F32),
                    shape((count, MB), BF16),
                    shape((packet_rows, MB), BF16),
                ),
                in_specs=[VMEM] * 4,
                out_specs=(VMEM,) * 3,
                compiler_params=LIMIT,
                name="merge",
            )(keep, keep_rows, got, shuffle)
            wide = next_wide
    volume = 1.0 / (layers * devices * width_y * width_z)
    summed, sampled = pl.pallas_call(
        functools.partial(final_kernel, wide, volume),
        out_shape=(shape((size, MB), F32), shape((2 * count, MB), BF16)),
        in_specs=[VMEM] * 4,
        out_specs=(VMEM,) * 2,
        compiler_params=LIMIT,
        name="finish",
    )(keep, keep_rows, got, final_from)
    galerkin = summed.reshape(own, params, MB)
    sampled = sampled.reshape(devices, rows, slots, MB)
    return (galerkin, jnp.transpose(sampled, (0, 2, 1, 3))[None])


def solution(mesh):
    return jax.shard_map(
        shards,
        mesh=mesh,
        in_specs=(
            P(None, ("groups", "cells"), None, None),
            P(None, None, ("groups", "cells"), None, None),
            P(None, None, ("groups", "cells"), None, None),
            P(None, None, ("groups", "cells"), None, None),
            P(None, ("groups", "cells"), None, None),
            P(("groups", "cells"), None, None),
            P(("groups", "cells"), None),
        ),
        out_specs=(
            P(("groups", "cells"), None, None),
            P(("groups", "cells"), None, None, None, None),
        ),
        check_vma=False,
    )
```

time: 38.5 us -> 36.4 us (0.945)
  blocking collectives: 22.4 us -> 0 us
  starting transfers between devices: 5.06 us -> 17.7 us
  waiting for transfers between devices: 0.01 us -> 7.94 us
  Pallas kernels: 3.36 us -> 5.86 us
  local copies, waits for them, and re-layouts: 5.51 us -> 3.59 us
  other arithmetic: 0.99 us -> 0.27 us
    all_to_all x1 -> x0, blocking collectives: 22.4 us -> none  [shards(): lax.all_to_all(payload, 'cells', split_axis=0, concat_axis=0, tiled=True)]
    ppermute x0 -> x4, starting transfers between devices: none -> 16.6 us  [shards(): lax.ppermute(packet, 'cells', [(i, i ^ 1 << step) for i in range(devices)])]
    ppermute x0 -> x4, waiting for transfers between devices: none -> 7.94 us  [shards(): lax.ppermute(packet, 'cells', [(i, i ^ 1 << step) for i in range(devices)])]
    ppermute x1, starting transfers between devices: 4.38 us -> 0.45 us  [shards(): inner = lax.ppermute(to_inner, 'cells', inner_pairs)]
    pallas_call x1 -> x7, Pallas kernels: 3.36 us -> 5.86 us  [the longest x1 2.03 us: shards(): pl.pallas_call(functools.partial(project_kernel, (params, layers, width_y...]
    unnamed x24 -> x22, local copies, waits for them, and re-layouts: 3.85 us -> 2.32 us
    slice x3 -> x0, local copies, waits for them, and re-layouts: 1.25 us -> none  [the longest x1 1.23 us: shards(): block = basis[:MB].reshape(MB, cells)]
    unnamed x1 -> x0, other arithmetic: 0.7 us -> none
  transfers between devices with their start and end apart: 2 -> 6, of which waited for: 0 -> 4; matrix products, arithmetic and copies ran while one was open for 3% -> 4% of each run, Pallas kernels for 0% -> 4%
where the time goes in v2:
time: 36.4 us; the launch traced here: 36.3 us
  starting transfers between devices  17.7 us (49%)
  waiting for transfers between devices  7.94 us (22%)
  Pallas kernels  5.86 us (16%)
  local copies, waits for them, and re-layouts  3.59 us (10%)
  between operations  0.91 us (2%)
    ppermute x4, starting transfers between devices, shards(): lax.ppermute(packet, 'cells', [(i, i ^ 1 << step) for i in range(devices)])  16.6 us
    ppermute x4, waiting for transfers between devices, shards(): lax.ppermute(packet, 'cells', [(i, i ^ 1 << step) for i in range(devices)])  7.94 us
    unnamed x22, local copies, waits for them, and re-layouts  2.32 us
    pallas_call x1, Pallas kernels, shards(): pl.pallas_call(functools.partial(project_kernel, (params, layers, width_y...  2.03 us
    pallas_call x1, Pallas kernels, shards(): pl.pallas_call(functools.partial(local_kernel, (params, layers, width_y,...  1.38 us
    pallas_call x1, Pallas kernels, shards(): pl.pallas_call(functools.partial(final_kernel, wide, volume), out_shape=(...  0.9 us
    pallas_call x3, Pallas kernels, shards(): pl.pallas_call(functools.partial(merge_kernel, wide, next_wide), out_shap...  0.79 us
    pallas_call x1, Pallas kernels, shards(): pl.pallas_call(functools.partial(pack_kernel, (params, layers, width_y, w...  0.76 us
  transfers between devices with their start and end apart: 6, of which 4 were waited for; matrix products, arithmetic and copies ran while one was open for 4% of the time, Pallas kernels for 4%

profile of v2, /device:TPU:0, one launch (start us, length us, event | category | flops | bytes accessed | tf_op | source)
XLA Modules:
  0.0 36.3 jit_solution(1938932987513920336)
XLA Ops:
  0.6 0.0 copy-start.1
  0.6 0.0 copy-start.2
  0.7 0.0 copy-start.3
  0.7 2.2 %copy.59 = bf16[64,8,16,128]{3,1,2,0:T(8,128)(2,1)S(1)} copy(bf16[64,8,16,128]{3,2,1,0:T(8,128)(2,1)} %bitcast.18) | data formatting | bytes 4194304
  2.8 0.0 copy-start.6
  2.9 0.0 copy-start.7
  2.9 0.0 copy-start.9
  2.9 0.0 copy-start.8
  2.9 0.0 copy-start.4
  2.9 0.0 copy-done.1
  2.9 0.0 copy-done.2
  2.9 0.0 copy-done.3
  2.9 0.8 %pack_halo.1 = (bf16[144,1024]{1,0:T(8,128)(2,1)}, bf16[144,1024]{1,0:T(8,128)(2,1)S(1)}) custom-call(s32[1]{0:T(128)} %bitcast.odd_ref, bf16[512,2048]{1,0:T(8,128)(2,1)S(1)} %bitcast.15, f32[2,3,2,8,128]{4,3,2,1,0:T(8,128)S(1)} %copy-done.1, f32[2,3,2,8,128]{4,3,2,1,0:T(8,128)S(1)} %copy-done.2, s32[2,3,2,8,128]{4,3,2,1,0:T(8,128)S(1)} %copy-done.3), custom_call_target="tpu_custom_call" | custom-call | tf_op jit(solution)/shard_map/pack_halo/pallas_call | solution.py:280
  3.7 0.5 %collective-permute-start = (bf16[144,1024]{1,0:T(8,128)(2,1)}, bf16[144,1024]{1,0:T(8,128)(2,1)S(1)}, u32[]{:S(2)}, u32[]{:S(2)}) collective-permute-start(bf16[144,1024]{1,0:T(8,128)(2,1)} %get-tuple-element.23), channel_id=1, source_target_pairs={{0,1},{1,0},{2,3},{3,2},{4,5},{5,4},{6,7},{7,6},{8,9},{9,8},{10,11... | collective-permute-start | bytes 884744 | tf_op jit(solution)/shard_map/ppermute | solution.py:293
  4.2 0.7 %collective-permute-start.1 = (bf16[144,1024]{1,0:T(8,128)(2,1)S(1)}, bf16[144,1024]{1,0:T(8,128)(2,1)S(1)}, u32[]{:S(2)}, u32[]{:S(2)}) collective-permute-start(bf16[144,1024]{1,0:T(8,128)(2,1)S(1)} %get-tuple-element.24), channel_id=1, source_target_pairs={{1,2},{2,1},{3,4},{4,3},{5,6},{6,5},{7,8},{8,7},{9,10},{10,9},{11,... | collective-permute-start | bytes 884744 | tf_op jit(solution)/shard_map/ppermute | solution.py:292
  4.8 0.0 copy-done.6
  4.8 0.1 copy.52
  4.9 0.1 reshape_squeeze.3
  5.0 0.0 copy-done.7
  5.0 0.1 iota_compare_fusion
  5.1 0.1 lt.103
  5.2 0.0 copy-done.9
  5.3 0.1 concatenate.3
  5.4 0.1 copy.53.cell_ref
  5.5 0.0 copy-done.8
  5.5 0.1 broadcast_add_fusion
  5.6 0.1 add.206.row_ref
  5.7 0.0 copy-done.4
  5.7 1.4 %local_stencil.1 = (f32[256,2048]{1,0:T(8,128)S(1)}, f32[2,8,128]{2,1,0:T(8,128)S(1)}, bf16[160,128]{1,0:T(8,128)(2,1)S(1)}, bf16[64,128]{1,0:T(8,128)(2,1)S(1)}, bf16[32,2048]{1,0:T(8,128)(2,1)S(1)}) custom-call(bf16[512,2048]{1,0:T(8,128)(2,1)S(1)} %bitcast.16, f32[2,3,2,8,128]{4,3,2,1,0:T(8,128)S(1)} %copy-done.1, f32[2,3,2,8,128]{4,3,2,1,0:T(8,128)S(1)} %copy-done.2, ...), custom_call_target="tpu_custom_call" | custom-call | flops 100000000 | bytes 6000000 | tf_op jit(solution)/shard_map/local_stencil/pallas_call | solution.py:335
  7.1 0.0 collective-permute-done.inner_ref
  7.1 0.0 collective-permute-done.1.outer_ref
  7.1 0.0 copy-start
  7.1 0.0 copy-start.5
  7.1 2.0 %project.1 = (f32[512,128]{1,0:T(8,128)S(1)}, bf16[144,128]{1,0:T(8,128)(2,1)S(1)}, bf16[1168,128]{1,0:T(8,128)(2,1)S(1)}) custom-call(s32[1]{0:T(128)} %bitcast.odd_ref, s32[16]{0:T(128)S(1)} %get-tuple-element.56.dest_ref, bf16[512,2048]{1,0:T(8,128)(2,1)S(1)} %bitcast.17, bf16[144,1024]{1,0:T(8,128)(2,1)S(1)} %collective-permute-done.inner_ref, ...), custom_call_target="tpu_custom_call" | custom-call | tf_op jit(solution)/shard_map/project/pallas_call | solution.py:355
  9.2 8.4 %collective-permute-start.2 = (bf16[1168,128]{1,0:T(8,128)(2,1)S(1)}, bf16[1168,128]{1,0:T(8,128)(2,1)S(1)}, u32[]{:S(2)}, u32[]{:S(2)}) collective-permute-start(bf16[1168,128]{1,0:T(8,128)(2,1)S(1)} %get-tuple-element.32), channel_id=1, source_target_pairs={{0,1},{1,0},{2,3},{3,2},{4,5},{5,4},{6,7},{7,6},{8,9},{9,8},{10,11... | collective-permute-start | bytes 897032 | tf_op jit(solution)/shard_map/ppermute | solution.py:376
  17.6 1.2 %collective-permute-done.2.got_ref = bf16[1168,128]{1,0:T(8,128)(2,1)S(1)} collective-permute-done((bf16[1168,128]{1,0:T(8,128)(2,1)S(1)}, bf16[1168,128]{1,0:T(8,128)(2,1)S(1)}, u32[]{:S(2)}, u32[]{:S(2)}) %collective-permute-start.2) | collective-permute-done | bytes 299040 | tf_op jit(solution)/shard_map/ppermute | solution.py:376
  18.8 0.0 copy-done
  18.8 0.3 merge.3
  19.1 2.8 %collective-permute-start.3 = (bf16[400,128]{1,0:T(8,128)(2,1)S(1)}, bf16[400,128]{1,0:T(8,128)(2,1)S(1)}, u32[]{:S(2)}, u32[]{:S(2)}) collective-permute-start(bf16[400,128]{1,0:T(8,128)(2,1)S(1)} %get-tuple-element.35), channel_id=1, source_target_pairs={{0,2},{1,3},{2,0},{3,1},{4,6},{5,7},{6,4},{7,5},{8,10},{9,11},{10,... | collective-permute-start | bytes 307208 | tf_op jit(solution)/shard_map/ppermute | solution.py:376
  21.9 0.0 copy-done.5
  21.9 0.7 %gather_fusion = s32[16]{0:T(128)S(1)} fusion(s32[16]{0:T(128)S(1)} %copy-done.5, s32[1024]{0:T(1024)S(1)} %pad_clamp_fusion), kind=kCustom, calls=%fused_computation | custom fusion | bytes 192 | tf_op jit(solution)/shard_map/gather | solution.py:331
  22.6 2.5 %collective-permute-done.3.got_ref = bf16[400,128]{1,0:T(8,128)(2,1)S(1)} collective-permute-done((bf16[400,128]{1,0:T(8,128)(2,1)S(1)}, bf16[400,128]{1,0:T(8,128)(2,1)S(1)}, u32[]{:S(2)}, u32[]{:S(2)}) %collective-permute-start.3) | collective-permute-done | bytes 102432 | tf_op jit(solution)/shard_map/ppermute | solution.py:376
  25.1 0.3 merge.4
  25.3 2.2 %collective-permute-start.4 = (bf16[272,128]{1,0:T(8,128)(2,1)S(1)}, bf16[272,128]{1,0:T(8,128)(2,1)S(1)}, u32[]{:S(2)}, u32[]{:S(2)}) collective-permute-start(bf16[272,128]{1,0:T(8,128)(2,1)S(1)} %get-tuple-element.38), channel_id=1, source_target_pairs={{0,4},{1,5},{2,6},{3,7},{4,0},{5,1},{6,2},{7,3},{8,12},{9,13},{10,... | collective-permute-start | bytes 208904 | tf_op jit(solution)/shard_map/ppermute | solution.py:376
  27.6 2.3 %collective-permute-done.4.got_ref = bf16[272,128]{1,0:T(8,128)(2,1)S(1)} collective-permute-done((bf16[272,128]{1,0:T(8,128)(2,1)S(1)}, bf16[272,128]{1,0:T(8,128)(2,1)S(1)}, u32[]{:S(2)}, u32[]{:S(2)}) %collective-permute-start.4) | collective-permute-done | bytes 69664 | tf_op jit(solution)/shard_map/ppermute | solution.py:376
  29.9 0.3 merge.5
  30.1 3.1 %collective-permute-start.5 = (bf16[208,128]{1,0:T(8,128)(2,1)S(1)}, bf16[208,128]{1,0:T(8,128)(2,1)S(1)}, u32[]{:S(2)}, u32[]{:S(2)}) collective-permute-start(bf16[208,128]{1,0:T(8,128)(2,1)S(1)} %get-tuple-element.41), channel_id=1, source_target_pairs={{0,8},{1,9},{2,10},{3,11},{4,12},{5,13},{6,14},{7,15},{8,0},{9,1},... | collective-permute-start | bytes 159752 | tf_op jit(solution)/shard_map/ppermute | solution.py:376
  33.2 0.1 iota_add_fusion
  33.3 0.1 add.207.final_ref
  33.4 1.9 %collective-permute-done.5.got_ref = bf16[208,128]{1,0:T(8,128)(2,1)S(1)} collective-permute-done((bf16[208,128]{1,0:T(8,128)(2,1)S(1)}, bf16[208,128]{1,0:T(8,128)(2,1)S(1)}, u32[]{:S(2)}, u32[]{:S(2)}) %collective-permute-start.5) | collective-permute-done | bytes 53280 | tf_op jit(solution)/shard_map/ppermute | solution.py:376
  35.3 0.9 %finish.1 = (f32[64,128]{1,0:T(8,128)}, bf16[288,128]{1,0:T(8,128)(2,1)}) custom-call(f32[64,128]{1,0:T(8,128)S(1)} %get-tuple-element.39.keep_ref, bf16[144,128]{1,0:T(8,128)(2,1)S(1)} %get-tuple-element.40.keep_rows_ref, bf16[208,128]{1,0:T(8,128)(2,1)S(1)} %collective-permute-done.5.got_ref, s32[288,1]{1,0:T(8,128)S(1)} %add.207.final_ref), custom_call_target="tpu_custom_call" | custom-call | tf_op jit(solution)/shard_map/finish/pallas_call | solution.py:395
  (6 shorter events, 0.0 us)
Async XLA Ops:
  0.6 2.3 %copy-start.1 = (f32[2,3,2,8,128]{4,3,2,1,0:T(8,128)S(1)}, f32[2,3,2,8,128]{4,3,2,1,0:T(8,128)}, u32[]{:S(2)}) copy-start(f32[2,3,2,8,128]{4,3,2,1,0:T(8,128)} %speed_ref.3) | copy-start | bytes 147460
  0.6 2.3 %copy-start.2 = (f32[2,3,2,8,128]{4,3,2,1,0:T(8,128)S(1)}, f32[2,3,2,8,128]{4,3,2,1,0:T(8,128)}, u32[]{:S(2)}) copy-start(f32[2,3,2,8,128]{4,3,2,1,0:T(8,128)} %diff_ref.3) | copy-start | bytes 147460
  0.7 2.3 %copy-start.3 = (s32[2,3,2,8,128]{4,3,2,1,0:T(8,128)S(1)}, s32[2,3,2,8,128]{4,3,2,1,0:T(8,128)}, u32[]{:S(2)}) copy-start(s32[2,3,2,8,128]{4,3,2,1,0:T(8,128)} %flag_ref.3) | copy-start | bytes 147460
  2.8 2.0 %copy-start.6 = (s32[1,16,2]{1,2,0:T(2,128)S(1)}, s32[1,16,2]{1,2,0:T(2,128)}, u32[]{:S(2)}) copy-start(s32[1,16,2]{1,2,0:T(2,128)} %param.17) | copy-start | bytes 388
  2.9 2.2 %copy-start.7 = (s32[1,16]{1,0:T(1,128)S(1)}, s32[1,16]{1,0:T(1,128)}, u32[]{:S(2)}) copy-start(s32[1,16]{1,0:T(1,128)} %param.18) | copy-start | bytes 196
  2.9 2.4 %copy-start.9 = (s32[16]{0:T(128)S(1)}, s32[16]{0:T(128)}, u32[]{:S(2)}) copy-start(s32[16]{0:T(128)} %constant.83.clone) | copy-start | bytes 196
  2.9 2.6 %copy-start.8 = (s32[18]{0:T(128)S(1)}, s32[18]{0:T(128)}, u32[]{:S(2)}) copy-start(s32[18]{0:T(128)} %constant.84.clone) | copy-start | bytes 220
  2.9 2.8 %copy-start.4 = (f32[2,2,8,128]{3,2,1,0:T(8,128)S(1)}, f32[2,2,8,128]{3,2,1,0:T(8,128)}, u32[]{:S(2)}) copy-start(f32[2,2,8,128]{3,2,1,0:T(8,128)} %react_ref.1) | copy-start | bytes 49156
  3.7 3.4 %collective-permute-start = (bf16[144,1024]{1,0:T(8,128)(2,1)}, bf16[144,1024]{1,0:T(8,128)(2,1)S(1)}, u32[]{:S(2)}, u32[]{:S(2)}) collective-permute-start(bf16[144,1024]{1,0:T(8,128)(2,1)} %get-tuple-element.23), channel_id=1, source_target_pairs={{0,1},{1,0},{2,3},{3,2},{4,5},{5,4},{6,7},{7,6},{8,9},{9,8},{10,11... | collective-permute-start | bytes 884744 | tf_op jit(solution)/shard_map/ppermute | solution.py:293
  4.2 2.9 %collective-permute-start.1 = (bf16[144,1024]{1,0:T(8,128)(2,1)S(1)}, bf16[144,1024]{1,0:T(8,128)(2,1)S(1)}, u32[]{:S(2)}, u32[]{:S(2)}) collective-permute-start(bf16[144,1024]{1,0:T(8,128)(2,1)S(1)} %get-tuple-element.24), channel_id=1, source_target_pairs={{1,2},{2,1},{3,4},{4,3},{5,6},{6,5},{7,8},{8,7},{9,10},{10,9},{11,... | collective-permute-start | bytes 884744 | tf_op jit(solution)/shard_map/ppermute | solution.py:292
  7.1 11.7 %copy-start = (s32[288,1]{1,0:T(8,128)S(1)}, s32[288,1]{1,0:T(8,128)}, u32[]{:S(2)}) copy-start(s32[288,1]{1,0:T(8,128)} %constant.86.clone.shuffle_ref) | copy-start | bytes 3460
  7.1 14.8 %copy-start.5 = (s32[16]{0:T(128)S(1)}, s32[16]{0:T(128)}, u32[]{:S(2)}) copy-start(s32[16]{0:T(128)} %constant.85.clone) | copy-start | bytes 196
  9.2 9.6 %collective-permute-start.2 = (bf16[1168,128]{1,0:T(8,128)(2,1)S(1)}, bf16[1168,128]{1,0:T(8,128)(2,1)S(1)}, u32[]{:S(2)}, u32[]{:S(2)}) collective-permute-start(bf16[1168,128]{1,0:T(8,128)(2,1)S(1)} %get-tuple-element.32), channel_id=1, source_target_pairs={{0,1},{1,0},{2,3},{3,2},{4,5},{5,4},{6,7},{7,6},{8,9},{9,8},{10,11... | collective-permute-start | bytes 897032 | tf_op jit(solution)/shard_map/ppermute | solution.py:376
  19.1 6.0 %collective-permute-start.3 = (bf16[400,128]{1,0:T(8,128)(2,1)S(1)}, bf16[400,128]{1,0:T(8,128)(2,1)S(1)}, u32[]{:S(2)}, u32[]{:S(2)}) collective-permute-start(bf16[400,128]{1,0:T(8,128)(2,1)S(1)} %get-tuple-element.35), channel_id=1, source_target_pairs={{0,2},{1,3},{2,0},{3,1},{4,6},{5,7},{6,4},{7,5},{8,10},{9,11},{10,... | collective-permute-start | bytes 307208 | tf_op jit(solution)/shard_map/ppermute | solution.py:376
  25.3 4.5 %collective-permute-start.4 = (bf16[272,128]{1,0:T(8,128)(2,1)S(1)}, bf16[272,128]{1,0:T(8,128)(2,1)S(1)}, u32[]{:S(2)}, u32[]{:S(2)}) collective-permute-start(bf16[272,128]{1,0:T(8,128)(2,1)S(1)} %get-tuple-element.38), channel_id=1, source_target_pairs={{0,4},{1,5},{2,6},{3,7},{4,0},{5,1},{6,2},{7,3},{8,12},{9,13},{10,... | collective-permute-start | bytes 208904 | tf_op jit(solution)/shard_map/ppermute | solution.py:376
  30.1 5.2 %collective-permute-start.5 = (bf16[208,128]{1,0:T(8,128)(2,1)S(1)}, bf16[208,128]{1,0:T(8,128)(2,1)S(1)}, u32[]{:S(2)}, u32[]{:S(2)}) collective-permute-start(bf16[208,128]{1,0:T(8,128)(2,1)S(1)} %get-tuple-element.41), channel_id=1, source_target_pairs={{0,8},{1,9},{2,10},{3,11},{4,12},{5,13},{6,14},{7,15},{8,0},{9,1},... | collective-permute-start | bytes 159752 | tf_op jit(solution)/shard_map/ppermute | solution.py:376

commit v3 on v2

--- a/solution.py
+++ b/solution.py
@@ -16,7 +16,6 @@
 I32 = jnp.int32
 OFFSETS = 7
 VMEM = pl.BlockSpec(memory_space=pltpu.VMEM)
-SMEM = pl.BlockSpec(memory_space=pltpu.SMEM)
 LIMIT = pltpu.CompilerParams(vmem_limit_bytes=40 * 1024 * 1024)
 
 
@@ -34,27 +33,37 @@
     return head, (value - head.astype(F32)).astype(BF16)
 
 
-def pack_kernel(dims, odd_ref, flat_ref, speed_ref, diff_ref, flag_ref, inner_ref, outer_ref):
-    params, layers, width_y, width_z, plane = dims
-    odd = odd_ref[0]
-    last = (layers - 1) * plane
-    to_inner = pl.multiple_of((1 - odd) * last, width_z)
-    to_outer = pl.multiple_of(odd * last, width_z)
-    inner_ref[:MB] = flat_ref[:MB, pl.ds(to_inner, plane)]
-    outer_ref[:MB] = flat_ref[:MB, pl.ds(to_outer, plane)]
-    speed = speed_ref[:, 0, layers - 1].reshape(params * width_y, width_z)
-    forward = flag_ref[:, 0, layers - 1].reshape(params * width_y, width_z) == 1
-    signed = jnp.where(forward, speed, -speed)
-    diff = diff_ref[:, 0, layers - 1].reshape(params * width_y, width_z)
-    for ref in (inner_ref, outer_ref):
-        ref[MB:] = jnp.zeros((params * width_y, plane), BF16)
-    for at, value in enumerate((signed, diff)):
-        for part in range(SPLITS):
+def core():
+    return lax.rem(lax.axis_index("cells"), 2)
+
+
+def face_parts(speed, diff, flag):
+    parts = []
+    for value in (jnp.where(flag == 1, speed, -speed), diff):
+        for _ in range(SPLITS):
             head = value.astype(BF16)
             value = value - head.astype(F32)
-            lane = (at * SPLITS + part) * width_z
-            inner_ref[MB:, lane : lane + width_z] = head
-            outer_ref[MB:, lane : lane + width_z] = head
+            parts.append(head)
+    return parts
+
+
+def pack_kernel(dims, basis_ref, speed_ref, diff_ref, flag_ref, outer_ref, speed_buf, diff_buf, flag_buf, sems):
+    params, layers = dims
+    last = layers - 1
+    layer = core() * last
+    copies = [
+        pltpu.make_async_copy(basis_ref.at[pl.ds(0, MB), layer], outer_ref.at[pl.ds(0, MB)], sems.at[0]),
+        pltpu.make_async_copy(speed_ref.at[:, 0, last], speed_buf, sems.at[1]),
+        pltpu.make_async_copy(diff_ref.at[:, 0, last], diff_buf, sems.at[2]),
+        pltpu.make_async_copy(flag_ref.at[:, 0, last], flag_buf, sems.at[3]),
+    ]
+    for copy in copies:
+        copy.start()
+    for copy in copies[1:]:
+        copy.wait()
+    for at, part in enumerate(face_parts(speed_buf[...], diff_buf[...], flag_buf[...])):
+        outer_ref[MB + at * params : MB + (at + 1) * params] = part
+    copies[0].wait()
 
 
 def local_kernel(
@@ -70,6 +79,7 @@
     in_ref,
     side_ref,
     center_ref,
+    inner_ref,
     coef_ref,
 ):
     params, layers, width_y, width_z, plane, samples = dims
@@ -128,6 +138,13 @@
                     total = product if total is None else total + product
                 acc_ref[param * MB : (param + 1) * MB, start : start + width_z] = total
 
+    start = pl.multiple_of((1 - core()) * (layers - 1) * plane, plane)
+    inner_ref[:MB] = flat_ref[:MB, pl.ds(start, plane)]
+    inner_ref[MB:] = jnp.zeros((params * width_y, plane), BF16)
+    faces = [ref[:, 0, layers - 1].reshape(params * width_y, width_z) for ref in (speed_ref, diff_ref, flag_ref)]
+    for at, part in enumerate(face_parts(*faces)):
+        inner_ref[MB:, at * width_z : (at + 1) * width_z] = part
+
     cells = layers * plane
     block = flat_ref[:MB, :]
     inside = picked(cell_ref[: 5 * samples], 0, cells)
@@ -137,68 +154,82 @@
     side_ref[samples:] = nt_dot(picked(cell_ref[6 * samples :], 0, cells), block).astype(BF16)
 
 
+def finish_layer(dims, from_next, layer, faces, halo, flat_ref, acc_ref, edge_ref, applied_ref, coef_ref):
+    params, layers, width_y, width_z, plane = dims
+    signed = faces[0] + faces[1] + faces[2]
+    diff = faces[3] + faces[4] + faces[5]
+    edge = edge_ref[...].reshape(params * width_y, width_z)
+    coef_ref[0] = jnp.where(from_next, edge, -(jnp.maximum(signed, 0.0) + diff))
+    coef_ref[1] = jnp.where(from_next, 0.0, diff - jnp.minimum(signed, 0.0))
+    for y in range(width_y):
+        at = pl.multiple_of(layer * plane + y * width_z, width_z)
+        lanes = slice(y * width_z, (y + 1) * width_z)
+        state = flat_ref[:MB, pl.ds(at, width_z)].astype(F32)
+        beside = halo[:MB, lanes].astype(F32)
+        for param in range(params):
+            modes = slice(param * MB, (param + 1) * MB)
+            row = param * width_y + y
+            total = acc_ref[modes, pl.ds(at, width_z)]
+            total = total + coef_ref[1, row : row + 1, :] * state
+            total = total + coef_ref[0, row : row + 1, :] * beside
+            applied_ref[modes, lanes] = total.astype(BF16)
+
+
+def near_kernel(dims, flat_ref, inner_ref, acc_ref, edge_ref, center_ref, cell_ref, sums_ref, picks_ref, side_ref, applied_ref, coef_ref):
+    params, layers, width_y, width_z, plane, samples = dims
+    odd = core() == 1
+    layer = (1 - core()) * (layers - 1)
+    start = pl.multiple_of(layer * plane, plane)
+    faces = [inner_ref[MB:, at * width_z : (at + 1) * width_z].astype(F32) for at in range(2 * SPLITS)]
+    finish_layer(dims[:5], jnp.logical_not(odd), layer, faces, inner_ref, flat_ref, acc_ref, edge_ref, applied_ref, coef_ref)
+    sums_ref[...] = nt_dot(flat_ref[:, pl.ds(start, plane)], applied_ref[...])
+    picks_ref[...] = nt_dot(center_ref[:, pl.ds(start, plane)], applied_ref[...])
+    below = cell_ref[5 * samples : 6 * samples] + plane
+    above = cell_ref[6 * samples :] - layers * plane
+    side_ref[...] = nt_dot(picked(jnp.where(odd, below, above), 0, plane), inner_ref[:MB]).astype(BF16)
+
+
 def project_kernel(
     dims,
-    odd_ref,
-    dest_ref,
+    relative,
     flat_ref,
-    inner_ref,
     outer_ref,
+    tail_ref,
     acc_ref,
     edge_ref,
     in_ref,
     side_ref,
     center_ref,
+    near_sums_ref,
+    near_picks_ref,
+    near_side_ref,
     cell_ref,
     row_ref,
     keep_ref,
     keep_rows_ref,
     packet_ref,
-    halo_ref,
-    prev_ref,
     applied_ref,
+    coef_ref,
     sums_ref,
 ):
     params, layers, width_y, width_z, plane, samples, devices, own = dims
-    cells = layers * plane
-    odd = odd_ref[0] == 1
-    halo_ref[0] = jnp.where(odd, inner_ref[:MB], outer_ref[:MB])
-    halo_ref[1] = jnp.where(odd, outer_ref[:MB], inner_ref[:MB])
-    tail = jnp.where(odd, inner_ref[MB:], outer_ref[MB:]).astype(F32)
+    odd = core() == 1
+    layer = core() * (layers - 1)
+    lane = pl.multiple_of(layer * plane, plane)
     faces = []
-    for at in range(2):
-        value = None
-        for part in range(SPLITS):
-            lane = (at * SPLITS + part) * width_z
-            piece = tail[:, lane : lane + width_z]
-            value = piece if value is None else value + piece
-        faces.append(value)
-    signed_prev, diff_prev = faces
-    prev_ref[0] = -(jnp.maximum(signed_prev, 0.0) + diff_prev)
-    prev_ref[1] = diff_prev - jnp.minimum(signed_prev, 0.0)
-
-    for layer in range(layers):
-        for y in range(width_y):
-            start = layer * plane + y * width_z
-            lanes = slice(y * width_z, (y + 1) * width_z)
-            for param in range(params):
-                modes = slice(param * MB, (param + 1) * MB)
-                total = acc_ref[modes, start : start + width_z]
-                row = param * width_y + y
-                if layer == 0:
-                    total = total + prev_ref[1, row : row + 1, :] * flat_ref[:MB, start : start + width_z].astype(F32)
-                    total = total + prev_ref[0, row : row + 1, :] * halo_ref[0, :, lanes].astype(F32)
-                if layer == layers - 1:
-                    total = total + edge_ref[param, y : y + 1, :] * halo_ref[1, :, lanes].astype(F32)
-                applied_ref[modes, start : start + width_z] = total.astype(BF16)
-
-    sums = nt_dot(flat_ref[...], applied_ref[...])
+    for at in range(2 * SPLITS):
+        part = tail_ref[MB + at * params : MB + (at + 1) * params].astype(F32)
+        faces.append(part.reshape(params * width_y, width_z))
+    finish_layer(dims[:5], odd, layer, faces, outer_ref, flat_ref, acc_ref, edge_ref, applied_ref, coef_ref)
+
+    sums = near_sums_ref[...] + nt_dot(flat_ref[:, pl.ds(lane, plane)], applied_ref[...])
     for param in range(params):
         sums_ref[pl.ds(param, sums.shape[0], stride=params), :] = sums[:, param * MB : (param + 1) * MB]
     size = own * params
     half = devices // 2
+    me = lax.axis_index("cells")
     for place in range(devices):
-        start = pl.multiple_of(dest_ref[place] * size, size)
+        start = pl.multiple_of((me ^ relative[place]) * size, size)
         terms = sums_ref[pl.ds(start, size), :]
         if place < half:
             keep_ref[place * size : (place + 1) * size] = terms
@@ -208,11 +239,14 @@
             packet_ref[at : at + size] = head
             packet_ref[half * size + at : half * size + at + size] = rest
 
-    got_applied = nt_dot(center_ref[...], applied_ref[...]).astype(BF16)
-    below = picked(cell_ref[5 * samples : 6 * samples], -plane, plane)
-    above = picked(cell_ref[6 * samples :], cells, plane)
-    got_below = nt_dot(below, halo_ref[0]).astype(BF16) + side_ref[:samples]
-    got_above = nt_dot(above, halo_ref[1]).astype(BF16) + side_ref[samples:]
+    picks = nt_dot(center_ref[:, pl.ds(lane, plane)], applied_ref[...])
+    got_applied = (near_picks_ref[...] + picks).astype(BF16)
+    below = cell_ref[5 * samples : 6 * samples] + plane
+    above = cell_ref[6 * samples :] - layers * plane
+    far = nt_dot(picked(jnp.where(odd, above, below), 0, plane), outer_ref[...]).astype(BF16)
+    near = near_side_ref[...]
+    got_below = side_ref[:samples] + jnp.where(odd, near, far)
+    got_above = side_ref[samples:] + jnp.where(odd, far, near)
     pieces = [got_applied[:, param * MB : (param + 1) * MB] for param in range(params)]
     pieces += [in_ref[:samples], got_below, got_above, in_ref[samples:]]
     gathered = jnp.concatenate(pieces, axis=0)
@@ -271,26 +305,30 @@
     rows = params + OFFSETS
     samples = devices * slots
     me = lax.axis_index("cells")
-    odd = (me % 2).astype(I32).reshape(1)
     steps = devices.bit_length() - 1
 
-    flat = basis.reshape(modes, cells)
     tail = params * width_y
-    halo = shape((MB + tail, plane), BF16)
-    to_inner, to_outer = pl.pallas_call(
-        functools.partial(pack_kernel, (params, layers, width_y, width_z, plane)),
-        out_shape=(halo, halo),
-        in_specs=[SMEM] + [VMEM] * 4,
-        out_specs=(VMEM, VMEM),
+    hbm = pl.BlockSpec(memory_space=pl.ANY)
+    to_outer = pl.pallas_call(
+        functools.partial(pack_kernel, (params, layers)),
+        out_shape=shape((MB + 2 * SPLITS * params, width_y, width_z), BF16),
+        in_specs=[hbm] * 4,
+        out_specs=VMEM,
+        scratch_shapes=[
+            pltpu.VMEM((params, width_y, width_z), F32),
+            pltpu.VMEM((params, width_y, width_z), F32),
+            pltpu.VMEM((params, width_y, width_z), I32),
+            pltpu.SemaphoreType.DMA((4,)),
+        ],
         compiler_params=LIMIT,
-        name="pack_halo",
-    )(odd, flat, face_speed, face_diffusion, upwind_flag)
+        name="pack_outer",
+    )(basis, face_speed, face_diffusion, upwind_flag)
     inner_pairs = [(i, i ^ 1) for i in range(devices)]
     outer_pairs = []
     for i in range(1, devices - 1, 2):
         outer_pairs += [(i, i + 1), (i + 1, i)]
     outer = lax.ppermute(to_outer, "cells", outer_pairs)
-    inner = lax.ppermute(to_inner, "cells", inner_pairs)
+    flat = basis.reshape(modes, cells)
 
     cell = sample_cell[0].reshape(samples, 1)
     slot_at = lax.broadcasted_iota(I32, (devices, slots), 1)
@@ -332,7 +370,7 @@
     final_from = (source[:, None] * block + jnp.asarray(in_block)[None]).reshape(-1, 1).astype(I32)
     shuffle = jnp.asarray(shuffle.reshape(-1, 1))
 
-    acc, edge, got_in, got_side, center = pl.pallas_call(
+    acc, edge, got_in, got_side, center, to_inner = pl.pallas_call(
         functools.partial(local_kernel, (params, layers, width_y, width_z, plane, samples)),
         out_shape=(
             shape((params * MB, cells), F32),
@@ -340,36 +378,70 @@
             shape((5 * samples, MB), BF16),
             shape((2 * samples, MB), BF16),
             shape((samples, cells), BF16),
+            shape((MB + tail, plane), BF16),
         ),
         in_specs=[VMEM] * 6,
-        out_specs=(VMEM,) * 5,
+        out_specs=(VMEM,) * 6,
         scratch_shapes=[pltpu.VMEM((params, layers, OFFSETS, width_y, width_z), F32)],
         compiler_params=LIMIT,
         cost_estimate=pl.CostEstimate(flops=100_000_000, bytes_accessed=6_000_000, transcendentals=0),
         name="local_stencil",
     )(flat, face_speed, face_diffusion, upwind_flag, reaction, targets)
 
+    inner = lax.ppermute(to_inner, "cells", inner_pairs)
+    near_sums, near_picks, near_side = pl.pallas_call(
+        functools.partial(near_kernel, (params, layers, width_y, width_z, plane, samples)),
+        out_shape=(
+            shape((modes, params * MB), F32),
+            shape((samples, params * MB), F32),
+            shape((samples, MB), BF16),
+        ),
+        in_specs=[VMEM] * 6,
+        out_specs=(VMEM,) * 3,
+        scratch_shapes=[pltpu.VMEM((params * MB, plane), BF16), pltpu.VMEM((2, tail, width_z), F32)],
+        compiler_params=LIMIT,
+        cost_estimate=pl.CostEstimate(flops=300_000_000, bytes_accessed=4_000_000, transcendentals=0),
+        name="near_layer",
+    )(flat, inner, acc, edge, center, targets)
+
     size = own * params
     half = devices // 2
     count = half * block
     keep, keep_rows, packet = pl.pallas_call(
-        functools.partial(project_kernel, (params, layers, width_y, width_z, plane, samples, devices, own)),
+        functools.partial(
+            project_kernel,
+            (params, layers, width_y, width_z, plane, samples, devices, own),
+            tuple(int(value) for value in relative),
+        ),
         out_shape=(
             shape((half * size, MB), F32),
             shape((count, MB), BF16),
             shape((2 * half * size + count, MB), BF16),
         ),
-        in_specs=[SMEM] * 2 + [VMEM] * 10,
+        in_specs=[VMEM] * 13,
         out_specs=(VMEM,) * 3,
         scratch_shapes=[
-            pltpu.VMEM((2, MB, plane), BF16),
+            pltpu.VMEM((params * MB, plane), BF16),
             pltpu.VMEM((2, tail, width_z), F32),
-            pltpu.VMEM((params * MB, cells), BF16),
             pltpu.VMEM((params * modes, MB), F32),
         ],
         compiler_params=LIMIT,
         name="project",
-    )(odd, dest.astype(I32), flat, inner, outer, acc, edge, got_in, got_side, center, targets, row_from)
+    )(
+        flat,
+        outer[:MB].reshape(MB, plane),
+        outer,
+        acc,
+        edge,
+        got_in,
+        got_side,
+        center,
+        near_sums,
+        near_picks,
+        near_side,
+        targets,
+        row_from,
+    )
 
     wide = True
     for step in range(steps):

time: 36.4 us -> 42 us (1.15)
  local copies, waits for them, and re-layouts: 3.59 us -> 6.67 us
  starting transfers between devices: 17.7 us -> 19 us
  waiting for transfers between devices: 7.94 us -> 8.71 us
  other arithmetic: 0.27 us -> 0.92 us
    unnamed x22 -> x29, local copies, waits for them, and re-layouts: 2.32 us -> 5.38 us
    ppermute x4, starting transfers between devices: 16.6 us -> 17.9 us  [shards(): lax.ppermute(packet, 'cells', [(i, i ^ 1 << step) for i in range(devices)])]
    pallas_call x1, Pallas kernels: 2.03 us -> 0.93 us  [shards(): pl.pallas_call(functools.partial(project_kernel, (params, layers, width_y...]
    ppermute x4, waiting for transfers between devices: 7.94 us -> 8.71 us  [shards(): lax.ppermute(packet, 'cells', [(i, i ^ 1 << step) for i in range(devices)])]
    pallas_call x1, Pallas kernels: 1.38 us -> 2.06 us  [shards(): pl.pallas_call(functools.partial(local_kernel, (params, layers, width_y,...]
    lt x1, other arithmetic: 0.07 us -> 0.73 us  [shards(): live = (slot_at < sample_count[0][:, None]).reshape(samples, 1)]
    pallas_call x1 -> x2, Pallas kernels: 0.76 us -> 0.94 us  [the longest x1 0.83 us: shards(): pl.pallas_call(functools.partial(near_kernel, (params, layers, width_y, w...]
  transfers between devices with their start and end apart: 6 -> 6, of which waited for: 4 -> 4; matrix products, arithmetic and copies ran while one was open for 4% -> 3% of each run, Pallas kernels for 4% -> 0%
where the time goes in v3:
time: 42 us; the launch traced here: 41.8 us
  starting transfers between devices  19 us (45%)
  waiting for transfers between devices  8.71 us (21%)
  local copies, waits for them, and re-layouts  6.67 us (16%)
  Pallas kernels  5.62 us (13%)
  other arithmetic  0.92 us (2%)
  between operations  0.92 us (2%)
    ppermute x4, starting transfers between devices, shards(): lax.ppermute(packet, 'cells', [(i, i ^ 1 << step) for i in range(devices)])  17.9 us
    ppermute x4, waiting for transfers between devices, shards(): lax.ppermute(packet, 'cells', [(i, i ^ 1 << step) for i in range(devices)])  8.71 us
    unnamed x29, local copies, waits for them, and re-layouts  5.38 us
    pallas_call x1, Pallas kernels, shards(): pl.pallas_call(functools.partial(local_kernel, (params, layers, width_y,...  2.06 us
    pallas_call x1, Pallas kernels, shards(): pl.pallas_call(functools.partial(project_kernel, (params, layers, width_y...  0.93 us
    pallas_call x1, Pallas kernels, shards(): pl.pallas_call(functools.partial(final_kernel, wide, volume), out_shape=(...  0.9 us
  transfers between devices with their start and end apart: 6, of which 4 were waited for; matrix products, arithmetic and copies ran while one was open for 3% of the time, Pallas kernels for 0%

profile of v3, /device:TPU:0, one launch (start us, length us, event | category | flops | bytes accessed | tf_op | source)
XLA Modules:
  0.0 41.8 jit_solution(12646794795313289595)
XLA Ops:
  0.6 0.8 %copy.52 = s32[1,16,2]{2,1,0:T(8,128)S(1)} copy(s32[1,16,2]{1,2,0:T(2,128)} %param.17) | data formatting | bytes 256 | tf_op args[5]
  1.4 0.1 reshape_squeeze.3
  1.5 0.7 %iota_compare_fusion = pred[16,2]{1,0:T(8,128)(4,1)S(1)} fusion(s32[16]{0:T(128)} %bitcast.24), kind=kLoop, calls=%fused_computation.4 | loop fusion | flops 32 | bytes 96 | tf_op jit(solution)/shard_map/lt | solution.py:335
  2.2 0.1 lt.96
  2.3 0.1 concatenate.3
  2.4 0.1 copy.53.cell_ref
  2.6 0.0 copy-start.4
  2.6 0.0 copy-start.5
  2.6 0.0 copy-start.6
  2.6 0.0 copy-start.7
  2.6 2.2 %copy.62 = bf16[64,8,16,128]{3,1,2,0:T(8,128)(2,1)S(1)} copy(bf16[64,8,16,128]{3,2,1,0:T(8,128)(2,1)} %bitcast.21) | data formatting | bytes 4194304
  4.8 0.0 copy-start
  4.8 0.0 copy-done.4
  4.8 0.0 copy-done.5
  4.8 0.0 copy-done.6
  4.9 0.0 copy-done.7
  4.9 0.0 copy-start.12
  4.9 0.0 copy-start.11
  4.9 2.1 %local_stencil.1 = (f32[256,2048]{1,0:T(8,128)S(1)}, f32[2,8,128]{2,1,0:T(8,128)S(1)}, bf16[160,128]{1,0:T(8,128)(2,1)S(1)}, bf16[64,128]{1,0:T(8,128)(2,1)S(1)}...) custom-call(bf16[512,2048]{1,0:T(8,128)(2,1)S(1)} %bitcast.18, f32[2,3,2,8,128]{4,3,2,1,0:T(8,128)S(1)} %copy-done.4, ...), custom_call_target="tpu_custom_call" | custom-call | flops 100000000 | bytes 6000000 | tf_op jit(solution)/shard_map/local_stencil/pallas_call | solution.py:373
  6.9 0.0 copy-start.1
  6.9 0.0 copy-start.8
  7.0 0.5 %collective-permute-start.1 = (bf16[144,1024]{1,0:T(8,128)(2,1)}, bf16[144,1024]{1,0:T(8,128)(2,1)S(1)}, u32[]{:S(2)}, u32[]{:S(2)}) collective-permute-start(bf16[144,1024]{1,0:T(8,128)(2,1)} %get-tuple-element.30), channel_id=1, source_target_pairs={{0,1},{1,0},{2,3},{3,2},{4,5},{5,4},{6,7},{7,6},{8,9},{9,8},{10,11... | collective-permute-start | bytes 884744 | tf_op jit(solution)/shard_map/ppermute | solution.py:391
  7.4 0.0 copy-done
  7.4 0.1 pack_outer.1
  7.5 0.8 %copy-done.1 = f32[256,2048]{1,0:T(8,128)} copy-done((f32[256,2048]{1,0:T(8,128)}, f32[256,2048]{1,0:T(8,128)S(1)}, u32[]{:S(2)}) %copy-start.1) | copy-done | bytes 2097176
  8.3 0.7 %collective-permute-start = (bf16[140,8,128]{2,1,0:T(8,128)(2,1)S(1)}, bf16[140,8,128]{2,1,0:T(8,128)(2,1)S(1)}, u32[]{:S(2)}, u32[]{:S(2)}) collective-permute-start(bf16[140,8,128]{2,1,0:T(8,128)(2,1)S(1)} %pack_outer.1), channel_id=1, source_target_pairs={{1,2},{2,1},{3,4},{4,3},{5,6},{6,5},{7,8},{8,7},{9,10},{10,9},{11,... | collective-permute-start | bytes 860168 | tf_op jit(solution)/shard_map/ppermute | solution.py:330
  8.9 0.0 copy-done.8
  9.0 0.0 copy-done.12
  9.0 0.0 copy-done.11
  9.0 0.1 broadcast_add_fusion
  9.1 0.1 add.201.row_ref
  9.2 0.0 collective-permute-done.tail_ref
  9.3 0.0 collective-permute-done.1.inner_ref
  9.3 0.0 copy-start.2
  9.3 1.6 %copy-done.2 = f32[256,2048]{1,0:T(8,128)S(1)} copy-done((f32[256,2048]{1,0:T(8,128)S(1)}, f32[256,2048]{1,0:T(8,128)}, u32[]{:S(2)}) %copy-start.2) | copy-done | bytes 2097176
  10.9 0.0 copy-start.9
  10.9 0.8 %near_layer.1 = (f32[512,256]{1,0:T(8,128)S(1)}, f32[32,256]{1,0:T(8,128)S(1)}, bf16[32,128]{1,0:T(8,128)(2,1)S(1)}) custom-call(bf16[512,2048]{1,0:T(8,128)(2,1)S(1)} %bitcast.19, bf16[144,1024]{1,0:T(8,128)(2,1)S(1)} %collective-permute-done.1.inner_ref, f32[256,2048]{1,0:T(8,128)S(1)} %copy-done.2, f32[2,8,128]{2,1,0:T(8,128)S(1)} %get-tuple-element.26.edge_ref, ...), custom_call_target="tpu_custom_call" | custom-call | flops 300000000 | bytes 4000000 | tf_op jit(solution)/shard_map/near_layer/pallas_call | solution.py:392
  11.7 0.0 copy-done.9
  11.7 0.0 copy-start.3
  11.7 0.0 copy-start.10
  11.7 0.9 %project.1 = (f32[512,128]{1,0:T(8,128)S(1)}, bf16[144,128]{1,0:T(8,128)(2,1)S(1)}, bf16[1168,128]{1,0:T(8,128)(2,1)S(1)}) custom-call(bf16[512,2048]{1,0:T(8,128)(2,1)S(1)} %bitcast.20, bf16[128,1024]{1,0:T(8,128)(2,1)S(1)} %bitcast.22, bf16[140,8,128]{2,1,0:T(8,128)(2,1)S(1)} %collective-permute-done.tail_ref, f32[256,2048]{1,0:T(8,128)S(1)} %copy-done.2, ...), custom_call_target="tpu_custom_call" | custom-call | tf_op jit(solution)/shard_map/project/pallas_call | solution.py:410
  12.7 10.8 %collective-permute-start.2 = (bf16[1168,128]{1,0:T(8,128)(2,1)S(1)}, bf16[1168,128]{1,0:T(8,128)(2,1)S(1)}, u32[]{:S(2)}, u32[]{:S(2)}) collective-permute-start(bf16[1168,128]{1,0:T(8,128)(2,1)S(1)} %get-tuple-element.36), channel_id=1, source_target_pairs={{0,1},{1,0},{2,3},{3,2},{4,5},{5,4},{6,7},{7,6},{8,9},{9,8},{10,11... | collective-permute-start | bytes 897032 | tf_op jit(solution)/shard_map/ppermute | solution.py:448
  23.4 1.2 %collective-permute-done.2.got_ref = bf16[1168,128]{1,0:T(8,128)(2,1)S(1)} collective-permute-done((bf16[1168,128]{1,0:T(8,128)(2,1)S(1)}, bf16[1168,128]{1,0:T(8,128)(2,1)S(1)}, u32[]{:S(2)}, u32[]{:S(2)}) %collective-permute-start.2) | collective-permute-done | bytes 299040 | tf_op jit(solution)/shard_map/ppermute | solution.py:448
  24.7 0.0 copy-done.3
  24.7 0.3 merge.3
  24.9 2.8 %collective-permute-start.3 = (bf16[400,128]{1,0:T(8,128)(2,1)S(1)}, bf16[400,128]{1,0:T(8,128)(2,1)S(1)}, u32[]{:S(2)}, u32[]{:S(2)}) collective-permute-start(bf16[400,128]{1,0:T(8,128)(2,1)S(1)} %get-tuple-element.39), channel_id=1, source_target_pairs={{0,2},{1,3},{2,0},{3,1},{4,6},{5,7},{6,4},{7,5},{8,10},{9,11},{10,... | collective-permute-start | bytes 307208 | tf_op jit(solution)/shard_map/ppermute | solution.py:448
  27.7 0.0 copy-done.10
  27.7 0.7 %gather_fusion = s32[16]{0:T(128)S(1)} fusion(s32[16]{0:T(128)S(1)} %copy-done.10, s32[1024]{0:T(1024)S(1)} %pad_clamp_fusion), kind=kCustom, calls=%fused_computation | custom fusion | bytes 192 | tf_op jit(solution)/shard_map/gather | solution.py:369
  28.4 2.5 %collective-permute-done.3.got_ref = bf16[400,128]{1,0:T(8,128)(2,1)S(1)} collective-permute-done((bf16[400,128]{1,0:T(8,128)(2,1)S(1)}, bf16[400,128]{1,0:T(8,128)(2,1)S(1)}, u32[]{:S(2)}, u32[]{:S(2)}) %collective-permute-start.3) | collective-permute-done | bytes 102432 | tf_op jit(solution)/shard_map/ppermute | solution.py:448
  30.9 0.3 merge.4
  31.2 1.6 %collective-permute-start.4 = (bf16[272,128]{1,0:T(8,128)(2,1)S(1)}, bf16[272,128]{1,0:T(8,128)(2,1)S(1)}, u32[]{:S(2)}, u32[]{:S(2)}) collective-permute-start(bf16[272,128]{1,0:T(8,128)(2,1)S(1)} %get-tuple-element.42), channel_id=1, source_target_pairs={{0,4},{1,5},{2,6},{3,7},{4,0},{5,1},{6,2},{7,3},{8,12},{9,13},{10,... | collective-permute-start | bytes 208904 | tf_op jit(solution)/shard_map/ppermute | solution.py:448
  32.8 2.7 %collective-permute-done.4.got_ref = bf16[272,128]{1,0:T(8,128)(2,1)S(1)} collective-permute-done((bf16[272,128]{1,0:T(8,128)(2,1)S(1)}, bf16[272,128]{1,0:T(8,128)(2,1)S(1)}, u32[]{:S(2)}, u32[]{:S(2)}) %collective-permute-start.4) | collective-permute-done | bytes 69664 | tf_op jit(solution)/shard_map/ppermute | solution.py:448
  35.6 0.3 merge.5
  35.8 2.7 %collective-permute-start.5 = (bf16[208,128]{1,0:T(8,128)(2,1)S(1)}, bf16[208,128]{1,0:T(8,128)(2,1)S(1)}, u32[]{:S(2)}, u32[]{:S(2)}) collective-permute-start(bf16[208,128]{1,0:T(8,128)(2,1)S(1)} %get-tuple-element.45), channel_id=1, source_target_pairs={{0,8},{1,9},{2,10},{3,11},{4,12},{5,13},{6,14},{7,15},{8,0},{9,1},... | collective-permute-start | bytes 159752 | tf_op jit(solution)/shard_map/ppermute | solution.py:448
  38.5 0.1 iota_add_fusion
  38.6 0.1 add.202.final_ref
  38.7 2.3 %collective-permute-done.5.got_ref = bf16[208,128]{1,0:T(8,128)(2,1)S(1)} collective-permute-done((bf16[208,128]{1,0:T(8,128)(2,1)S(1)}, bf16[208,128]{1,0:T(8,128)(2,1)S(1)}, u32[]{:S(2)}, u32[]{:S(2)}) %collective-permute-start.5) | collective-permute-done | bytes 53280 | tf_op jit(solution)/shard_map/ppermute | solution.py:448
  40.9 0.9 %finish.1 = (f32[64,128]{1,0:T(8,128)}, bf16[288,128]{1,0:T(8,128)(2,1)}) custom-call(f32[64,128]{1,0:T(8,128)S(1)} %get-tuple-element.43.keep_ref, bf16[144,128]{1,0:T(8,128)(2,1)S(1)} %get-tuple-element.44.keep_rows_ref, bf16[208,128]{1,0:T(8,128)(2,1)S(1)} %collective-permute-done.5.got_ref, s32[288,1]{1,0:T(8,128)S(1)} %add.202.final_ref), custom_call_target="tpu_custom_call" | custom-call | tf_op jit(solution)/shard_map/finish/pallas_call | solution.py:467
  (8 shorter events, 0.1 us)
Async XLA Ops:
  2.6 2.2 %copy-start.4 = (f32[2,3,2,8,128]{4,3,2,1,0:T(8,128)S(1)}, f32[2,3,2,8,128]{4,3,2,1,0:T(8,128)}, u32[]{:S(2)}) copy-start(f32[2,3,2,8,128]{4,3,2,1,0:T(8,128)} %speed_ref.3) | copy-start | bytes 147460
  2.6 2.2 %copy-start.5 = (f32[2,3,2,8,128]{4,3,2,1,0:T(8,128)S(1)}, f32[2,3,2,8,128]{4,3,2,1,0:T(8,128)}, u32[]{:S(2)}) copy-start(f32[2,3,2,8,128]{4,3,2,1,0:T(8,128)} %diff_ref.3) | copy-start | bytes 147460
  2.6 2.2 %copy-start.6 = (s32[2,3,2,8,128]{4,3,2,1,0:T(8,128)S(1)}, s32[2,3,2,8,128]{4,3,2,1,0:T(8,128)}, u32[]{:S(2)}) copy-start(s32[2,3,2,8,128]{4,3,2,1,0:T(8,128)} %flag_ref.3) | copy-start | bytes 147460
  2.6 2.2 %copy-start.7 = (f32[2,2,8,128]{3,2,1,0:T(8,128)S(1)}, f32[2,2,8,128]{3,2,1,0:T(8,128)}, u32[]{:S(2)}) copy-start(f32[2,2,8,128]{3,2,1,0:T(8,128)} %react_ref.1) | copy-start | bytes 49156
  4.8 2.6 %copy-start = (bf16[512,2,8,128]{3,2,1,0:T(8,128)(2,1)S(1)}, bf16[512,2,8,128]{3,2,1,0:T(8,128)(2,1)}, u32[]{:S(2)}) copy-start(bf16[512,2,8,128]{3,2,1,0:T(8,128)(2,1)} %basis_ref.1) | copy-start | bytes 6291460
  4.9 4.1 %copy-start.12 = (s32[16]{0:T(128)S(1)}, s32[16]{0:T(128)}, u32[]{:S(2)}) copy-start(s32[16]{0:T(128)} %constant.73.clone) | copy-start | bytes 196
  4.9 4.1 %copy-start.11 = (s32[18]{0:T(128)S(1)}, s32[18]{0:T(128)}, u32[]{:S(2)}) copy-start(s32[18]{0:T(128)} %constant.74.clone) | copy-start | bytes 220
  6.9 1.3 %copy-start.1 = (f32[256,2048]{1,0:T(8,128)}, f32[256,2048]{1,0:T(8,128)S(1)}, u32[]{:S(2)}) copy-start(f32[256,2048]{1,0:T(8,128)S(1)} %get-tuple-element.25.acc_ref) | copy-start | bytes 6291460
  6.9 2.0 %copy-start.8 = (bf16[64,128]{1,0:T(8,128)(2,1)}, bf16[64,128]{1,0:T(8,128)(2,1)S(1)}, u32[]{:S(2)}) copy-start(bf16[64,128]{1,0:T(8,128)(2,1)S(1)} %get-tuple-element.28.side_ref) | copy-start | bytes 49156
  7.0 2.3 %collective-permute-start.1 = (bf16[144,1024]{1,0:T(8,128)(2,1)}, bf16[144,1024]{1,0:T(8,128)(2,1)S(1)}, u32[]{:S(2)}, u32[]{:S(2)}) collective-permute-start(bf16[144,1024]{1,0:T(8,128)(2,1)} %get-tuple-element.30), channel_id=1, source_target_pairs={{0,1},{1,0},{2,3},{3,2},{4,5},{5,4},{6,7},{7,6},{8,9},{9,8},{10,11... | collective-permute-start | bytes 884744 | tf_op jit(solution)/shard_map/ppermute | solution.py:391
  8.3 0.9 %collective-permute-start = (bf16[140,8,128]{2,1,0:T(8,128)(2,1)S(1)}, bf16[140,8,128]{2,1,0:T(8,128)(2,1)S(1)}, u32[]{:S(2)}, u32[]{:S(2)}) collective-permute-start(bf16[140,8,128]{2,1,0:T(8,128)(2,1)S(1)} %pack_outer.1), channel_id=1, source_target_pairs={{1,2},{2,1},{3,4},{4,3},{5,6},{6,5},{7,8},{8,7},{9,10},{10,9},{11,... | collective-permute-start | bytes 860168 | tf_op jit(solution)/shard_map/ppermute | solution.py:330
  9.3 1.6 %copy-start.2 = (f32[256,2048]{1,0:T(8,128)S(1)}, f32[256,2048]{1,0:T(8,128)}, u32[]{:S(2)}) copy-start(f32[256,2048]{1,0:T(8,128)} %copy-done.1) | copy-start | bytes 6291460
  10.9 0.8 %copy-start.9 = (bf16[64,128]{1,0:T(8,128)(2,1)S(1)}, bf16[64,128]{1,0:T(8,128)(2,1)}, u32[]{:S(2)}) copy-start(bf16[64,128]{1,0:T(8,128)(2,1)} %copy-done.8) | copy-start | bytes 49156
  11.7 12.9 %copy-start.3 = (s32[288,1]{1,0:T(8,128)S(1)}, s32[288,1]{1,0:T(8,128)}, u32[]{:S(2)}) copy-start(s32[288,1]{1,0:T(8,128)} %constant.76.clone.shuffle_ref) | copy-start | bytes 3460
  11.7 16.0 %copy-start.10 = (s32[16]{0:T(128)S(1)}, s32[16]{0:T(128)}, u32[]{:S(2)}) copy-start(s32[16]{0:T(128)} %constant.75.clone) | copy-start | bytes 196
  12.7 12.0 %collective-permute-start.2 = (bf16[1168,128]{1,0:T(8,128)(2,1)S(1)}, bf16[1168,128]{1,0:T(8,128)(2,1)S(1)}, u32[]{:S(2)}, u32[]{:S(2)}) collective-permute-start(bf16[1168,128]{1,0:T(8,128)(2,1)S(1)} %get-tuple-element.36), channel_id=1, source_target_pairs={{0,1},{1,0},{2,3},{3,2},{4,5},{5,4},{6,7},{7,6},{8,9},{9,8},{10,11... | collective-permute-start | bytes 897032 | tf_op jit(solution)/shard_map/ppermute | solution.py:448
  24.9 6.0 %collective-permute-start.3 = (bf16[400,128]{1,0:T(8,128)(2,1)S(1)}, bf16[400,128]{1,0:T(8,128)(2,1)S(1)}, u32[]{:S(2)}, u32[]{:S(2)}) collective-permute-start(bf16[400,128]{1,0:T(8,128)(2,1)S(1)} %get-tuple-element.39), channel_id=1, source_target_pairs={{0,2},{1,3},{2,0},{3,1},{4,6},{5,7},{6,4},{7,5},{8,10},{9,11},{10,... | collective-permute-start | bytes 307208 | tf_op jit(solution)/shard_map/ppermute | solution.py:448
  31.2 4.4 %collective-permute-start.4 = (bf16[272,128]{1,0:T(8,128)(2,1)S(1)}, bf16[272,128]{1,0:T(8,128)(2,1)S(1)}, u32[]{:S(2)}, u32[]{:S(2)}) collective-permute-start(bf16[272,128]{1,0:T(8,128)(2,1)S(1)} %get-tuple-element.42), channel_id=1, source_target_pairs={{0,4},{1,5},{2,6},{3,7},{4,0},{5,1},{6,2},{7,3},{8,12},{9,13},{10,... | collective-permute-start | bytes 208904 | tf_op jit(solution)/shard_map/ppermute | solution.py:448
  35.8 5.1 %collective-permute-start.5 = (bf16[208,128]{1,0:T(8,128)(2,1)S(1)}, bf16[208,128]{1,0:T(8,128)(2,1)S(1)}, u32[]{:S(2)}, u32[]{:S(2)}) collective-permute-start(bf16[208,128]{1,0:T(8,128)(2,1)S(1)} %get-tuple-element.45), channel_id=1, source_target_pairs={{0,8},{1,9},{2,10},{3,11},{4,12},{5,13},{6,14},{7,15},{8,0},{9,1},... | collective-permute-start | bytes 159752 | tf_op jit(solution)/shard_map/ppermute | solution.py:448

commit v4 on v3

v4 whole, which is shorter than its diff:
```python
import functools

import jax
import jax.numpy as jnp
import numpy as np
from jax import lax
from jax.experimental import pallas as pl
from jax.experimental.pallas import tpu as pltpu
from jax.sharding import PartitionSpec as P

MB = 128
SPLITS = 3
NARROW_STEPS = 3
BF16 = jnp.bfloat16
F32 = jnp.float32
I32 = jnp.int32
OFFSETS = 7
VMEM = pl.BlockSpec(memory_space=pltpu.VMEM)
ALONE = pltpu.CompilerParams(vmem_limit_bytes=60 * 1024 * 1024)
SMALL = pl.CostEstimate(flops=1, bytes_accessed=1, transcendentals=0)
LIMIT = pltpu.CompilerParams(vmem_limit_bytes=20 * 1024 * 1024)


def nt_dot(left, right):
    return lax.dot_general(left, right, (((1,), (1,)), ((), ())), preferred_element_type=F32)


def picked(targets, start, count):
    lanes = lax.broadcasted_iota(I32, (1, count), 1) + start
    return jnp.where(targets == lanes, 1.0, 0.0).astype(BF16)


def column(row):
    size = row.shape[1]
    down = lax.broadcasted_iota(I32, (size, size), 0)
    across = lax.broadcasted_iota(I32, (size, size), 1)
    spread = jnp.where(down == across, row.astype(F32), 0.0)
    return jnp.sum(spread, axis=1, keepdims=True).astype(I32)


def halves(value):
    head = value.astype(BF16)
    return head, (value - head.astype(F32)).astype(BF16)


def core():
    return lax.rem(lax.axis_index("cells"), 2)


def face_parts(speed, diff, flag):
    parts = []
    for value in (jnp.where(flag == 1, speed, -speed), diff):
        for _ in range(SPLITS):
            head = value.astype(BF16)
            value = value - head.astype(F32)
            parts.append(head)
    return parts


def pack_kernel(dims, basis_ref, speed_ref, diff_ref, flag_ref, inner_ref, outer_ref, speed_buf, diff_buf, flag_buf, sems):
    params, layers = dims
    last = layers - 1
    block = pl.ds(0, MB)
    outer = pltpu.make_async_copy(basis_ref.at[block, core() * last], outer_ref.at[block], sems.at[0])
    inner = pltpu.make_async_copy(basis_ref.at[block, (1 - core()) * last], inner_ref.at[block], sems.at[1])
    copies = [
        pltpu.make_async_copy(speed_ref.at[:, 0, last], speed_buf, sems.at[2]),
        pltpu.make_async_copy(diff_ref.at[:, 0, last], diff_buf, sems.at[3]),
        pltpu.make_async_copy(flag_ref.at[:, 0, last], flag_buf, sems.at[4]),
    ]
    for copy in copies + [outer, inner]:
        copy.start()
    for copy in copies:
        copy.wait()
    for at, part in enumerate(face_parts(speed_buf[...], diff_buf[...], flag_buf[...])):
        inner_ref[MB + at * params : MB + (at + 1) * params] = part
        outer_ref[MB + at * params : MB + (at + 1) * params] = part
    outer.wait()
    inner.wait()


def load_kernel(basis_ref, cell_ref, count_ref, after_ref, basis_out, cell_out, count_out, sems):
    del after_ref
    pairs = ((basis_ref, basis_out), (cell_ref, cell_out), (count_ref, count_out))
    copies = [pltpu.make_async_copy(source, out, sems.at[at]) for at, (source, out) in enumerate(pairs)]
    for copy in copies:
        copy.start()
    for copy in copies:
        copy.wait()


def local_kernel(
    dims,
    flat_ref,
    speed_ref,
    diff_ref,
    flag_ref,
    react_ref,
    sampled_ref,
    count_ref,
    acc_ref,
    edge_ref,
    in_ref,
    center_ref,
    cell_ref,
    coef_ref,
    pick_ref,
):
    params, layers, width_y, width_z, plane, samples = dims
    y_at = lax.broadcasted_iota(I32, (width_y, width_z), 0)
    z_at = lax.broadcasted_iota(I32, (width_y, width_z), 1)
    for param in range(params):
        uppers, nexts = [], []
        for layer in range(layers):
            up_d, next_d = [], []
            for axis_d in range(3):
                forward = flag_ref[param, axis_d, layer] == 1
                speed = speed_ref[param, axis_d, layer]
                diff = diff_ref[param, axis_d, layer]
                up_d.append(jnp.where(forward, speed, 0.0) + diff)
                next_d.append(jnp.where(forward, 0.0, -speed) - diff)
            uppers.append(up_d)
            nexts.append(next_d)
        edge_ref[param] = nexts[layers - 1][0]
        for layer in range(layers):
            diag = react_ref[param, layer]
            diag = diag + uppers[layer][0] + uppers[layer][1] + uppers[layer][2]
            if layer > 0:
                diag = diag - nexts[layer - 1][0]
                coef_ref[param, layer, 2] = -uppers[layer - 1][0]
            coef_ref[param, layer, 1] = nexts[layer][0]
            for axis_d, at, shift_axis, size in ((1, y_at, 0, width_y), (2, z_at, 1, width_z)):
                up, following = uppers[layer][axis_d], nexts[layer][axis_d]
                low_up = jnp.where(at == 0, 0.0, pltpu.roll(up, 1, shift_axis))
                low_next = jnp.where(at == 0, 0.0, pltpu.roll(following, 1, shift_axis))
                diag = diag - low_next
                coef_ref[param, layer, 1 + 2 * axis_d] = jnp.where(at == size - 1, 0.0, following)
                coef_ref[param, layer, 2 + 2 * axis_d] = -low_up
            coef_ref[param, layer, 0] = diag

    def tile(layer, y):
        start = layer * plane + y * width_z
        return flat_ref[:MB, start : start + width_z].astype(F32)

    for layer in range(layers):
        for y in range(width_y):
            start = layer * plane + y * width_z
            state = tile(layer, y)
            terms = [(0, state), (5, pltpu.roll(state, width_z - 1, 1)), (6, pltpu.roll(state, 1, 1))]
            if layer < layers - 1:
                terms.append((1, tile(layer + 1, y)))
            if layer > 0:
                terms.append((2, tile(layer - 1, y)))
            if y < width_y - 1:
                terms.append((3, tile(layer, y + 1)))
            if y > 0:
                terms.append((4, tile(layer, y - 1)))
            for param in range(params):
                total = None
                for at, term in terms:
                    product = coef_ref[param, layer, at, y : y + 1, :] * term
                    total = product if total is None else total + product
                acc_ref[param * MB : (param + 1) * MB, start : start + width_z] = total

    count = column(count_ref[...])
    slots = sampled_ref.shape[0]
    held = []
    for slot in range(slots):
        held.append(jnp.where(slot < count, column(sampled_ref[slot : slot + 1]), -4 * layers * plane))
    cell = jnp.concatenate(held, axis=0)
    cell_ref[...] = cell
    z_of = lax.broadcasted_iota(I32, (1, width_z), 1)
    for layer in range(layers):
        for y in range(width_y):
            start = layer * plane + y * width_z
            away = z_of - (cell - start)
            hits = [away == 0, away == -plane, away == plane]
            hits.append(away == -width_z if y < width_y - 1 else None)
            hits.append(away == width_z if y > 0 else None)
            hits.append((away == -1) & (z_of < width_z - 1))
            hits.append((away == 1) & (z_of > 0))
            for at, hit in enumerate(hits):
                value = jnp.zeros((samples, width_z), BF16)
                if hit is not None:
                    value = jnp.where(hit, 1.0, 0.0).astype(BF16)
                pick_ref[at * samples : (at + 1) * samples, start : start + width_z] = value
    center_ref[...] = pick_ref[:samples]
    in_ref[...] = nt_dot(pick_ref[...], flat_ref[:MB, :]).astype(BF16)


def finish_layer(dims, from_next, layer, halo_ref, flat_ref, acc_ref, edge_ref, applied_ref, coef_ref, spread_ref, beside_ref):
    params, layers, width_y, width_z, plane = dims
    faces = []
    for at in range(2 * SPLITS):
        part = halo_ref[MB + at * params : MB + (at + 1) * params].astype(F32)
        faces.append(part.reshape(params * width_y, width_z))
    signed = faces[0] + faces[1] + faces[2]
    diff = faces[3] + faces[4] + faces[5]
    edge = edge_ref[...].reshape(params * width_y, width_z)
    coef_ref[0] = jnp.where(from_next, edge, -(jnp.maximum(signed, 0.0) + diff))
    coef_ref[1] = jnp.where(from_next, 0.0, diff - jnp.minimum(signed, 0.0))
    spread_ref[...] = halo_ref[:MB].astype(F32).reshape(MB * width_y, width_z)
    for y in range(width_y):
        at = pl.multiple_of(layer * plane + y * width_z, width_z)
        lanes = slice(y * width_z, (y + 1) * width_z)
        state = flat_ref[:MB, pl.ds(at, width_z)].astype(F32)
        beside = spread_ref[pl.ds(y, MB, stride=width_y), :]
        beside_ref[:, lanes] = beside.astype(BF16)
        for param in range(params):
            modes = slice(param * MB, (param + 1) * MB)
            row = param * width_y + y
            total = acc_ref[modes, pl.ds(at, width_z)]
            total = total + coef_ref[1, row : row + 1, :] * state
            total = total + coef_ref[0, row : row + 1, :] * beside
            applied_ref[modes, lanes] = total.astype(BF16)


def near_kernel(dims, flat_ref, inner_ref, acc_ref, edge_ref, center_ref, cell_ref, sums_ref, picks_ref, side_ref, *scratch):
    params, layers, width_y, width_z, plane, samples = dims
    odd = core() == 1
    layer = (1 - core()) * (layers - 1)
    start = pl.multiple_of(layer * plane, plane)
    finish_layer(dims[:5], jnp.logical_not(odd), layer, inner_ref, flat_ref, acc_ref, edge_ref, *scratch)
    applied_ref, beside_ref = scratch[0], scratch[3]
    sums_ref[...] = nt_dot(flat_ref[:, pl.ds(start, plane)], applied_ref[...])
    picks_ref[...] = nt_dot(center_ref[:, pl.ds(start, plane)], applied_ref[...])
    below = cell_ref[...]
    above = below - (layers - 1) * plane
    side_ref[...] = nt_dot(picked(jnp.where(odd, below, above), 0, plane), beside_ref[...]).astype(BF16)


def project_kernel(
    dims,
    relative,
    flat_ref,
    outer_ref,
    acc_ref,
    edge_ref,
    in_ref,
    center_ref,
    near_sums_ref,
    near_picks_ref,
    near_side_ref,
    cell_ref,
    table_ref,
    keep_ref,
    keep_rows_ref,
    packet_ref,
    sums_ref,
    *scratch,
):
    params, layers, width_y, width_z, plane, samples, devices, own = dims
    odd = core() == 1
    layer = core() * (layers - 1)
    lane = pl.multiple_of(layer * plane, plane)
    finish_layer(dims[:5], odd, layer, outer_ref, flat_ref, acc_ref, edge_ref, *scratch)
    applied_ref, beside_ref = scratch[0], scratch[3]

    sums = near_sums_ref[...] + nt_dot(flat_ref[:, pl.ds(lane, plane)], applied_ref[...])
    for param in range(params):
        sums_ref[pl.ds(param, sums.shape[0], stride=params), :] = sums[:, param * MB : (param + 1) * MB]
    size = own * params
    half = devices // 2
    me = lax.axis_index("cells")
    for place in range(devices):
        start = pl.multiple_of((me ^ relative[place]) * size, size)
        terms = sums_ref[pl.ds(start, size), :]
        if place < half:
            keep_ref[place * size : (place + 1) * size] = terms
        else:
            head, rest = halves(terms)
            at = (place - half) * size
            packet_ref[at : at + size] = head
            packet_ref[half * size + at : half * size + at + size] = rest

    picks = nt_dot(center_ref[:, pl.ds(lane, plane)], applied_ref[...])
    got_applied = (near_picks_ref[...] + picks).astype(BF16)
    below = cell_ref[...]
    above = below - (layers - 1) * plane
    far = nt_dot(picked(jnp.where(odd, above, below), 0, plane), beside_ref[...]).astype(BF16)
    near = near_side_ref[...]
    got_below = in_ref[samples : 2 * samples] + jnp.where(odd, near, far)
    got_above = in_ref[2 * samples : 3 * samples] + jnp.where(odd, far, near)
    pieces = [got_applied[:, param * MB : (param + 1) * MB] for param in range(params)]
    pieces += [in_ref[:samples], got_below, got_above, in_ref[3 * samples :]]
    gathered = jnp.concatenate(pieces, axis=0)
    order = picked((table_ref[:, 1:2] ^ me) + table_ref[:, 2:3], 0, gathered.shape[0])
    ordered = jnp.dot(order, gathered, preferred_element_type=F32).astype(BF16)
    count = ordered.shape[0] // 2
    keep_rows_ref[...] = ordered[:count]
    packet_ref[2 * half * size :] = ordered[count:]


def merge_kernel(wide_in, wide_out, keep_ref, keep_rows_ref, got_ref, table_ref, keep_out, rows_out, packet_out):
    size = keep_ref.shape[0]
    half = size // 2
    total = keep_ref[...] + got_ref[:size].astype(F32)
    if wide_in:
        total = total + got_ref[size : 2 * size].astype(F32)
    keep_out[...] = total[:half]
    if wide_out:
        head, rest = halves(total[half:])
        packet_out[:half] = head
        packet_out[half : 2 * half] = rest
    else:
        packet_out[:half] = total[half:].astype(BF16)
    count = keep_rows_ref.shape[0]
    rows = jnp.concatenate([keep_rows_ref[...], got_ref[got_ref.shape[0] - count :]], axis=0)
    order = picked(table_ref[:, 0:1], 0, 2 * count)
    ordered = jnp.dot(order, rows, preferred_element_type=F32).astype(BF16)
    rows_out[...] = ordered[:count]
    packet_out[packet_out.shape[0] - count :] = ordered[count:]


def final_kernel(wide_in, volume, steps, block, keep_ref, keep_rows_ref, got_ref, table_ref, sum_out, rows_out):
    size = keep_ref.shape[0]
    total = keep_ref[...] + got_ref[:size].astype(F32)
    if wide_in:
        total = total + got_ref[size : 2 * size].astype(F32)
    sum_out[...] = volume * total
    count = keep_rows_ref.shape[0]
    rows = jnp.concatenate([keep_rows_ref[...], got_ref[got_ref.shape[0] - count :]], axis=0)
    me = lax.axis_index("cells")
    mine = (me >> (steps - 1)) << (steps - 1)
    for step in range(steps - 1):
        mine = mine + (((me >> step) & 1) << (steps - 2 - step))
    order = picked((table_ref[:, 3:4] ^ mine) * block + table_ref[:, 4:5], 0, 2 * count)
    rows_out[...] = jnp.dot(order, rows, preferred_element_type=F32).astype(BF16)


def shape(dims, dtype):
    return jax.ShapeDtypeStruct(dims, dtype)


def shards(basis, face_speed, face_diffusion, upwind_flag, reaction, sample_cell, sample_count):
    modes, layers, width_y, width_z = basis.shape
    params = face_speed.shape[0]
    devices = lax.axis_size("cells")
    slots = sample_cell.shape[2]
    plane = width_y * width_z
    cells = layers * plane
    own = modes // devices
    rows = params + OFFSETS
    samples = devices * slots
    steps = devices.bit_length() - 1

    tail = params * width_y
    hbm = pl.BlockSpec(memory_space=pltpu.HBM)
    planes = 2 * SPLITS * params
    packed = shape((MB + planes, width_y, width_z), BF16)
    to_inner, to_outer = pl.pallas_call(
        functools.partial(pack_kernel, (params, layers)),
        out_shape=(packed, packed),
        in_specs=[hbm] * 4,
        out_specs=(VMEM, VMEM),
        scratch_shapes=[
            pltpu.VMEM((params, width_y, width_z), F32),
            pltpu.VMEM((params, width_y, width_z), F32),
            pltpu.VMEM((params, width_y, width_z), I32),
            pltpu.SemaphoreType.DMA((5,)),
        ],
        compiler_params=ALONE,
        name="pack_halo",
    )(basis, face_speed, face_diffusion, upwind_flag)
    inner_pairs = [(i, i ^ 1) for i in range(devices)]
    outer_pairs = []
    for i in range(1, devices - 1, 2):
        outer_pairs += [(i, i + 1), (i + 1, i)]
    inner = lax.ppermute(to_inner, "cells", inner_pairs)
    outer = lax.ppermute(to_outer, "cells", outer_pairs)

    loaded, cells_in, counts_in = pl.pallas_call(
        load_kernel,
        out_shape=(shape(basis.shape, BF16), shape((slots, devices), I32), shape((1, devices), I32)),
        in_specs=[hbm] * 3 + [VMEM],
        out_specs=(VMEM,) * 3,
        scratch_shapes=[pltpu.SemaphoreType.DMA((3,))],
        compiler_params=LIMIT,
        name="load",
    )(basis, sample_cell[0].T, sample_count, to_outer)
    flat = loaded.reshape(modes, cells)

    block = slots * rows
    relative = [sum(((place >> (steps - 1 - step)) & 1) << step for step in range(steps)) for place in range(devices)]
    block = slots * rows
    table = np.zeros((devices, block, 8), np.int32)
    in_block = np.arange(block)
    for place in range(devices):
        turned = ((place & 1) << (steps - 1)) + (place >> 1)
        table[place, :, 0] = turned * block + in_block
        table[place, :, 1] = relative[place]
        table[place, :, 2] = (in_block // slots) * samples + (in_block % slots) * devices
        table[relative[place], :, 3] = turned
        table[place, :, 4] = in_block
    table = jnp.asarray(table.reshape(devices * block, 8))

    acc, edge, got_in, center, cell = pl.pallas_call(
        functools.partial(local_kernel, (params, layers, width_y, width_z, plane, samples)),
        out_shape=(
            shape((params * MB, cells), F32),
            shape((params, width_y, width_z), F32),
            shape((OFFSETS * samples, MB), BF16),
            shape((samples, cells), BF16),
            shape((samples, 1), I32),
        ),
        in_specs=[VMEM] * 7,
        out_specs=(VMEM,) * 5,
        scratch_shapes=[
            pltpu.VMEM((params, layers, OFFSETS, width_y, width_z), F32),
            pltpu.VMEM((OFFSETS * samples, cells), BF16),
        ],
        compiler_params=LIMIT,
        cost_estimate=SMALL,
        name="local_stencil",
    )(flat, face_speed, face_diffusion, upwind_flag, reaction, cells_in, counts_in)

    finish_scratch = [
        pltpu.VMEM((params * MB, plane), BF16),
        pltpu.VMEM((2, tail, width_z), F32),
        pltpu.VMEM((MB * width_y, width_z), F32),
        pltpu.VMEM((MB, plane), BF16),
    ]
    near_sums, near_picks, near_side = pl.pallas_call(
        functools.partial(near_kernel, (params, layers, width_y, width_z, plane, samples)),
        out_shape=(
            shape((modes, params * MB), F32),
            shape((samples, params * MB), F32),
            shape((samples, MB), BF16),
        ),
        in_specs=[VMEM] * 6,
        out_specs=(VMEM,) * 3,
        scratch_shapes=finish_scratch,
        compiler_params=LIMIT,
        cost_estimate=SMALL,
        name="near_layer",
    )(flat, inner, acc, edge, center, cell)

    size = own * params
    half = devices // 2
    count = half * block
    keep, keep_rows, packet = pl.pallas_call(
        functools.partial(
            project_kernel,
            (params, layers, width_y, width_z, plane, samples, devices, own),
            relative,
        ),
        out_shape=(
            shape((half * size, MB), F32),
            shape((count, MB), BF16),
            shape((2 * half * size + count, MB), BF16),
        ),
        in_specs=[VMEM] * 11,
        out_specs=(VMEM,) * 3,
        scratch_shapes=[pltpu.VMEM((params * modes, MB), F32)] + finish_scratch,
        compiler_params=LIMIT,
        name="project",
    )(
        flat,
        outer,
        acc,
        edge,
        got_in,
        center,
        near_sums,
        near_picks,
        near_side,
        cell,
        table,
    )

    wide = True
    for step in range(steps):
        got = lax.ppermute(packet, "cells", [(i, i ^ (1 << step)) for i in range(devices)])
        if step < steps - 1:
            next_wide = not 0 < step + 1 <= NARROW_STEPS
            half //= 2
            packet_rows = (2 if next_wide else 1) * half * size + count
            keep, keep_rows, packet = pl.pallas_call(
                functools.partial(merge_kernel, wide, next_wide),
                out_shape=(
                    shape((half * size, MB), F32),
                    shape((count, MB), BF16),
                    shape((packet_rows, MB), BF16),
                ),
                in_specs=[VMEM] * 4,
                out_specs=(VMEM,) * 3,
                compiler_params=LIMIT,
                name="merge",
            )(keep, keep_rows, got, table)
            wide = next_wide
    volume = 1.0 / (layers * devices * width_y * width_z)
    summed, sampled = pl.pallas_call(
        functools.partial(final_kernel, wide, volume, steps, block),
        out_shape=(shape((size, MB), F32), shape((2 * count, MB), BF16)),
        in_specs=[VMEM] * 4,
        out_specs=(VMEM,) * 2,
        compiler_params=LIMIT,
        name="finish",
    )(keep, keep_rows, got, table)
    galerkin = summed.reshape(own, params, MB)
    sampled = sampled.reshape(devices, rows, slots, MB)
    return (galerkin, jnp.transpose(sampled, (0, 2, 1, 3))[None])


def solution(mesh):
    return jax.shard_map(
        shards,
        mesh=mesh,
        in_specs=(
            P(None, ("groups", "cells"), None, None),
            P(None, None, ("groups", "cells"), None, None),
            P(None, None, ("groups", "cells"), None, None),
            P(None, None, ("groups", "cells"), None, None),
            P(None, ("groups", "cells"), None, None),
            P(("groups", "cells"), None, None),
            P(("groups", "cells"), None),
        ),
        out_specs=(
            P(("groups", "cells"), None, None),
            P(("groups", "cells"), None, None, None, None),
        ),
        check_vma=False,
    )
```

time: 42 us -> 34.7 us (0.83)
  local copies, waits for them, and re-layouts: 6.67 us -> 1.79 us
  starting transfers between devices: 19 us -> 15.5 us
  Pallas kernels: 5.62 us -> 7.53 us
  other arithmetic: 0.92 us -> 0 us
    unnamed x29 -> x19, local copies, waits for them, and re-layouts: 5.38 us -> 1.79 us
    ppermute x4, starting transfers between devices: 17.9 us -> 14.3 us  [shards(): lax.ppermute(packet, 'cells', [(i, i ^ 1 << step) for i in range(devices)])]
    pallas_call x1, Pallas kernels: 0.11 us -> 2.1 us  [shards(): pl.pallas_call(functools.partial(pack_kernel, (params, layers)), out_shap...]
    lt x1 -> x0, other arithmetic: 0.73 us -> none  [shards(): live = (slot_at < sample_count[0][:, None]).reshape(samples, 1)]
    gather x1 -> x0, local copies, waits for them, and re-layouts: 0.66 us -> none  [shards(): source = jnp.asarray(came)[jnp.arange(devices) ^ me]]
    pallas_call x1, Pallas kernels: 2.06 us -> 1.55 us  [shards(): pl.pallas_call(functools.partial(local_kernel, (params, layers, width_y,...]
    pallas_call x1 -> x2, Pallas kernels: 0.9 us -> 1.14 us  [the longest x1 0.97 us: shards(): pl.pallas_call(functools.partial(final_kernel, wide, volume, steps, block...]
  transfers between devices with their start and end apart: 6 -> 6, of which waited for: 4 -> 4; matrix products, arithmetic and copies ran while one was open for 3% -> 2% of each run, Pallas kernels for 0% -> 8%
where the time goes in v4:
time: 34.7 us; the launch traced here: 34.5 us
  starting transfers between devices  15.5 us (45%)
  waiting for transfers between devices  8.81 us (25%)
  Pallas kernels  7.53 us (22%)
  local copies, waits for them, and re-layouts  1.79 us (5%)
  between operations  0.82 us (2%)
    ppermute x4, starting transfers between devices, shards(): lax.ppermute(packet, 'cells', [(i, i ^ 1 << step) for i in range(devices)])  14.3 us
    ppermute x4, waiting for transfers between devices, shards(): lax.ppermute(packet, 'cells', [(i, i ^ 1 << step) for i in range(devices)])  8.8 us
    pallas_call x1, Pallas kernels, shards(): pl.pallas_call(functools.partial(pack_kernel, (params, layers)), out_shap...  2.1 us
    unnamed x19, local copies, waits for them, and re-layouts  1.79 us
    pallas_call x1, Pallas kernels, shards(): pl.pallas_call(functools.partial(local_kernel, (params, layers, width_y,...  1.55 us
    pallas_call x1, Pallas kernels, shards(): pl.pallas_call(functools.partial(project_kernel, (params, layers, width_y...  1.02 us
    pallas_call x1, Pallas kernels, shards(): pl.pallas_call(functools.partial(final_kernel, wide, volume, steps, block...  0.97 us
    pallas_call x1, Pallas kernels, shards(): pl.pallas_call(functools.partial(near_kernel, (params, layers, width_y, w...  0.93 us
  transfers between devices with their start and end apart: 6, of which 4 were waited for; matrix products, arithmetic and copies ran while one was open for 2% of the time, Pallas kernels for 8%

profile of v4, /device:TPU:0, one launch (start us, length us, event | category | flops | bytes accessed | tf_op | source)
XLA Modules:
  0.0 34.5 jit_solution(12138874834215001743)
XLA Ops:
  0.6 0.0 copy-start
  0.6 0.0 copy-start.8
  0.6 0.0 copy-start.7
  0.7 2.1 %pack_halo.1 = (bf16[140,8,128]{2,1,0:T(8,128)(2,1)}, bf16[140,8,128]{2,1,0:T(8,128)(2,1)}) custom-call(bf16[512,2,8,128]{3,2,1,0:T(8,128)(2,1)} %basis_ref.3, f32[2,3,2,8,128]{4,3,2,1,0:T(8,128)} %speed_ref.3, f32[2,3,2,8,128]{4,3,2,1,0:T(8,128)} %diff_ref.3, s32[2,3,2,8,128]{4,3,2,1,0:T(8,128)} %flag_ref.3), custom_call_target="tpu_custom_call" | custom-call | tf_op jit(solution)/shard_map/pack_halo/pallas_call | solution.py:351
  2.8 0.5 %collective-permute-start.1 = (bf16[140,8,128]{2,1,0:T(8,128)(2,1)}, bf16[140,8,128]{2,1,0:T(8,128)(2,1)S(1)}, u32[]{:S(2)}, u32[]{:S(2)}) collective-permute-start(bf16[140,8,128]{2,1,0:T(8,128)(2,1)} %get-tuple-element.37), channel_id=1, source_target_pairs={{0,1},{1,0},{2,3},{3,2},{4,5},{5,4},{6,7},{7,6},{8,9},{9,8},{10,11... | collective-permute-start | bytes 860168 | tf_op jit(solution)/shard_map/ppermute | solution.py:369
  3.3 0.7 %collective-permute-start = (bf16[140,8,128]{2,1,0:T(8,128)(2,1)}, bf16[140,8,128]{2,1,0:T(8,128)(2,1)S(1)}, u32[]{:S(2)}, u32[]{:S(2)}) collective-permute-start(bf16[140,8,128]{2,1,0:T(8,128)(2,1)} %get-tuple-element.29.after_ref), channel_id=1, source_target_pairs={{1,2},{2,1},{3,4},{4,3},{5,6},{6,5},{7,8},{8,7},{9,10},{10,9},{11,... | collective-permute-start | bytes 860168 | tf_op jit(solution)/shard_map/ppermute | solution.py:370
  4.0 0.0 copy-done
  4.0 0.0 copy-done.8
  4.0 0.0 copy-done.7
  4.0 0.0 copy-start.2
  4.0 0.9 %copy-done.2 = bf16[140,8,128]{2,1,0:T(8,128)(2,1)S(1)} copy-done((bf16[140,8,128]{2,1,0:T(8,128)(2,1)S(1)}, bf16[140,8,128]{2,1,0:T(8,128)(2,1)}, u32[]{:S(2)}) %copy-start.2) | copy-done | bytes 286744
  5.0 0.2 load.1
  5.1 0.0 copy-start.3
  5.1 0.0 copy-start.4
  5.2 0.0 copy-start.5
  5.2 0.0 copy-start.6
  5.2 0.5 %copy.12 = bf16[64,8,16,128]{3,1,2,0:T(8,128)(2,1)S(1)} copy(bf16[64,8,16,128]{3,2,1,0:T(8,128)(2,1)S(1)} %bitcast.17) | data formatting | bytes 4194304
  5.7 0.2 copy-done.3
  5.9 0.0 copy-done.4
  6.0 0.0 copy-done.5
  6.0 0.0 copy-done.6
  6.0 1.6 %local_stencil.1 = (f32[256,2048]{1,0:T(8,128)S(1)}, f32[2,8,128]{2,1,0:T(8,128)S(1)}, bf16[224,128]{1,0:T(8,128)(2,1)S(1)}, bf16[32,2048]{1,0:T(8,128)(2,1)S(1)}, s32[32,1]{1,0:T(8,128)S(1)}) custom-call(bf16[512,2048]{1,0:T(8,128)(2,1)S(1)} %bitcast.14, f32[2,3,2,8,128]{4,3,2,1,0:T(8,128)S(1)} %copy-done.3, f32[2,3,2,8,128]{4,3,2,1,0:T(8,128)S(1)} %copy-done.4, ...), custom_call_target="tpu_custom_call" | custom-call | flops 1 | bytes 1 | tf_op jit(solution)/shard_map/local_stencil/pallas_call | solution.py:397
  7.5 0.0 collective-permute-done.1.inner_ref
  7.6 0.0 copy-start.1
  7.6 0.9 %near_layer.1 = (f32[512,256]{1,0:T(8,128)S(1)}, f32[32,256]{1,0:T(8,128)S(1)}, bf16[32,128]{1,0:T(8,128)(2,1)S(1)}) custom-call(bf16[512,2048]{1,0:T(8,128)(2,1)S(1)} %bitcast.15, bf16[140,8,128]{2,1,0:T(8,128)(2,1)S(1)} %collective-permute-done.1.inner_ref, f32[256,2048]{1,0:T(8,128)S(1)} %get-tuple-element.33.acc_ref, ...), custom_call_target="tpu_custom_call" | custom-call | flops 1 | bytes 1 | tf_op jit(solution)/shard_map/near_layer/pallas_call | solution.py:423
  8.5 0.0 collective-permute-done.outer_ref
  8.5 0.0 copy-done.1
  8.5 1.0 %project.1 = (f32[512,128]{1,0:T(8,128)S(1)}, bf16[144,128]{1,0:T(8,128)(2,1)S(1)}, bf16[1168,128]{1,0:T(8,128)(2,1)S(1)}) custom-call(bf16[512,2048]{1,0:T(8,128)(2,1)S(1)} %bitcast.16, bf16[140,8,128]{2,1,0:T(8,128)(2,1)S(1)} %collective-permute-done.outer_ref, f32[256,2048]{1,0:T(8,128)S(1)} %get-tuple-element.33.acc_ref, ...), custom_call_target="tpu_custom_call" | custom-call | tf_op jit(solution)/shard_map/project/pallas_call | solution.py:441
  9.6 6.3 %collective-permute-start.2 = (bf16[1168,128]{1,0:T(8,128)(2,1)S(1)}, bf16[1168,128]{1,0:T(8,128)(2,1)S(1)}, u32[]{:S(2)}, u32[]{:S(2)}) collective-permute-start(bf16[1168,128]{1,0:T(8,128)(2,1)S(1)} %get-tuple-element.44), channel_id=1, source_target_pairs={{0,1},{1,0},{2,3},{3,2},{4,5},{5,4},{6,7},{7,6},{8,9},{9,8},{10,11... | collective-permute-start | bytes 897032 | tf_op jit(solution)/shard_map/ppermute | solution.py:473
  15.9 1.2 %collective-permute-done.2.got_ref = bf16[1168,128]{1,0:T(8,128)(2,1)S(1)} collective-permute-done((bf16[1168,128]{1,0:T(8,128)(2,1)S(1)}, bf16[1168,128]{1,0:T(8,128)(2,1)S(1)}, u32[]{:S(2)}, u32[]{:S(2)}) %collective-permute-start.2) | collective-permute-done | bytes 299040 | tf_op jit(solution)/shard_map/ppermute | solution.py:473
  17.1 0.3 merge.3
  17.4 2.7 %collective-permute-start.3 = (bf16[400,128]{1,0:T(8,128)(2,1)S(1)}, bf16[400,128]{1,0:T(8,128)(2,1)S(1)}, u32[]{:S(2)}, u32[]{:S(2)}) collective-permute-start(bf16[400,128]{1,0:T(8,128)(2,1)S(1)} %get-tuple-element.47), channel_id=1, source_target_pairs={{0,2},{1,3},{2,0},{3,1},{4,6},{5,7},{6,4},{7,5},{8,10},{9,11},{10,... | collective-permute-start | bytes 307208 | tf_op jit(solution)/shard_map/ppermute | solution.py:473
  20.1 3.2 %collective-permute-done.3.got_ref = bf16[400,128]{1,0:T(8,128)(2,1)S(1)} collective-permute-done((bf16[400,128]{1,0:T(8,128)(2,1)S(1)}, bf16[400,128]{1,0:T(8,128)(2,1)S(1)}, u32[]{:S(2)}, u32[]{:S(2)}) %collective-permute-start.3) | collective-permute-done | bytes 102432 | tf_op jit(solution)/shard_map/ppermute | solution.py:473
  23.3 0.3 merge.4
  23.5 2.2 %collective-permute-start.4 = (bf16[272,128]{1,0:T(8,128)(2,1)S(1)}, bf16[272,128]{1,0:T(8,128)(2,1)S(1)}, u32[]{:S(2)}, u32[]{:S(2)}) collective-permute-start(bf16[272,128]{1,0:T(8,128)(2,1)S(1)} %get-tuple-element.50), channel_id=1, source_target_pairs={{0,4},{1,5},{2,6},{3,7},{4,0},{5,1},{6,2},{7,3},{8,12},{9,13},{10,... | collective-permute-start | bytes 208904 | tf_op jit(solution)/shard_map/ppermute | solution.py:473
  25.7 2.3 %collective-permute-done.4.got_ref = bf16[272,128]{1,0:T(8,128)(2,1)S(1)} collective-permute-done((bf16[272,128]{1,0:T(8,128)(2,1)S(1)}, bf16[272,128]{1,0:T(8,128)(2,1)S(1)}, u32[]{:S(2)}, u32[]{:S(2)}) %collective-permute-start.4) | collective-permute-done | bytes 69664 | tf_op jit(solution)/shard_map/ppermute | solution.py:473
  28.0 0.3 merge.5
  28.3 3.1 %collective-permute-start.5 = (bf16[208,128]{1,0:T(8,128)(2,1)S(1)}, bf16[208,128]{1,0:T(8,128)(2,1)S(1)}, u32[]{:S(2)}, u32[]{:S(2)}) collective-permute-start(bf16[208,128]{1,0:T(8,128)(2,1)S(1)} %get-tuple-element.53), channel_id=1, source_target_pairs={{0,8},{1,9},{2,10},{3,11},{4,12},{5,13},{6,14},{7,15},{8,0},{9,1},... | collective-permute-start | bytes 159752 | tf_op jit(solution)/shard_map/ppermute | solution.py:473
  31.4 2.1 %collective-permute-done.5.got_ref = bf16[208,128]{1,0:T(8,128)(2,1)S(1)} collective-permute-done((bf16[208,128]{1,0:T(8,128)(2,1)S(1)}, bf16[208,128]{1,0:T(8,128)(2,1)S(1)}, u32[]{:S(2)}, u32[]{:S(2)}) %collective-permute-start.5) | collective-permute-done | bytes 53280 | tf_op jit(solution)/shard_map/ppermute | solution.py:473
  33.5 1.0 %finish.1 = (f32[64,128]{1,0:T(8,128)}, bf16[288,128]{1,0:T(8,128)(2,1)}) custom-call(f32[64,128]{1,0:T(8,128)S(1)} %get-tuple-element.51.keep_ref, bf16[144,128]{1,0:T(8,128)(2,1)S(1)} %get-tuple-element.52.keep_rows_ref, bf16[208,128]{1,0:T(8,128)(2,1)S(1)} %collective-permute-done.5.got_ref, s32[288,8]{1,0:T(8,128)S(1)} %copy-done.1), custom_call_target="tpu_custom_call" | custom-call | tf_op jit(solution)/shard_map/finish/pallas_call | solution.py:492
Async XLA Ops:
  0.6 3.3 %copy-start = (bf16[512,2,8,128]{3,2,1,0:T(8,128)(2,1)S(1)}, bf16[512,2,8,128]{3,2,1,0:T(8,128)(2,1)}, u32[]{:S(2)}) copy-start(bf16[512,2,8,128]{3,2,1,0:T(8,128)(2,1)} %basis_ref.3) | copy-start | bytes 6291460
  0.6 3.3 %copy-start.8 = (s32[1,16]{1,0:T(1,128)S(1)}, s32[1,16]{1,0:T(1,128)}, u32[]{:S(2)}) copy-start(s32[1,16]{1,0:T(1,128)} %count_ref.1) | copy-start | bytes 196
  0.6 3.3 %copy-start.7 = (s32[1,16,2]{1,2,0:T(2,128)S(1)}, s32[1,16,2]{1,2,0:T(2,128)}, u32[]{:S(2)}) copy-start(s32[1,16,2]{1,2,0:T(2,128)} %param.13) | copy-start | bytes 388
  2.8 4.8 %collective-permute-start.1 = (bf16[140,8,128]{2,1,0:T(8,128)(2,1)}, bf16[140,8,128]{2,1,0:T(8,128)(2,1)S(1)}, u32[]{:S(2)}, u32[]{:S(2)}) collective-permute-start(bf16[140,8,128]{2,1,0:T(8,128)(2,1)} %get-tuple-element.37), channel_id=1, source_target_pairs={{0,1},{1,0},{2,3},{3,2},{4,5},{5,4},{6,7},{7,6},{8,9},{9,8},{10,11... | collective-permute-start | bytes 860168 | tf_op jit(solution)/shard_map/ppermute | solution.py:369
  3.3 5.2 %collective-permute-start = (bf16[140,8,128]{2,1,0:T(8,128)(2,1)}, bf16[140,8,128]{2,1,0:T(8,128)(2,1)S(1)}, u32[]{:S(2)}, u32[]{:S(2)}) collective-permute-start(bf16[140,8,128]{2,1,0:T(8,128)(2,1)} %get-tuple-element.29.after_ref), channel_id=1, source_target_pairs={{1,2},{2,1},{3,4},{4,3},{5,6},{6,5},{7,8},{8,7},{9,10},{10,9},{11,... | collective-permute-start | bytes 860168 | tf_op jit(solution)/shard_map/ppermute | solution.py:370
  4.0 1.0 %copy-start.2 = (bf16[140,8,128]{2,1,0:T(8,128)(2,1)S(1)}, bf16[140,8,128]{2,1,0:T(8,128)(2,1)}, u32[]{:S(2)}) copy-start(bf16[140,8,128]{2,1,0:T(8,128)(2,1)} %get-tuple-element.29.after_ref) | copy-start | bytes 860164
  5.1 0.8 %copy-start.3 = (f32[2,3,2,8,128]{4,3,2,1,0:T(8,128)S(1)}, f32[2,3,2,8,128]{4,3,2,1,0:T(8,128)}, u32[]{:S(2)}) copy-start(f32[2,3,2,8,128]{4,3,2,1,0:T(8,128)} %speed_ref.3) | copy-start | bytes 147460
  5.1 0.8 %copy-start.4 = (f32[2,3,2,8,128]{4,3,2,1,0:T(8,128)S(1)}, f32[2,3,2,8,128]{4,3,2,1,0:T(8,128)}, u32[]{:S(2)}) copy-start(f32[2,3,2,8,128]{4,3,2,1,0:T(8,128)} %diff_ref.3) | copy-start | bytes 147460
  5.2 0.8 %copy-start.5 = (s32[2,3,2,8,128]{4,3,2,1,0:T(8,128)S(1)}, s32[2,3,2,8,128]{4,3,2,1,0:T(8,128)}, u32[]{:S(2)}) copy-start(s32[2,3,2,8,128]{4,3,2,1,0:T(8,128)} %flag_ref.3) | copy-start | bytes 147460
  5.2 0.8 %copy-start.6 = (f32[2,2,8,128]{3,2,1,0:T(8,128)S(1)}, f32[2,2,8,128]{3,2,1,0:T(8,128)}, u32[]{:S(2)}) copy-start(f32[2,2,8,128]{3,2,1,0:T(8,128)} %react_ref.1) | copy-start | bytes 49156
  7.6 1.0 %copy-start.1 = (s32[288,8]{1,0:T(8,128)S(1)}, s32[288,8]{1,0:T(8,128)}, u32[]{:S(2)}) copy-start(s32[288,8]{1,0:T(8,128)} %constant.2.clone.table_ref) | copy-start | bytes 27652
  9.6 7.5 %collective-permute-start.2 = (bf16[1168,128]{1,0:T(8,128)(2,1)S(1)}, bf16[1168,128]{1,0:T(8,128)(2,1)S(1)}, u32[]{:S(2)}, u32[]{:S(2)}) collective-permute-start(bf16[1168,128]{1,0:T(8,128)(2,1)S(1)} %get-tuple-element.44), channel_id=1, source_target_pairs={{0,1},{1,0},{2,3},{3,2},{4,5},{5,4},{6,7},{7,6},{8,9},{9,8},{10,11... | collective-permute-start | bytes 897032 | tf_op jit(solution)/shard_map/ppermute | solution.py:473
  17.4 5.9 %collective-permute-start.3 = (bf16[400,128]{1,0:T(8,128)(2,1)S(1)}, bf16[400,128]{1,0:T(8,128)(2,1)S(1)}, u32[]{:S(2)}, u32[]{:S(2)}) collective-permute-start(bf16[400,128]{1,0:T(8,128)(2,1)S(1)} %get-tuple-element.47), channel_id=1, source_target_pairs={{0,2},{1,3},{2,0},{3,1},{4,6},{5,7},{6,4},{7,5},{8,10},{9,11},{10,... | collective-permute-start | bytes 307208 | tf_op jit(solution)/shard_map/ppermute | solution.py:473
  23.5 4.5 %collective-permute-start.4 = (bf16[272,128]{1,0:T(8,128)(2,1)S(1)}, bf16[272,128]{1,0:T(8,128)(2,1)S(1)}, u32[]{:S(2)}, u32[]{:S(2)}) collective-permute-start(bf16[272,128]{1,0:T(8,128)(2,1)S(1)} %get-tuple-element.50), channel_id=1, source_target_pairs={{0,4},{1,5},{2,6},{3,7},{4,0},{5,1},{6,2},{7,3},{8,12},{9,13},{10,... | collective-permute-start | bytes 208904 | tf_op jit(solution)/shard_map/ppermute | solution.py:473
  28.3 5.2 %collective-permute-start.5 = (bf16[208,128]{1,0:T(8,128)(2,1)S(1)}, bf16[208,128]{1,0:T(8,128)(2,1)S(1)}, u32[]{:S(2)}, u32[]{:S(2)}) collective-permute-start(bf16[208,128]{1,0:T(8,128)(2,1)S(1)} %get-tuple-element.53), channel_id=1, source_target_pairs={{0,8},{1,9},{2,10},{3,11},{4,12},{5,13},{6,14},{7,15},{8,0},{9,1},... | collective-permute-start | bytes 159752 | tf_op jit(solution)/shard_map/ppermute | solution.py:473

commit v5 on v4

--- a/solution.py
+++ b/solution.py
@@ -10,7 +10,9 @@
 
 MB = 128
 SPLITS = 3
-NARROW_STEPS = 3
+NARROW_STEPS = 1
+DIRECT = 4
+ORDER = (3, 2, 1)
 BF16 = jnp.bfloat16
 F32 = jnp.float32
 I32 = jnp.int32
@@ -36,6 +38,10 @@
     across = lax.broadcasted_iota(I32, (size, size), 1)
     spread = jnp.where(down == across, row.astype(F32), 0.0)
     return jnp.sum(spread, axis=1, keepdims=True).astype(I32)
+
+
+def round_up(value, multiple):
+    return -(-value // multiple) * multiple
 
 
 def halves(value):
@@ -284,7 +290,8 @@
     pieces = [got_applied[:, param * MB : (param + 1) * MB] for param in range(params)]
     pieces += [in_ref[:samples], got_below, got_above, in_ref[3 * samples :]]
     gathered = jnp.concatenate(pieces, axis=0)
-    order = picked((table_ref[:, 1:2] ^ me) + table_ref[:, 2:3], 0, gathered.shape[0])
+    total_rows = gathered.shape[0]
+    order = picked((table_ref[:total_rows, 1:2] ^ me) + table_ref[:total_rows, 2:3], 0, gathered.shape[0])
     ordered = jnp.dot(order, gathered, preferred_element_type=F32).astype(BF16)
     count = ordered.shape[0] // 2
     keep_rows_ref[...] = ordered[:count]
@@ -306,26 +313,52 @@
         packet_out[:half] = total[half:].astype(BF16)
     count = keep_rows_ref.shape[0]
     rows = jnp.concatenate([keep_rows_ref[...], got_ref[got_ref.shape[0] - count :]], axis=0)
-    order = picked(table_ref[:, 0:1], 0, 2 * count)
+    order = picked(table_ref[: 2 * count, 0:1], 0, 2 * count)
     ordered = jnp.dot(order, rows, preferred_element_type=F32).astype(BF16)
     rows_out[...] = ordered[:count]
     packet_out[packet_out.shape[0] - count :] = ordered[count:]
 
 
-def final_kernel(wide_in, volume, steps, block, keep_ref, keep_rows_ref, got_ref, table_ref, sum_out, rows_out):
+def spread_kernel(wide_in, room, keep_ref, keep_rows_ref, got_ref, table_ref, keep_out, rows_out, *packets_out):
     size = keep_ref.shape[0]
     total = keep_ref[...] + got_ref[:size].astype(F32)
     if wide_in:
         total = total + got_ref[size : 2 * size].astype(F32)
-    sum_out[...] = volume * total
+    part = size // DIRECT
     count = keep_rows_ref.shape[0]
     rows = jnp.concatenate([keep_rows_ref[...], got_ref[got_ref.shape[0] - count :]], axis=0)
+    order = picked(table_ref[: DIRECT * room, 5:6], 0, 2 * count)
+    ordered = jnp.dot(order, rows, preferred_element_type=F32).astype(BF16)
+    keep_out[...] = total[:part]
+    rows_out[...] = ordered[:room]
+    for at, packet_out in enumerate(packets_out, 1):
+        packet_out[:part] = total[at * part : (at + 1) * part].astype(BF16)
+        packet_out[part:] = ordered[at * room : (at + 1) * room]
+
+
+def final_kernel(volume, steps, block, keep_ref, keep_rows_ref, *refs):
+    got_refs, table_ref, sum_out, rows_out = refs[: DIRECT - 1], refs[-3], refs[-2], refs[-1]
+    size = keep_ref.shape[0]
+    room = keep_rows_ref.shape[0]
+    total = keep_ref[...]
+    rows = [keep_rows_ref[...]] + [None] * (DIRECT - 1)
+    for at, got_ref in zip(ORDER, got_refs):
+        total = total + got_ref[:size].astype(F32)
+        rows[at] = got_ref[size:]
+    sum_out[...] = volume * total
     me = lax.axis_index("cells")
-    mine = (me >> (steps - 1)) << (steps - 1)
-    for step in range(steps - 1):
-        mine = mine + (((me >> step) & 1) << (steps - 2 - step))
-    order = picked((table_ref[:, 3:4] ^ mine) * block + table_ref[:, 4:5], 0, 2 * count)
-    rows_out[...] = jnp.dot(order, rows, preferred_element_type=F32).astype(BF16)
+    mine = 0
+    for step, place in enumerate(places(steps)):
+        mine = mine + (((me >> step) & 1) << place)
+    came = table_ref[: rows_out.shape[0], 3:4] ^ mine
+    low = steps - 2
+    start = (came >> low) * room + (came & ((1 << low) - 1)) * block
+    order = picked(start + table_ref[: rows_out.shape[0], 4:5], 0, DIRECT * room)
+    rows_out[...] = jnp.dot(order, jnp.concatenate(rows, axis=0), preferred_element_type=F32).astype(BF16)
+
+
+def places(steps):
+    return [steps - 3 - step for step in range(steps - 2)] + [steps - 1, steps - 2]
 
 
 def shape(dims, dtype):
@@ -383,16 +416,21 @@
     block = slots * rows
     relative = [sum(((place >> (steps - 1 - step)) & 1) << step for step in range(steps)) for place in range(devices)]
     block = slots * rows
-    table = np.zeros((devices, block, 8), np.int32)
+    share = devices // DIRECT * block
+    room = round_up(share, 16)
+    table = np.full((DIRECT * room, 8), -1, np.int32)
     in_block = np.arange(block)
     for place in range(devices):
-        turned = ((place & 1) << (steps - 1)) + (place >> 1)
-        table[place, :, 0] = turned * block + in_block
-        table[place, :, 1] = relative[place]
-        table[place, :, 2] = (in_block // slots) * samples + (in_block % slots) * devices
-        table[relative[place], :, 3] = turned
-        table[place, :, 4] = in_block
-    table = jnp.asarray(table.reshape(devices * block, 8))
+        turned = (((place & 1) << (steps - 1)) + (place >> 1)) * block + in_block
+        at = slice(place * block, (place + 1) * block)
+        table[at, 0] = turned
+        table[at, 1] = relative[place]
+        table[at, 2] = (in_block // slots) * samples + (in_block % slots) * devices
+        table[at, 3] = sum(((place >> step) & 1) << to for step, to in enumerate(places(steps)))
+        table[at, 4] = in_block
+        start = place * block // share * room + place * block % share
+        table[start : start + block, 5] = turned
+    table = jnp.asarray(table)
 
     acc, edge, got_in, center, cell = pl.pallas_call(
         functools.partial(local_kernel, (params, layers, width_y, width_z, plane, samples)),
@@ -469,10 +507,10 @@
     )
 
     wide = True
-    for step in range(steps):
+    for step in range(steps - 2):
         got = lax.ppermute(packet, "cells", [(i, i ^ (1 << step)) for i in range(devices)])
-        if step < steps - 1:
-            next_wide = not 0 < step + 1 <= NARROW_STEPS
+        if step < steps - 3:
+            next_wide = step + 1 > NARROW_STEPS
             half //= 2
             packet_rows = (2 if next_wide else 1) * half * size + count
             keep, keep_rows, packet = pl.pallas_call(
@@ -488,15 +526,28 @@
                 name="merge",
             )(keep, keep_rows, got, table)
             wide = next_wide
+    sent = shape((size + room, MB), BF16)
+    keep, keep_rows, *packets = pl.pallas_call(
+        functools.partial(spread_kernel, wide, room),
+        out_shape=(shape((size, MB), F32), shape((room, MB), BF16)) + (sent,) * (DIRECT - 1),
+        in_specs=[VMEM] * 4,
+        out_specs=(VMEM,) * (DIRECT + 1),
+        compiler_params=LIMIT,
+        name="spread",
+    )(keep, keep_rows, got, table)
+    got = [None] * DIRECT
+    for at in ORDER:
+        mask = ((at >> 1) << (steps - 2)) | ((at & 1) << (steps - 1))
+        got[at] = lax.ppermute(packets[at - 1], "cells", [(i, i ^ mask) for i in range(devices)])
     volume = 1.0 / (layers * devices * width_y * width_z)
     summed, sampled = pl.pallas_call(
-        functools.partial(final_kernel, wide, volume, steps, block),
+        functools.partial(final_kernel, volume, steps, block),
         out_shape=(shape((size, MB), F32), shape((2 * count, MB), BF16)),
-        in_specs=[VMEM] * 4,
+        in_specs=[VMEM] * (DIRECT + 2),
         out_specs=(VMEM,) * 2,
         compiler_params=LIMIT,
         name="finish",
-    )(keep, keep_rows, got, table)
+    )(keep, keep_rows, *[got[at] for at in ORDER], table)
     galerkin = summed.reshape(own, params, MB)
     sampled = sampled.reshape(devices, rows, slots, MB)
     return (galerkin, jnp.transpose(sampled, (0, 2, 1, 3))[None])

time: 34.7 us -> 33.8 us (0.974)
  starting transfers between devices: 15.5 us -> 15.1 us
    ppermute x4 -> x2, starting transfers between devices: 14.3 us -> 9.03 us  [shards(): lax.ppermute(packet, 'cells', [(i, i ^ 1 << step) for i in range(devices)])]
    ppermute x0 -> x3, starting transfers between devices: none -> 4.88 us  [shards(): lax.ppermute(packets[at - 1], 'cells', [(i, i ^ mask) for i in range(devi...]
    ppermute x4 -> x2, waiting for transfers between devices: 8.8 us -> 4.4 us  [shards(): lax.ppermute(packet, 'cells', [(i, i ^ 1 << step) for i in range(devices)])]
    ppermute x0 -> x3, waiting for transfers between devices: none -> 4.22 us  [shards(): lax.ppermute(packets[at - 1], 'cells', [(i, i ^ mask) for i in range(devi...]
    pallas_call x3 -> x1, Pallas kernels: 0.79 us -> 0.26 us  [shards(): pl.pallas_call(functools.partial(merge_kernel, wide, next_wide), out_shap...]
    pallas_call x1 -> x2, Pallas kernels: 0.97 us -> 1.24 us  [the longest x1 0.97 us: shards(): pl.pallas_call(functools.partial(final_kernel, volume, steps, block), out...]
  transfers between devices with their start and end apart: 6 -> 7, of which waited for: 4 -> 5; matrix products, arithmetic and copies ran while one was open for 2% -> 2% of each run, Pallas kernels for 8% -> 8%
where the time goes in v5:
time: 33.8 us; the launch traced here: 33.6 us
  starting transfers between devices  15.1 us (45%)
  waiting for transfers between devices  8.62 us (26%)
  Pallas kernels  7.27 us (22%)
  local copies, waits for them, and re-layouts  1.79 us (5%)
  between operations  0.82 us (2%)
    ppermute x2, starting transfers between devices, shards(): lax.ppermute(packet, 'cells', [(i, i ^ 1 << step) for i in range(devices)])  9.03 us
    ppermute x3, starting transfers between devices, shards(): lax.ppermute(packets[at - 1], 'cells', [(i, i ^ mask) for i in range(devi...  4.88 us
    ppermute x2, waiting for transfers between devices, shards(): lax.ppermute(packet, 'cells', [(i, i ^ 1 << step) for i in range(devices)])  4.4 us
    ppermute x3, waiting for transfers between devices, shards(): lax.ppermute(packets[at - 1], 'cells', [(i, i ^ mask) for i in range(devi...  4.22 us
    pallas_call x1, Pallas kernels, shards(): pl.pallas_call(functools.partial(pack_kernel, (params, layers)), out_shap...  2.1 us
    unnamed x19, local copies, waits for them, and re-layouts  1.79 us
    pallas_call x1, Pallas kernels, shards(): pl.pallas_call(functools.partial(local_kernel, (params, layers, width_y,...  1.55 us
    pallas_call x1, Pallas kernels, shards(): pl.pallas_call(functools.partial(project_kernel, (params, layers, width_y...  1.02 us
  transfers between devices with their start and end apart: 7, of which 5 were waited for; matrix products, arithmetic and copies ran while one was open for 2% of the time, Pallas kernels for 8%

profile of v5, /device:TPU:0, one launch (start us, length us, event | category | flops | bytes accessed | tf_op | source)
XLA Modules:
  0.0 33.6 jit_solution(4332520243569693974)
XLA Ops:
  0.6 0.0 copy-start
  0.6 0.0 copy-start.8
  0.6 0.0 copy-start.7
  0.7 2.1 %pack_halo.1 = (bf16[140,8,128]{2,1,0:T(8,128)(2,1)}, bf16[140,8,128]{2,1,0:T(8,128)(2,1)}) custom-call(bf16[512,2,8,128]{3,2,1,0:T(8,128)(2,1)} %basis_ref.3, f32[2,3,2,8,128]{4,3,2,1,0:T(8,128)} %speed_ref.3, f32[2,3,2,8,128]{4,3,2,1,0:T(8,128)} %diff_ref.3, s32[2,3,2,8,128]{4,3,2,1,0:T(8,128)} %flag_ref.3), custom_call_target="tpu_custom_call" | custom-call | tf_op jit(solution)/shard_map/pack_halo/pallas_call | solution.py:384
  2.8 0.5 %collective-permute-start.1 = (bf16[140,8,128]{2,1,0:T(8,128)(2,1)}, bf16[140,8,128]{2,1,0:T(8,128)(2,1)S(1)}, u32[]{:S(2)}, u32[]{:S(2)}) collective-permute-start(bf16[140,8,128]{2,1,0:T(8,128)(2,1)} %get-tuple-element.36), channel_id=1, source_target_pairs={{0,1},{1,0},{2,3},{3,2},{4,5},{5,4},{6,7},{7,6},{8,9},{9,8},{10,11... | collective-permute-start | bytes 860168 | tf_op jit(solution)/shard_map/ppermute | solution.py:402
  3.3 0.7 %collective-permute-start = (bf16[140,8,128]{2,1,0:T(8,128)(2,1)}, bf16[140,8,128]{2,1,0:T(8,128)(2,1)S(1)}, u32[]{:S(2)}, u32[]{:S(2)}) collective-permute-start(bf16[140,8,128]{2,1,0:T(8,128)(2,1)} %get-tuple-element.28.after_ref), channel_id=1, source_target_pairs={{1,2},{2,1},{3,4},{4,3},{5,6},{6,5},{7,8},{8,7},{9,10},{10,9},{11,... | collective-permute-start | bytes 860168 | tf_op jit(solution)/shard_map/ppermute | solution.py:403
  4.0 0.0 copy-done
  4.0 0.0 copy-done.8
  4.0 0.0 copy-done.7
  4.0 0.0 copy-start.2
  4.0 0.9 %copy-done.2 = bf16[140,8,128]{2,1,0:T(8,128)(2,1)S(1)} copy-done((bf16[140,8,128]{2,1,0:T(8,128)(2,1)S(1)}, bf16[140,8,128]{2,1,0:T(8,128)(2,1)}, u32[]{:S(2)}) %copy-start.2) | copy-done | bytes 286744
  5.0 0.2 load.1
  5.1 0.0 copy-start.3
  5.1 0.0 copy-start.4
  5.2 0.0 copy-start.5
  5.2 0.0 copy-start.6
  5.2 0.5 %copy.12 = bf16[64,8,16,128]{3,1,2,0:T(8,128)(2,1)S(1)} copy(bf16[64,8,16,128]{3,2,1,0:T(8,128)(2,1)S(1)} %bitcast.17) | data formatting | bytes 4194304
  5.7 0.2 copy-done.3
  5.9 0.0 copy-done.4
  6.0 0.0 copy-done.5
  6.0 0.0 copy-done.6
  6.0 1.6 %local_stencil.1 = (f32[256,2048]{1,0:T(8,128)S(1)}, f32[2,8,128]{2,1,0:T(8,128)S(1)}, bf16[224,128]{1,0:T(8,128)(2,1)S(1)}, bf16[32,2048]{1,0:T(8,128)(2,1)S(1)}, s32[32,1]{1,0:T(8,128)S(1)}) custom-call(bf16[512,2048]{1,0:T(8,128)(2,1)S(1)} %bitcast.14, f32[2,3,2,8,128]{4,3,2,1,0:T(8,128)S(1)} %copy-done.3, f32[2,3,2,8,128]{4,3,2,1,0:T(8,128)S(1)} %copy-done.4, ...), custom_call_target="tpu_custom_call" | custom-call | flops 1 | bytes 1 | tf_op jit(solution)/shard_map/local_stencil/pallas_call | solution.py:435
  7.5 0.0 collective-permute-done.1.inner_ref
  7.6 0.0 copy-start.1
  7.6 0.9 %near_layer.1 = (f32[512,256]{1,0:T(8,128)S(1)}, f32[32,256]{1,0:T(8,128)S(1)}, bf16[32,128]{1,0:T(8,128)(2,1)S(1)}) custom-call(bf16[512,2048]{1,0:T(8,128)(2,1)S(1)} %bitcast.15, bf16[140,8,128]{2,1,0:T(8,128)(2,1)S(1)} %collective-permute-done.1.inner_ref, f32[256,2048]{1,0:T(8,128)S(1)} %get-tuple-element.32.acc_ref, ...), custom_call_target="tpu_custom_call" | custom-call | flops 1 | bytes 1 | tf_op jit(solution)/shard_map/near_layer/pallas_call | solution.py:461
  8.5 0.0 collective-permute-done.outer_ref
  8.5 0.0 copy-done.1
  8.5 1.0 %project.1 = (f32[512,128]{1,0:T(8,128)S(1)}, bf16[144,128]{1,0:T(8,128)(2,1)S(1)}, bf16[1168,128]{1,0:T(8,128)(2,1)S(1)}) custom-call(bf16[512,2048]{1,0:T(8,128)(2,1)S(1)} %bitcast.16, bf16[140,8,128]{2,1,0:T(8,128)(2,1)S(1)} %collective-permute-done.outer_ref, f32[256,2048]{1,0:T(8,128)S(1)} %get-tuple-element.32.acc_ref, ...), custom_call_target="tpu_custom_call" | custom-call | tf_op jit(solution)/shard_map/project/pallas_call | solution.py:479
  9.6 6.3 %collective-permute-start.2 = (bf16[1168,128]{1,0:T(8,128)(2,1)S(1)}, bf16[1168,128]{1,0:T(8,128)(2,1)S(1)}, u32[]{:S(2)}, u32[]{:S(2)}) collective-permute-start(bf16[1168,128]{1,0:T(8,128)(2,1)S(1)} %get-tuple-element.43), channel_id=1, source_target_pairs={{0,1},{1,0},{2,3},{3,2},{4,5},{5,4},{6,7},{7,6},{8,9},{9,8},{10,11... | collective-permute-start | bytes 897032 | tf_op jit(solution)/shard_map/ppermute | solution.py:511
  15.9 1.2 %collective-permute-done.2.got_ref = bf16[1168,128]{1,0:T(8,128)(2,1)S(1)} collective-permute-done((bf16[1168,128]{1,0:T(8,128)(2,1)S(1)}, bf16[1168,128]{1,0:T(8,128)(2,1)S(1)}, u32[]{:S(2)}, u32[]{:S(2)}) %collective-permute-start.2) | collective-permute-done | bytes 299040 | tf_op jit(solution)/shard_map/ppermute | solution.py:511
  17.1 0.3 merge.1
  17.4 2.7 %collective-permute-start.3 = (bf16[400,128]{1,0:T(8,128)(2,1)S(1)}, bf16[400,128]{1,0:T(8,128)(2,1)S(1)}, u32[]{:S(2)}, u32[]{:S(2)}) collective-permute-start(bf16[400,128]{1,0:T(8,128)(2,1)S(1)} %get-tuple-element.46), channel_id=1, source_target_pairs={{0,2},{1,3},{2,0},{3,1},{4,6},{5,7},{6,4},{7,5},{8,10},{9,11},{10,... | collective-permute-start | bytes 307208 | tf_op jit(solution)/shard_map/ppermute | solution.py:511
  20.1 3.2 %collective-permute-done.3.got_ref = bf16[400,128]{1,0:T(8,128)(2,1)S(1)} collective-permute-done((bf16[400,128]{1,0:T(8,128)(2,1)S(1)}, bf16[400,128]{1,0:T(8,128)(2,1)S(1)}, u32[]{:S(2)}, u32[]{:S(2)}) %collective-permute-start.3) | collective-permute-done | bytes 102432 | tf_op jit(solution)/shard_map/ppermute | solution.py:511
  23.3 0.3 spread.1
  23.5 4.2 %collective-permute-start.4 = (bf16[144,128]{1,0:T(8,128)(2,1)S(1)}, bf16[144,128]{1,0:T(8,128)(2,1)S(1)}, u32[]{:S(2)}, u32[]{:S(2)}) collective-permute-start(bf16[144,128]{1,0:T(8,128)(2,1)S(1)} %get-tuple-element.49), channel_id=1, source_target_pairs={{0,12},{1,13},{2,14},{3,15},{4,8},{5,9},{6,10},{7,11},{8,4},{9,5},... | collective-permute-start | bytes 110600 | tf_op jit(solution)/shard_map/ppermute | solution.py:541
  27.8 0.0 collective-permute-start.5
  27.8 0.6 %collective-permute-start.6 = (bf16[144,128]{1,0:T(8,128)(2,1)S(1)}, bf16[144,128]{1,0:T(8,128)(2,1)S(1)}, u32[]{:S(2)}, u32[]{:S(2)}) collective-permute-start(bf16[144,128]{1,0:T(8,128)(2,1)S(1)} %get-tuple-element.51), channel_id=1, source_target_pairs={{0,8},{1,9},{2,10},{3,11},{4,12},{5,13},{6,14},{7,15},{8,0},{9,1},... | collective-permute-start | bytes 110600 | tf_op jit(solution)/shard_map/ppermute | solution.py:541
  28.4 1.3 %collective-permute-done.4.refs_0_ = bf16[144,128]{1,0:T(8,128)(2,1)S(1)} collective-permute-done((bf16[144,128]{1,0:T(8,128)(2,1)S(1)}, bf16[144,128]{1,0:T(8,128)(2,1)S(1)}, u32[]{:S(2)}, u32[]{:S(2)}) %collective-permute-start.4) | collective-permute-done | bytes 36896 | tf_op jit(solution)/shard_map/ppermute | solution.py:541
  29.7 2.0 %collective-permute-done.5.refs_1_ = bf16[144,128]{1,0:T(8,128)(2,1)S(1)} collective-permute-done((bf16[144,128]{1,0:T(8,128)(2,1)S(1)}, bf16[144,128]{1,0:T(8,128)(2,1)S(1)}, u32[]{:S(2)}, u32[]{:S(2)}) %collective-permute-start.5) | collective-permute-done | bytes 36896 | tf_op jit(solution)/shard_map/ppermute | solution.py:541
  31.7 0.9 %collective-permute-done.6.refs_2_ = bf16[144,128]{1,0:T(8,128)(2,1)S(1)} collective-permute-done((bf16[144,128]{1,0:T(8,128)(2,1)S(1)}, bf16[144,128]{1,0:T(8,128)(2,1)S(1)}, u32[]{:S(2)}, u32[]{:S(2)}) %collective-permute-start.6) | collective-permute-done | bytes 36896 | tf_op jit(solution)/shard_map/ppermute | solution.py:541
  32.6 1.0 %finish.1 = (f32[64,128]{1,0:T(8,128)}, bf16[288,128]{1,0:T(8,128)(2,1)}) custom-call(f32[64,128]{1,0:T(8,128)S(1)} %get-tuple-element.47.keep_ref, bf16[80,128]{1,0:T(8,128)(2,1)S(1)} %get-tuple-element.48.keep_rows_ref, bf16[144,128]{1,0:T(8,128)(2,1)S(1)} %collective-permute-done.4.refs_0_, bf16[144,128]{1,0:T(8,128)(2,1)S(1)} %collective-permute-done.5.refs_1_, ...), custom_call_target="tpu_custom_call" | custom-call | tf_op jit(solution)/shard_map/finish/pallas_call | solution.py:543
Async XLA Ops:
  0.6 3.3 %copy-start = (bf16[512,2,8,128]{3,2,1,0:T(8,128)(2,1)S(1)}, bf16[512,2,8,128]{3,2,1,0:T(8,128)(2,1)}, u32[]{:S(2)}) copy-start(bf16[512,2,8,128]{3,2,1,0:T(8,128)(2,1)} %basis_ref.3) | copy-start | bytes 6291460
  0.6 3.3 %copy-start.8 = (s32[1,16]{1,0:T(1,128)S(1)}, s32[1,16]{1,0:T(1,128)}, u32[]{:S(2)}) copy-start(s32[1,16]{1,0:T(1,128)} %count_ref.1) | copy-start | bytes 196
  0.6 3.3 %copy-start.7 = (s32[1,16,2]{1,2,0:T(2,128)S(1)}, s32[1,16,2]{1,2,0:T(2,128)}, u32[]{:S(2)}) copy-start(s32[1,16,2]{1,2,0:T(2,128)} %param.13) | copy-start | bytes 388
  2.8 4.8 %collective-permute-start.1 = (bf16[140,8,128]{2,1,0:T(8,128)(2,1)}, bf16[140,8,128]{2,1,0:T(8,128)(2,1)S(1)}, u32[]{:S(2)}, u32[]{:S(2)}) collective-permute-start(bf16[140,8,128]{2,1,0:T(8,128)(2,1)} %get-tuple-element.36), channel_id=1, source_target_pairs={{0,1},{1,0},{2,3},{3,2},{4,5},{5,4},{6,7},{7,6},{8,9},{9,8},{10,11... | collective-permute-start | bytes 860168 | tf_op jit(solution)/shard_map/ppermute | solution.py:402
  3.3 5.2 %collective-permute-start = (bf16[140,8,128]{2,1,0:T(8,128)(2,1)}, bf16[140,8,128]{2,1,0:T(8,128)(2,1)S(1)}, u32[]{:S(2)}, u32[]{:S(2)}) collective-permute-start(bf16[140,8,128]{2,1,0:T(8,128)(2,1)} %get-tuple-element.28.after_ref), channel_id=1, source_target_pairs={{1,2},{2,1},{3,4},{4,3},{5,6},{6,5},{7,8},{8,7},{9,10},{10,9},{11,... | collective-permute-start | bytes 860168 | tf_op jit(solution)/shard_map/ppermute | solution.py:403
  4.0 1.0 %copy-start.2 = (bf16[140,8,128]{2,1,0:T(8,128)(2,1)S(1)}, bf16[140,8,128]{2,1,0:T(8,128)(2,1)}, u32[]{:S(2)}) copy-start(bf16[140,8,128]{2,1,0:T(8,128)(2,1)} %get-tuple-element.28.after_ref) | copy-start | bytes 860164
  5.1 0.8 %copy-start.3 = (f32[2,3,2,8,128]{4,3,2,1,0:T(8,128)S(1)}, f32[2,3,2,8,128]{4,3,2,1,0:T(8,128)}, u32[]{:S(2)}) copy-start(f32[2,3,2,8,128]{4,3,2,1,0:T(8,128)} %speed_ref.3) | copy-start | bytes 147460
  5.1 0.8 %copy-start.4 = (f32[2,3,2,8,128]{4,3,2,1,0:T(8,128)S(1)}, f32[2,3,2,8,128]{4,3,2,1,0:T(8,128)}, u32[]{:S(2)}) copy-start(f32[2,3,2,8,128]{4,3,2,1,0:T(8,128)} %diff_ref.3) | copy-start | bytes 147460
  5.2 0.8 %copy-start.5 = (s32[2,3,2,8,128]{4,3,2,1,0:T(8,128)S(1)}, s32[2,3,2,8,128]{4,3,2,1,0:T(8,128)}, u32[]{:S(2)}) copy-start(s32[2,3,2,8,128]{4,3,2,1,0:T(8,128)} %flag_ref.3) | copy-start | bytes 147460
  5.2 0.8 %copy-start.6 = (f32[2,2,8,128]{3,2,1,0:T(8,128)S(1)}, f32[2,2,8,128]{3,2,1,0:T(8,128)}, u32[]{:S(2)}) copy-start(f32[2,2,8,128]{3,2,1,0:T(8,128)} %react_ref.1) | copy-start | bytes 49156
  7.6 1.0 %copy-start.1 = (s32[320,8]{1,0:T(8,128)S(1)}, s32[320,8]{1,0:T(8,128)}, u32[]{:S(2)}) copy-start(s32[320,8]{1,0:T(8,128)} %constant.2.clone.table_ref.refs_3_) | copy-start | bytes 30724
  9.6 7.5 %collective-permute-start.2 = (bf16[1168,128]{1,0:T(8,128)(2,1)S(1)}, bf16[1168,128]{1,0:T(8,128)(2,1)S(1)}, u32[]{:S(2)}, u32[]{:S(2)}) collective-permute-start(bf16[1168,128]{1,0:T(8,128)(2,1)S(1)} %get-tuple-element.43), channel_id=1, source_target_pairs={{0,1},{1,0},{2,3},{3,2},{4,5},{5,4},{6,7},{7,6},{8,9},{9,8},{10,11... | collective-permute-start | bytes 897032 | tf_op jit(solution)/shard_map/ppermute | solution.py:511
  17.4 5.9 %collective-permute-start.3 = (bf16[400,128]{1,0:T(8,128)(2,1)S(1)}, bf16[400,128]{1,0:T(8,128)(2,1)S(1)}, u32[]{:S(2)}, u32[]{:S(2)}) collective-permute-start(bf16[400,128]{1,0:T(8,128)(2,1)S(1)} %get-tuple-element.46), channel_id=1, source_target_pairs={{0,2},{1,3},{2,0},{3,1},{4,6},{5,7},{6,4},{7,5},{8,10},{9,11},{10,... | collective-permute-start | bytes 307208 | tf_op jit(solution)/shard_map/ppermute | solution.py:511
  23.5 6.2 %collective-permute-start.4 = (bf16[144,128]{1,0:T(8,128)(2,1)S(1)}, bf16[144,128]{1,0:T(8,128)(2,1)S(1)}, u32[]{:S(2)}, u32[]{:S(2)}) collective-permute-start(bf16[144,128]{1,0:T(8,128)(2,1)S(1)} %get-tuple-element.49), channel_id=1, source_target_pairs={{0,12},{1,13},{2,14},{3,15},{4,8},{5,9},{6,10},{7,11},{8,4},{9,5},... | collective-permute-start | bytes 110600 | tf_op jit(solution)/shard_map/ppermute | solution.py:541
  27.8 4.0 %collective-permute-start.5 = (bf16[144,128]{1,0:T(8,128)(2,1)S(1)}, bf16[144,128]{1,0:T(8,128)(2,1)S(1)}, u32[]{:S(2)}, u32[]{:S(2)}) collective-permute-start(bf16[144,128]{1,0:T(8,128)(2,1)S(1)} %get-tuple-element.50), channel_id=1, source_target_pairs={{0,4},{1,5},{2,6},{3,7},{4,0},{5,1},{6,2},{7,3},{8,12},{9,13},{10,... | collective-permute-start | bytes 110600 | tf_op jit(solution)/shard_map/ppermute | solution.py:541
  27.8 4.9 %collective-permute-start.6 = (bf16[144,128]{1,0:T(8,128)(2,1)S(1)}, bf16[144,128]{1,0:T(8,128)(2,1)S(1)}, u32[]{:S(2)}, u32[]{:S(2)}) collective-permute-start(bf16[144,128]{1,0:T(8,128)(2,1)S(1)} %get-tuple-element.51), channel_id=1, source_target_pairs={{0,8},{1,9},{2,10},{3,11},{4,12},{5,13},{6,14},{7,15},{8,0},{9,1},... | collective-permute-start | bytes 110600 | tf_op jit(solution)/shard_map/ppermute | solution.py:541

commit v6 on v5

--- a/solution.py
+++ b/solution.py
@@ -18,7 +18,6 @@
 I32 = jnp.int32
 OFFSETS = 7
 VMEM = pl.BlockSpec(memory_space=pltpu.VMEM)
-ALONE = pltpu.CompilerParams(vmem_limit_bytes=60 * 1024 * 1024)
 SMALL = pl.CostEstimate(flops=1, bytes_accessed=1, transcendentals=0)
 LIMIT = pltpu.CompilerParams(vmem_limit_bytes=20 * 1024 * 1024)
 
@@ -392,9 +391,9 @@
             pltpu.VMEM((params, width_y, width_z), I32),
             pltpu.SemaphoreType.DMA((5,)),
         ],
-        compiler_params=ALONE,
+        compiler_params=LIMIT,
         name="pack_halo",
-    )(basis, face_speed, face_diffusion, upwind_flag)
+    )(*[pltpu.with_memory_space_constraint(value, pltpu.HBM) for value in (basis, face_speed, face_diffusion, upwind_flag)])
     inner_pairs = [(i, i ^ 1) for i in range(devices)]
     outer_pairs = []
     for i in range(1, devices - 1, 2):

time: 33.8 us -> 32.8 us (0.970)
  local copies, waits for them, and re-layouts: 1.79 us -> 0.84 us
  Pallas kernels: 7.27 us -> 6.44 us
  starting transfers between devices: 15.1 us -> 15.8 us
    unnamed x19 -> x17, local copies, waits for them, and re-layouts: 1.79 us -> 0.84 us
    pallas_call x1, Pallas kernels: 2.1 us -> 1.27 us  [shards(): pl.pallas_call(functools.partial(pack_kernel, (params, layers)), out_shap...]
    ppermute x2, starting transfers between devices: 9.03 us -> 9.78 us  [shards(): lax.ppermute(packet, 'cells', [(i, i ^ 1 << step) for i in range(devices)])]
where the time goes in v6:
time: 32.8 us; the launch traced here: 32.5 us
  starting transfers between devices  15.8 us (48%)
  waiting for transfers between devices  8.62 us (26%)
  Pallas kernels  6.44 us (20%)
  local copies, waits for them, and re-layouts  0.84 us (3%)
  between operations  0.81 us (2%)
    ppermute x2, starting transfers between devices, shards(): lax.ppermute(packet, 'cells', [(i, i ^ 1 << step) for i in range(devices)])  9.78 us
    ppermute x3, starting transfers between devices, shards(): lax.ppermute(packets[at - 1], 'cells', [(i, i ^ mask) for i in range(devi...  4.88 us
    ppermute x2, waiting for transfers between devices, shards(): lax.ppermute(packet, 'cells', [(i, i ^ 1 << step) for i in range(devices)])  4.4 us
    ppermute x3, waiting for transfers between devices, shards(): lax.ppermute(packets[at - 1], 'cells', [(i, i ^ mask) for i in range(devi...  4.22 us
    pallas_call x1, Pallas kernels, shards(): pl.pallas_call(functools.partial(local_kernel, (params, layers, width_y,...  1.55 us
    pallas_call x1, Pallas kernels, shards(): pl.pallas_call(functools.partial(pack_kernel, (params, layers)), out_shap...  1.27 us
    pallas_call x1, Pallas kernels, shards(): pl.pallas_call(functools.partial(project_kernel, (params, layers, width_y...  1.02 us
    pallas_call x1, Pallas kernels, shards(): pl.pallas_call(functools.partial(final_kernel, volume, steps, block), out...  0.97 us
  transfers between devices with their start and end apart: 7, of which 5 were waited for; matrix products, arithmetic and copies ran while one was open for 2% of the time, Pallas kernels for 8%

profile of v6, /device:TPU:0, one launch (start us, length us, event | category | flops | bytes accessed | tf_op | source)
XLA Modules:
  0.0 32.5 jit_solution(14766272484650341538)
XLA Ops:
  0.6 0.0 copy-start
  0.6 0.0 copy-start.7
  0.6 0.0 copy-start.6
  0.7 1.3 %pack_halo.1 = (bf16[140,8,128]{2,1,0:T(8,128)(2,1)S(1)}, bf16[140,8,128]{2,1,0:T(8,128)(2,1)S(1)}) custom-call(bf16[512,2,8,128]{3,2,1,0:T(8,128)(2,1)} %basis_ref.3, f32[2,3,2,8,128]{4,3,2,1,0:T(8,128)} %speed_ref.3, f32[2,3,2,8,128]{4,3,2,1,0:T(8,128)} %diff_ref.3, s32[2,3,2,8,128]{4,3,2,1,0:T(8,128)} %flag_ref.3), custom_call_target="tpu_custom_call" | custom-call | tf_op jit(solution)/shard_map/pack_halo/pallas_call | solution.py:383
  1.9 0.5 %collective-permute-start.1 = (bf16[140,8,128]{2,1,0:T(8,128)(2,1)S(1)}, bf16[140,8,128]{2,1,0:T(8,128)(2,1)S(1)}, u32[]{:S(2)}, u32[]{:S(2)}) collective-permute-start(bf16[140,8,128]{2,1,0:T(8,128)(2,1)S(1)} %get-tuple-element.36), channel_id=1, source_target_pairs={{0,1},{1,0},{2,3},{3,2},{4,5},{5,4},{6,7},{7,6},{8,9},{9,8},{10,11... | collective-permute-start | bytes 860168 | tf_op jit(solution)/shard_map/ppermute | solution.py:401
  2.5 0.7 %collective-permute-start = (bf16[140,8,128]{2,1,0:T(8,128)(2,1)S(1)}, bf16[140,8,128]{2,1,0:T(8,128)(2,1)S(1)}, u32[]{:S(2)}, u32[]{:S(2)}) collective-permute-start(bf16[140,8,128]{2,1,0:T(8,128)(2,1)S(1)} %get-tuple-element.28.after_ref), channel_id=1, source_target_pairs={{1,2},{2,1},{3,4},{4,3},{5,6},{6,5},{7,8},{8,7},{9,10},{10,9},{11,... | collective-permute-start | bytes 860168 | tf_op jit(solution)/shard_map/ppermute | solution.py:402
  3.1 0.0 copy-done
  3.1 0.0 copy-done.7
  3.2 0.0 copy-done.6
  3.2 0.2 load.1
  3.3 0.0 copy-start.2
  3.4 0.0 copy-start.3
  3.4 0.0 copy-start.4
  3.4 0.0 copy-start.5
  3.4 0.5 %copy.12 = bf16[64,8,16,128]{3,1,2,0:T(8,128)(2,1)S(1)} copy(bf16[64,8,16,128]{3,2,1,0:T(8,128)(2,1)S(1)} %bitcast.17) | data formatting | bytes 4194304
  3.9 0.2 copy-done.2
  4.1 0.0 copy-done.3
  4.2 0.0 copy-done.4
  4.2 0.0 copy-done.5
  4.2 1.6 %local_stencil.1 = (f32[256,2048]{1,0:T(8,128)S(1)}, f32[2,8,128]{2,1,0:T(8,128)S(1)}, bf16[224,128]{1,0:T(8,128)(2,1)S(1)}, bf16[32,2048]{1,0:T(8,128)(2,1)S(1)}, s32[32,1]{1,0:T(8,128)S(1)}) custom-call(bf16[512,2048]{1,0:T(8,128)(2,1)S(1)} %bitcast.14, f32[2,3,2,8,128]{4,3,2,1,0:T(8,128)S(1)} %copy-done.2, f32[2,3,2,8,128]{4,3,2,1,0:T(8,128)S(1)} %copy-done.3, ...), custom_call_target="tpu_custom_call" | custom-call | flops 1 | bytes 1 | tf_op jit(solution)/shard_map/local_stencil/pallas_call | solution.py:434
  5.8 0.0 collective-permute-done.1.inner_ref
  5.8 0.0 copy-start.1
  5.8 0.9 %near_layer.1 = (f32[512,256]{1,0:T(8,128)S(1)}, f32[32,256]{1,0:T(8,128)S(1)}, bf16[32,128]{1,0:T(8,128)(2,1)S(1)}) custom-call(bf16[512,2048]{1,0:T(8,128)(2,1)S(1)} %bitcast.15, bf16[140,8,128]{2,1,0:T(8,128)(2,1)S(1)} %collective-permute-done.1.inner_ref, f32[256,2048]{1,0:T(8,128)S(1)} %get-tuple-element.32.acc_ref, ...), custom_call_target="tpu_custom_call" | custom-call | flops 1 | bytes 1 | tf_op jit(solution)/shard_map/near_layer/pallas_call | solution.py:460
  6.7 0.0 collective-permute-done.outer_ref
  6.7 0.0 copy-done.1
  6.7 1.0 %project.1 = (f32[512,128]{1,0:T(8,128)S(1)}, bf16[144,128]{1,0:T(8,128)(2,1)S(1)}, bf16[1168,128]{1,0:T(8,128)(2,1)S(1)}) custom-call(bf16[512,2048]{1,0:T(8,128)(2,1)S(1)} %bitcast.16, bf16[140,8,128]{2,1,0:T(8,128)(2,1)S(1)} %collective-permute-done.outer_ref, f32[256,2048]{1,0:T(8,128)S(1)} %get-tuple-element.32.acc_ref, ...), custom_call_target="tpu_custom_call" | custom-call | tf_op jit(solution)/shard_map/project/pallas_call | solution.py:478
  7.8 7.0 %collective-permute-start.2 = (bf16[1168,128]{1,0:T(8,128)(2,1)S(1)}, bf16[1168,128]{1,0:T(8,128)(2,1)S(1)}, u32[]{:S(2)}, u32[]{:S(2)}) collective-permute-start(bf16[1168,128]{1,0:T(8,128)(2,1)S(1)} %get-tuple-element.43), channel_id=1, source_target_pairs={{0,1},{1,0},{2,3},{3,2},{4,5},{5,4},{6,7},{7,6},{8,9},{9,8},{10,11... | collective-permute-start | bytes 897032 | tf_op jit(solution)/shard_map/ppermute | solution.py:510
  14.7 1.2 %collective-permute-done.2.got_ref = bf16[1168,128]{1,0:T(8,128)(2,1)S(1)} collective-permute-done((bf16[1168,128]{1,0:T(8,128)(2,1)S(1)}, bf16[1168,128]{1,0:T(8,128)(2,1)S(1)}, u32[]{:S(2)}, u32[]{:S(2)}) %collective-permute-start.2) | collective-permute-done | bytes 299040 | tf_op jit(solution)/shard_map/ppermute | solution.py:510
  16.0 0.3 merge.1
  16.2 2.8 %collective-permute-start.3 = (bf16[400,128]{1,0:T(8,128)(2,1)S(1)}, bf16[400,128]{1,0:T(8,128)(2,1)S(1)}, u32[]{:S(2)}, u32[]{:S(2)}) collective-permute-start(bf16[400,128]{1,0:T(8,128)(2,1)S(1)} %get-tuple-element.46), channel_id=1, source_target_pairs={{0,2},{1,3},{2,0},{3,1},{4,6},{5,7},{6,4},{7,5},{8,10},{9,11},{10,... | collective-permute-start | bytes 307208 | tf_op jit(solution)/shard_map/ppermute | solution.py:510
  19.0 3.2 %collective-permute-done.3.got_ref = bf16[400,128]{1,0:T(8,128)(2,1)S(1)} collective-permute-done((bf16[400,128]{1,0:T(8,128)(2,1)S(1)}, bf16[400,128]{1,0:T(8,128)(2,1)S(1)}, u32[]{:S(2)}, u32[]{:S(2)}) %collective-permute-start.3) | collective-permute-done | bytes 102432 | tf_op jit(solution)/shard_map/ppermute | solution.py:510
  22.2 0.3 spread.1
  22.5 4.2 %collective-permute-start.4 = (bf16[144,128]{1,0:T(8,128)(2,1)S(1)}, bf16[144,128]{1,0:T(8,128)(2,1)S(1)}, u32[]{:S(2)}, u32[]{:S(2)}) collective-permute-start(bf16[144,128]{1,0:T(8,128)(2,1)S(1)} %get-tuple-element.49), channel_id=1, source_target_pairs={{0,12},{1,13},{2,14},{3,15},{4,8},{5,9},{6,10},{7,11},{8,4},{9,5},... | collective-permute-start | bytes 110600 | tf_op jit(solution)/shard_map/ppermute | solution.py:540
  26.7 0.0 collective-permute-start.5
  26.7 0.6 %collective-permute-start.6 = (bf16[144,128]{1,0:T(8,128)(2,1)S(1)}, bf16[144,128]{1,0:T(8,128)(2,1)S(1)}, u32[]{:S(2)}, u32[]{:S(2)}) collective-permute-start(bf16[144,128]{1,0:T(8,128)(2,1)S(1)} %get-tuple-element.51), channel_id=1, source_target_pairs={{0,8},{1,9},{2,10},{3,11},{4,12},{5,13},{6,14},{7,15},{8,0},{9,1},... | collective-permute-start | bytes 110600 | tf_op jit(solution)/shard_map/ppermute | solution.py:540
  27.4 1.3 %collective-permute-done.4.refs_0_ = bf16[144,128]{1,0:T(8,128)(2,1)S(1)} collective-permute-done((bf16[144,128]{1,0:T(8,128)(2,1)S(1)}, bf16[144,128]{1,0:T(8,128)(2,1)S(1)}, u32[]{:S(2)}, u32[]{:S(2)}) %collective-permute-start.4) | collective-permute-done | bytes 36896 | tf_op jit(solution)/shard_map/ppermute | solution.py:540
  28.7 2.0 %collective-permute-done.5.refs_1_ = bf16[144,128]{1,0:T(8,128)(2,1)S(1)} collective-permute-done((bf16[144,128]{1,0:T(8,128)(2,1)S(1)}, bf16[144,128]{1,0:T(8,128)(2,1)S(1)}, u32[]{:S(2)}, u32[]{:S(2)}) %collective-permute-start.5) | collective-permute-done | bytes 36896 | tf_op jit(solution)/shard_map/ppermute | solution.py:540
  30.7 0.9 %collective-permute-done.6.refs_2_ = bf16[144,128]{1,0:T(8,128)(2,1)S(1)} collective-permute-done((bf16[144,128]{1,0:T(8,128)(2,1)S(1)}, bf16[144,128]{1,0:T(8,128)(2,1)S(1)}, u32[]{:S(2)}, u32[]{:S(2)}) %collective-permute-start.6) | collective-permute-done | bytes 36896 | tf_op jit(solution)/shard_map/ppermute | solution.py:540
  31.6 1.0 %finish.1 = (f32[64,128]{1,0:T(8,128)}, bf16[288,128]{1,0:T(8,128)(2,1)}) custom-call(f32[64,128]{1,0:T(8,128)S(1)} %get-tuple-element.47.keep_ref, bf16[80,128]{1,0:T(8,128)(2,1)S(1)} %get-tuple-element.48.keep_rows_ref, bf16[144,128]{1,0:T(8,128)(2,1)S(1)} %collective-permute-done.4.refs_0_, bf16[144,128]{1,0:T(8,128)(2,1)S(1)} %collective-permute-done.5.refs_1_, ...), custom_call_target="tpu_custom_call" | custom-call | tf_op jit(solution)/shard_map/finish/pallas_call | solution.py:542
Async XLA Ops:
  0.6 2.5 %copy-start = (bf16[512,2,8,128]{3,2,1,0:T(8,128)(2,1)S(1)}, bf16[512,2,8,128]{3,2,1,0:T(8,128)(2,1)}, u32[]{:S(2)}) copy-start(bf16[512,2,8,128]{3,2,1,0:T(8,128)(2,1)} %basis_ref.3) | copy-start | bytes 6291460
  0.6 2.5 %copy-start.7 = (s32[1,16]{1,0:T(1,128)S(1)}, s32[1,16]{1,0:T(1,128)}, u32[]{:S(2)}) copy-start(s32[1,16]{1,0:T(1,128)} %count_ref.1) | copy-start | bytes 196
  0.6 2.5 %copy-start.6 = (s32[1,16,2]{1,2,0:T(2,128)S(1)}, s32[1,16,2]{1,2,0:T(2,128)}, u32[]{:S(2)}) copy-start(s32[1,16,2]{1,2,0:T(2,128)} %param.13) | copy-start | bytes 388
  1.9 3.8 %collective-permute-start.1 = (bf16[140,8,128]{2,1,0:T(8,128)(2,1)S(1)}, bf16[140,8,128]{2,1,0:T(8,128)(2,1)S(1)}, u32[]{:S(2)}, u32[]{:S(2)}) collective-permute-start(bf16[140,8,128]{2,1,0:T(8,128)(2,1)S(1)} %get-tuple-element.36), channel_id=1, source_target_pairs={{0,1},{1,0},{2,3},{3,2},{4,5},{5,4},{6,7},{7,6},{8,9},{9,8},{10,11... | collective-permute-start | bytes 860168 | tf_op jit(solution)/shard_map/ppermute | solution.py:401
  2.5 4.3 %collective-permute-start = (bf16[140,8,128]{2,1,0:T(8,128)(2,1)S(1)}, bf16[140,8,128]{2,1,0:T(8,128)(2,1)S(1)}, u32[]{:S(2)}, u32[]{:S(2)}) collective-permute-start(bf16[140,8,128]{2,1,0:T(8,128)(2,1)S(1)} %get-tuple-element.28.after_ref), channel_id=1, source_target_pairs={{1,2},{2,1},{3,4},{4,3},{5,6},{6,5},{7,8},{8,7},{9,10},{10,9},{11,... | collective-permute-start | bytes 860168 | tf_op jit(solution)/shard_map/ppermute | solution.py:402
  3.3 0.8 %copy-start.2 = (f32[2,3,2,8,128]{4,3,2,1,0:T(8,128)S(1)}, f32[2,3,2,8,128]{4,3,2,1,0:T(8,128)}, u32[]{:S(2)}) copy-start(f32[2,3,2,8,128]{4,3,2,1,0:T(8,128)} %speed_ref.3) | copy-start | bytes 147460
  3.4 0.8 %copy-start.3 = (f32[2,3,2,8,128]{4,3,2,1,0:T(8,128)S(1)}, f32[2,3,2,8,128]{4,3,2,1,0:T(8,128)}, u32[]{:S(2)}) copy-start(f32[2,3,2,8,128]{4,3,2,1,0:T(8,128)} %diff_ref.3) | copy-start | bytes 147460
  3.4 0.8 %copy-start.4 = (s32[2,3,2,8,128]{4,3,2,1,0:T(8,128)S(1)}, s32[2,3,2,8,128]{4,3,2,1,0:T(8,128)}, u32[]{:S(2)}) copy-start(s32[2,3,2,8,128]{4,3,2,1,0:T(8,128)} %flag_ref.3) | copy-start | bytes 147460
  3.4 0.8 %copy-start.5 = (f32[2,2,8,128]{3,2,1,0:T(8,128)S(1)}, f32[2,2,8,128]{3,2,1,0:T(8,128)}, u32[]{:S(2)}) copy-start(f32[2,2,8,128]{3,2,1,0:T(8,128)} %react_ref.1) | copy-start | bytes 49156
  5.8 1.0 %copy-start.1 = (s32[320,8]{1,0:T(8,128)S(1)}, s32[320,8]{1,0:T(8,128)}, u32[]{:S(2)}) copy-start(s32[320,8]{1,0:T(8,128)} %constant.2.clone.table_ref.refs_3_) | copy-start | bytes 30724
  7.8 8.2 %collective-permute-start.2 = (bf16[1168,128]{1,0:T(8,128)(2,1)S(1)}, bf16[1168,128]{1,0:T(8,128)(2,1)S(1)}, u32[]{:S(2)}, u32[]{:S(2)}) collective-permute-start(bf16[1168,128]{1,0:T(8,128)(2,1)S(1)} %get-tuple-element.43), channel_id=1, source_target_pairs={{0,1},{1,0},{2,3},{3,2},{4,5},{5,4},{6,7},{7,6},{8,9},{9,8},{10,11... | collective-permute-start | bytes 897032 | tf_op jit(solution)/shard_map/ppermute | solution.py:510
  16.2 6.0 %collective-permute-start.3 = (bf16[400,128]{1,0:T(8,128)(2,1)S(1)}, bf16[400,128]{1,0:T(8,128)(2,1)S(1)}, u32[]{:S(2)}, u32[]{:S(2)}) collective-permute-start(bf16[400,128]{1,0:T(8,128)(2,1)S(1)} %get-tuple-element.46), channel_id=1, source_target_pairs={{0,2},{1,3},{2,0},{3,1},{4,6},{5,7},{6,4},{7,5},{8,10},{9,11},{10,... | collective-permute-start | bytes 307208 | tf_op jit(solution)/shard_map/ppermute | solution.py:510
  22.5 6.2 %collective-permute-start.4 = (bf16[144,128]{1,0:T(8,128)(2,1)S(1)}, bf16[144,128]{1,0:T(8,128)(2,1)S(1)}, u32[]{:S(2)}, u32[]{:S(2)}) collective-permute-start(bf16[144,128]{1,0:T(8,128)(2,1)S(1)} %get-tuple-element.49), channel_id=1, source_target_pairs={{0,12},{1,13},{2,14},{3,15},{4,8},{5,9},{6,10},{7,11},{8,4},{9,5},... | collective-permute-start | bytes 110600 | tf_op jit(solution)/shard_map/ppermute | solution.py:540
  26.7 4.0 %collective-permute-start.5 = (bf16[144,128]{1,0:T(8,128)(2,1)S(1)}, bf16[144,128]{1,0:T(8,128)(2,1)S(1)}, u32[]{:S(2)}, u32[]{:S(2)}) collective-permute-start(bf16[144,128]{1,0:T(8,128)(2,1)S(1)} %get-tuple-element.50), channel_id=1, source_target_pairs={{0,4},{1,5},{2,6},{3,7},{4,0},{5,1},{6,2},{7,3},{8,12},{9,13},{10,... | collective-permute-start | bytes 110600 | tf_op jit(solution)/shard_map/ppermute | solution.py:540
  26.7 4.9 %collective-permute-start.6 = (bf16[144,128]{1,0:T(8,128)(2,1)S(1)}, bf16[144,128]{1,0:T(8,128)(2,1)S(1)}, u32[]{:S(2)}, u32[]{:S(2)}) collective-permute-start(bf16[144,128]{1,0:T(8,128)(2,1)S(1)} %get-tuple-element.51), channel_id=1, source_target_pairs={{0,8},{1,9},{2,10},{3,11},{4,12},{5,13},{6,14},{7,15},{8,0},{9,1},... | collective-permute-start | bytes 110600 | tf_op jit(solution)/shard_map/ppermute | solution.py:540

commit v7 on v6

--- a/solution.py
+++ b/solution.py
@@ -62,26 +62,32 @@
     return parts
 
 
-def pack_kernel(dims, basis_ref, speed_ref, diff_ref, flag_ref, inner_ref, outer_ref, speed_buf, diff_buf, flag_buf, sems):
+def pack_kernel(dims, basis_ref, speed_ref, diff_ref, flag_ref, low_ref, high_ref, outer_ref, speed_buf, diff_buf, flag_buf, sems):
     params, layers = dims
     last = layers - 1
+    half = MB // 2
     block = pl.ds(0, MB)
-    outer = pltpu.make_async_copy(basis_ref.at[block, core() * last], outer_ref.at[block], sems.at[0])
-    inner = pltpu.make_async_copy(basis_ref.at[block, (1 - core()) * last], inner_ref.at[block], sems.at[1])
+    low, high = pl.ds(0, half), pl.ds(half, half)
+    beside = (1 - core()) * last
+    layers_out = [
+        pltpu.make_async_copy(basis_ref.at[block, core() * last], outer_ref.at[block], sems.at[0]),
+        pltpu.make_async_copy(basis_ref.at[low, beside], low_ref.at[low], sems.at[1]),
+        pltpu.make_async_copy(basis_ref.at[high, beside], high_ref, sems.at[5]),
+    ]
     copies = [
         pltpu.make_async_copy(speed_ref.at[:, 0, last], speed_buf, sems.at[2]),
         pltpu.make_async_copy(diff_ref.at[:, 0, last], diff_buf, sems.at[3]),
         pltpu.make_async_copy(flag_ref.at[:, 0, last], flag_buf, sems.at[4]),
     ]
-    for copy in copies + [outer, inner]:
+    for copy in copies + layers_out:
         copy.start()
     for copy in copies:
         copy.wait()
     for at, part in enumerate(face_parts(speed_buf[...], diff_buf[...], flag_buf[...])):
-        inner_ref[MB + at * params : MB + (at + 1) * params] = part
+        low_ref[half + at * params : half + (at + 1) * params] = part
         outer_ref[MB + at * params : MB + (at + 1) * params] = part
-    outer.wait()
-    inner.wait()
+    for copy in layers_out:
+        copy.wait()
 
 
 def load_kernel(basis_ref, cell_ref, count_ref, after_ref, basis_out, cell_out, count_out, sems):
@@ -193,18 +199,21 @@
     in_ref[...] = nt_dot(pick_ref[...], flat_ref[:MB, :]).astype(BF16)
 
 
-def finish_layer(dims, from_next, layer, halo_ref, flat_ref, acc_ref, edge_ref, applied_ref, coef_ref, spread_ref, beside_ref):
+def finish_layer(dims, from_next, layer, halo_refs, flat_ref, acc_ref, edge_ref, applied_ref, coef_ref, spread_ref, beside_ref):
     params, layers, width_y, width_z, plane = dims
+    held = MB // len(halo_refs)
     faces = []
     for at in range(2 * SPLITS):
-        part = halo_ref[MB + at * params : MB + (at + 1) * params].astype(F32)
+        part = halo_refs[0][held + at * params : held + (at + 1) * params].astype(F32)
         faces.append(part.reshape(params * width_y, width_z))
     signed = faces[0] + faces[1] + faces[2]
     diff = faces[3] + faces[4] + faces[5]
     edge = edge_ref[...].reshape(params * width_y, width_z)
     coef_ref[0] = jnp.where(from_next, edge, -(jnp.maximum(signed, 0.0) + diff))
     coef_ref[1] = jnp.where(from_next, 0.0, diff - jnp.minimum(signed, 0.0))
-    spread_ref[...] = halo_ref[:MB].astype(F32).reshape(MB * width_y, width_z)
+    size = held * width_y
+    for at, halo_ref in enumerate(halo_refs):
+        spread_ref[at * size : (at + 1) * size] = halo_ref[:held].astype(F32).reshape(size, width_z)
     for y in range(width_y):
         at = pl.multiple_of(layer * plane + y * width_z, width_z)
         lanes = slice(y * width_z, (y + 1) * width_z)
@@ -220,12 +229,12 @@
             applied_ref[modes, lanes] = total.astype(BF16)
 
 
-def near_kernel(dims, flat_ref, inner_ref, acc_ref, edge_ref, center_ref, cell_ref, sums_ref, picks_ref, side_ref, *scratch):
+def near_kernel(dims, flat_ref, low_ref, high_ref, acc_ref, edge_ref, center_ref, cell_ref, sums_ref, picks_ref, side_ref, *scratch):
     params, layers, width_y, width_z, plane, samples = dims
     odd = core() == 1
     layer = (1 - core()) * (layers - 1)
     start = pl.multiple_of(layer * plane, plane)
-    finish_layer(dims[:5], jnp.logical_not(odd), layer, inner_ref, flat_ref, acc_ref, edge_ref, *scratch)
+    finish_layer(dims[:5], jnp.logical_not(odd), layer, (low_ref, high_ref), flat_ref, acc_ref, edge_ref, *scratch)
     applied_ref, beside_ref = scratch[0], scratch[3]
     sums_ref[...] = nt_dot(flat_ref[:, pl.ds(start, plane)], applied_ref[...])
     picks_ref[...] = nt_dot(center_ref[:, pl.ds(start, plane)], applied_ref[...])
@@ -258,7 +267,7 @@
     odd = core() == 1
     layer = core() * (layers - 1)
     lane = pl.multiple_of(layer * plane, plane)
-    finish_layer(dims[:5], odd, layer, outer_ref, flat_ref, acc_ref, edge_ref, *scratch)
+    finish_layer(dims[:5], odd, layer, (outer_ref,), flat_ref, acc_ref, edge_ref, *scratch)
     applied_ref, beside_ref = scratch[0], scratch[3]
 
     sums = near_sums_ref[...] + nt_dot(flat_ref[:, pl.ds(lane, plane)], applied_ref[...])
@@ -379,17 +388,20 @@
     tail = params * width_y
     hbm = pl.BlockSpec(memory_space=pltpu.HBM)
     planes = 2 * SPLITS * params
-    packed = shape((MB + planes, width_y, width_z), BF16)
-    to_inner, to_outer = pl.pallas_call(
+    to_low, to_high, to_outer = pl.pallas_call(
         functools.partial(pack_kernel, (params, layers)),
-        out_shape=(packed, packed),
+        out_shape=(
+            shape((MB // 2 + planes, width_y, width_z), BF16),
+            shape((MB // 2, width_y, width_z), BF16),
+            shape((MB + planes, width_y, width_z), BF16),
+        ),
         in_specs=[hbm] * 4,
-        out_specs=(VMEM, VMEM),
+        out_specs=(VMEM,) * 3,
         scratch_shapes=[
             pltpu.VMEM((params, width_y, width_z), F32),
             pltpu.VMEM((params, width_y, width_z), F32),
             pltpu.VMEM((params, width_y, width_z), I32),
-            pltpu.SemaphoreType.DMA((5,)),
+            pltpu.SemaphoreType.DMA((6,)),
         ],
         compiler_params=LIMIT,
         name="pack_halo",
@@ -398,7 +410,8 @@
     outer_pairs = []
     for i in range(1, devices - 1, 2):
         outer_pairs += [(i, i + 1), (i + 1, i)]
-    inner = lax.ppermute(to_inner, "cells", inner_pairs)
+    low = lax.ppermute(to_low, "cells", inner_pairs)
+    high = lax.ppermute(to_high, "cells", inner_pairs)
     outer = lax.ppermute(to_outer, "cells", outer_pairs)
 
     loaded, cells_in, counts_in = pl.pallas_call(
@@ -464,13 +477,13 @@
             shape((samples, params * MB), F32),
             shape((samples, MB), BF16),
         ),
-        in_specs=[VMEM] * 6,
+        in_specs=[VMEM] * 7,
         out_specs=(VMEM,) * 3,
         scratch_shapes=finish_scratch,
         compiler_params=LIMIT,
         cost_estimate=SMALL,
         name="near_layer",
-    )(flat, inner, acc, edge, center, cell)
+    )(flat, low, high, acc, edge, center, cell)
 
     size = own * params
     half = devices // 2

time: 32.8 us -> 32.2 us (0.982)
  starting transfers between devices: 15.8 us -> 15.4 us
    ppermute x2, starting transfers between devices: 9.78 us -> 5.77 us  [shards(): lax.ppermute(packet, 'cells', [(i, i ^ 1 << step) for i in range(devices)])]
    ppermute x1 -> x2, starting transfers between devices: 0.52 us -> 4.46 us  [the longest x1 4.38 us: shards(): low = lax.ppermute(to_low, 'cells', inner_pairs)]
    ppermute x3, starting transfers between devices: 4.88 us -> 4.45 us  [shards(): lax.ppermute(packets[at - 1], 'cells', [(i, i ^ mask) for i in range(devi...]
  transfers between devices with their start and end apart: 7 -> 8, of which waited for: 5 -> 5; matrix products, arithmetic and copies ran while one was open for 2% -> 2% of each run, Pallas kernels for 8% -> 8%
where the time goes in v7:
time: 32.2 us; the launch traced here: 31.9 us
  starting transfers between devices  15.4 us (48%)
  waiting for transfers between devices  8.46 us (26%)
  Pallas kernels  6.47 us (20%)
  local copies, waits for them, and re-layouts  0.84 us (3%)
  between operations  0.79 us (2%)
    ppermute x2, starting transfers between devices, shards(): lax.ppermute(packet, 'cells', [(i, i ^ 1 << step) for i in range(devices)])  5.77 us
    ppermute x3, starting transfers between devices, shards(): lax.ppermute(packets[at - 1], 'cells', [(i, i ^ mask) for i in range(devi...  4.45 us
    ppermute x2, waiting for transfers between devices, shards(): lax.ppermute(packet, 'cells', [(i, i ^ 1 << step) for i in range(devices)])  4.4 us
    ppermute x1, starting transfers between devices, shards(): low = lax.ppermute(to_low, 'cells', inner_pairs)  4.38 us
    ppermute x3, waiting for transfers between devices, shards(): lax.ppermute(packets[at - 1], 'cells', [(i, i ^ mask) for i in range(devi...  4.06 us
    pallas_call x1, Pallas kernels, shards(): pl.pallas_call(functools.partial(local_kernel, (params, layers, width_y,...  1.55 us
    pallas_call x1, Pallas kernels, shards(): pl.pallas_call(functools.partial(pack_kernel, (params, layers)), out_shap...  1.3 us
    pallas_call x1, Pallas kernels, shards(): pl.pallas_call(functools.partial(project_kernel, (params, layers, width_y...  1.02 us
  transfers between devices with their start and end apart: 8, of which 5 were waited for; matrix products, arithmetic and copies ran while one was open for 2% of the time, Pallas kernels for 8%

profile of v7, /device:TPU:0, one launch (start us, length us, event | category | flops | bytes accessed | tf_op | source)
XLA Modules:
  0.0 31.9 jit_solution(5271748946727302431)
XLA Ops:
  0.6 0.0 copy-start
  0.6 0.0 copy-start.7
  0.6 0.0 copy-start.6
  0.7 1.3 %pack_halo.1 = (bf16[76,8,128]{2,1,0:T(8,128)(2,1)S(1)}, bf16[64,8,128]{2,1,0:T(8,128)(2,1)S(1)}, bf16[140,8,128]{2,1,0:T(8,128)(2,1)S(1)}) custom-call(bf16[512,2,8,128]{3,2,1,0:T(8,128)(2,1)} %basis_ref.3, f32[2,3,2,8,128]{4,3,2,1,0:T(8,128)} %speed_ref.3, f32[2,3,2,8,128]{4,3,2,1,0:T(8,128)} %diff_ref.3, s32[2,3,2,8,128]{4,3,2,1,0:T(8,128)} %flag_ref.3), custom_call_target="tpu_custom_call" | custom-call | tf_op jit(solution)/shard_map/pack_halo/pallas_call | solution.py:391
  2.0 0.7 %collective-permute-start = (bf16[140,8,128]{2,1,0:T(8,128)(2,1)S(1)}, bf16[140,8,128]{2,1,0:T(8,128)(2,1)S(1)}, u32[]{:S(2)}, u32[]{:S(2)}) collective-permute-start(bf16[140,8,128]{2,1,0:T(8,128)(2,1)S(1)} %get-tuple-element.29.after_ref), channel_id=1, source_target_pairs={{1,2},{2,1},{3,4},{4,3},{5,6},{6,5},{7,8},{8,7},{9,10},{10,9},{11,... | collective-permute-start | bytes 860168 | tf_op jit(solution)/shard_map/ppermute | solution.py:415
  2.6 4.4 %collective-permute-start.1 = (bf16[76,8,128]{2,1,0:T(8,128)(2,1)S(1)}, bf16[76,8,128]{2,1,0:T(8,128)(2,1)S(1)}, u32[]{:S(2)}, u32[]{:S(2)}) collective-permute-start(bf16[76,8,128]{2,1,0:T(8,128)(2,1)S(1)} %get-tuple-element.37), channel_id=1, source_target_pairs={{0,1},{1,0},{2,3},{3,2},{4,5},{5,4},{6,7},{7,6},{8,9},{9,8},{10,11... | collective-permute-start | bytes 466952 | tf_op jit(solution)/shard_map/ppermute | solution.py:413
  7.0 0.1 collective-permute-start.2
  7.1 0.0 copy-done
  7.1 0.0 copy-done.7
  7.1 0.0 copy-done.6
  7.1 0.2 load.1
  7.3 0.0 copy-start.2
  7.3 0.0 copy-start.3
  7.3 0.0 copy-start.4
  7.3 0.0 copy-start.5
  7.3 0.6 %copy.12 = bf16[64,8,16,128]{3,1,2,0:T(8,128)(2,1)S(1)} copy(bf16[64,8,16,128]{3,2,1,0:T(8,128)(2,1)S(1)} %bitcast.17) | data formatting | bytes 4194304
  7.9 0.2 copy-done.2
  8.1 0.0 copy-done.3
  8.1 0.0 copy-done.4
  8.2 0.0 copy-done.5
  8.2 1.5 %local_stencil.1 = (f32[256,2048]{1,0:T(8,128)S(1)}, f32[2,8,128]{2,1,0:T(8,128)S(1)}, bf16[224,128]{1,0:T(8,128)(2,1)S(1)}, bf16[32,2048]{1,0:T(8,128)(2,1)S(1)}, s32[32,1]{1,0:T(8,128)S(1)}) custom-call(bf16[512,2048]{1,0:T(8,128)(2,1)S(1)} %bitcast.14, f32[2,3,2,8,128]{4,3,2,1,0:T(8,128)S(1)} %copy-done.2, f32[2,3,2,8,128]{4,3,2,1,0:T(8,128)S(1)} %copy-done.3, ...), custom_call_target="tpu_custom_call" | custom-call | flops 1 | bytes 1 | tf_op jit(solution)/shard_map/local_stencil/pallas_call | solution.py:447
  9.7 0.0 collective-permute-done.2.high_ref
  9.7 0.0 collective-permute-done.1.low_ref
  9.7 0.0 copy-start.1
  9.7 0.9 %near_layer.1 = (f32[512,256]{1,0:T(8,128)S(1)}, f32[32,256]{1,0:T(8,128)S(1)}, bf16[32,128]{1,0:T(8,128)(2,1)S(1)}) custom-call(bf16[512,2048]{1,0:T(8,128)(2,1)S(1)} %bitcast.15, bf16[76,8,128]{2,1,0:T(8,128)(2,1)S(1)} %collective-permute-done.1.low_ref, bf16[64,8,128]{2,1,0:T(8,128)(2,1)S(1)} %collective-permute-done.2.high_ref, ...), custom_call_target="tpu_custom_call" | custom-call | flops 1 | bytes 1 | tf_op jit(solution)/shard_map/near_layer/pallas_call | solution.py:473
  10.7 0.0 collective-permute-done.outer_ref
  10.7 0.0 copy-done.1
  10.7 1.0 %project.1 = (f32[512,128]{1,0:T(8,128)S(1)}, bf16[144,128]{1,0:T(8,128)(2,1)S(1)}, bf16[1168,128]{1,0:T(8,128)(2,1)S(1)}) custom-call(bf16[512,2048]{1,0:T(8,128)(2,1)S(1)} %bitcast.16, bf16[140,8,128]{2,1,0:T(8,128)(2,1)S(1)} %collective-permute-done.outer_ref, f32[256,2048]{1,0:T(8,128)S(1)} %get-tuple-element.33.acc_ref, ...), custom_call_target="tpu_custom_call" | custom-call | tf_op jit(solution)/shard_map/project/pallas_call | solution.py:491
  11.7 3.0 %collective-permute-start.3 = (bf16[1168,128]{1,0:T(8,128)(2,1)S(1)}, bf16[1168,128]{1,0:T(8,128)(2,1)S(1)}, u32[]{:S(2)}, u32[]{:S(2)}) collective-permute-start(bf16[1168,128]{1,0:T(8,128)(2,1)S(1)} %get-tuple-element.45), channel_id=1, source_target_pairs={{0,1},{1,0},{2,3},{3,2},{4,5},{5,4},{6,7},{7,6},{8,9},{9,8},{10,11... | collective-permute-start | bytes 897032 | tf_op jit(solution)/shard_map/ppermute | solution.py:523
  14.7 1.2 %collective-permute-done.3.got_ref = bf16[1168,128]{1,0:T(8,128)(2,1)S(1)} collective-permute-done((bf16[1168,128]{1,0:T(8,128)(2,1)S(1)}, bf16[1168,128]{1,0:T(8,128)(2,1)S(1)}, u32[]{:S(2)}, u32[]{:S(2)}) %collective-permute-start.3) | collective-permute-done | bytes 299040 | tf_op jit(solution)/shard_map/ppermute | solution.py:523
  15.9 0.3 merge.1
  16.2 2.8 %collective-permute-start.4 = (bf16[400,128]{1,0:T(8,128)(2,1)S(1)}, bf16[400,128]{1,0:T(8,128)(2,1)S(1)}, u32[]{:S(2)}, u32[]{:S(2)}) collective-permute-start(bf16[400,128]{1,0:T(8,128)(2,1)S(1)} %get-tuple-element.48), channel_id=1, source_target_pairs={{0,2},{1,3},{2,0},{3,1},{4,6},{5,7},{6,4},{7,5},{8,10},{9,11},{10,... | collective-permute-start | bytes 307208 | tf_op jit(solution)/shard_map/ppermute | solution.py:523
  19.0 3.2 %collective-permute-done.4.got_ref = bf16[400,128]{1,0:T(8,128)(2,1)S(1)} collective-permute-done((bf16[400,128]{1,0:T(8,128)(2,1)S(1)}, bf16[400,128]{1,0:T(8,128)(2,1)S(1)}, u32[]{:S(2)}, u32[]{:S(2)}) %collective-permute-start.4) | collective-permute-done | bytes 102432 | tf_op jit(solution)/shard_map/ppermute | solution.py:523
  22.2 0.3 spread.1
  22.4 3.7 %collective-permute-start.5 = (bf16[144,128]{1,0:T(8,128)(2,1)S(1)}, bf16[144,128]{1,0:T(8,128)(2,1)S(1)}, u32[]{:S(2)}, u32[]{:S(2)}) collective-permute-start(bf16[144,128]{1,0:T(8,128)(2,1)S(1)} %get-tuple-element.51), channel_id=1, source_target_pairs={{0,12},{1,13},{2,14},{3,15},{4,8},{5,9},{6,10},{7,11},{8,4},{9,5},... | collective-permute-start | bytes 110600 | tf_op jit(solution)/shard_map/ppermute | solution.py:553
  26.1 0.0 collective-permute-start.6
  26.1 0.8 %collective-permute-start.7 = (bf16[144,128]{1,0:T(8,128)(2,1)S(1)}, bf16[144,128]{1,0:T(8,128)(2,1)S(1)}, u32[]{:S(2)}, u32[]{:S(2)}) collective-permute-start(bf16[144,128]{1,0:T(8,128)(2,1)S(1)} %get-tuple-element.53), channel_id=1, source_target_pairs={{0,8},{1,9},{2,10},{3,11},{4,12},{5,13},{6,14},{7,15},{8,0},{9,1},... | collective-permute-start | bytes 110600 | tf_op jit(solution)/shard_map/ppermute | solution.py:553
  26.9 1.4 %collective-permute-done.5.refs_0_ = bf16[144,128]{1,0:T(8,128)(2,1)S(1)} collective-permute-done((bf16[144,128]{1,0:T(8,128)(2,1)S(1)}, bf16[144,128]{1,0:T(8,128)(2,1)S(1)}, u32[]{:S(2)}, u32[]{:S(2)}) %collective-permute-start.5) | collective-permute-done | bytes 36896 | tf_op jit(solution)/shard_map/ppermute | solution.py:553
  28.3 1.8 %collective-permute-done.6.refs_1_ = bf16[144,128]{1,0:T(8,128)(2,1)S(1)} collective-permute-done((bf16[144,128]{1,0:T(8,128)(2,1)S(1)}, bf16[144,128]{1,0:T(8,128)(2,1)S(1)}, u32[]{:S(2)}, u32[]{:S(2)}) %collective-permute-start.6) | collective-permute-done | bytes 36896 | tf_op jit(solution)/shard_map/ppermute | solution.py:553
  30.0 0.9 %collective-permute-done.7.refs_2_ = bf16[144,128]{1,0:T(8,128)(2,1)S(1)} collective-permute-done((bf16[144,128]{1,0:T(8,128)(2,1)S(1)}, bf16[144,128]{1,0:T(8,128)(2,1)S(1)}, u32[]{:S(2)}, u32[]{:S(2)}) %collective-permute-start.7) | collective-permute-done | bytes 36896 | tf_op jit(solution)/shard_map/ppermute | solution.py:553
  30.9 1.0 %finish.1 = (f32[64,128]{1,0:T(8,128)}, bf16[288,128]{1,0:T(8,128)(2,1)}) custom-call(f32[64,128]{1,0:T(8,128)S(1)} %get-tuple-element.49.keep_ref, bf16[80,128]{1,0:T(8,128)(2,1)S(1)} %get-tuple-element.50.keep_rows_ref, bf16[144,128]{1,0:T(8,128)(2,1)S(1)} %collective-permute-done.5.refs_0_, bf16[144,128]{1,0:T(8,128)(2,1)S(1)} %collective-permute-done.6.refs_1_, ...), custom_call_target="tpu_custom_call" | custom-call | tf_op jit(solution)/shard_map/finish/pallas_call | solution.py:555
Async XLA Ops:
  0.6 6.5 %copy-start = (bf16[512,2,8,128]{3,2,1,0:T(8,128)(2,1)S(1)}, bf16[512,2,8,128]{3,2,1,0:T(8,128)(2,1)}, u32[]{:S(2)}) copy-start(bf16[512,2,8,128]{3,2,1,0:T(8,128)(2,1)} %basis_ref.3) | copy-start | bytes 6291460
  0.6 6.5 %copy-start.7 = (s32[1,16]{1,0:T(1,128)S(1)}, s32[1,16]{1,0:T(1,128)}, u32[]{:S(2)}) copy-start(s32[1,16]{1,0:T(1,128)} %count_ref.1) | copy-start | bytes 196
  0.6 6.5 %copy-start.6 = (s32[1,16,2]{1,2,0:T(2,128)S(1)}, s32[1,16,2]{1,2,0:T(2,128)}, u32[]{:S(2)}) copy-start(s32[1,16,2]{1,2,0:T(2,128)} %param.13) | copy-start | bytes 388
  2.0 8.7 %collective-permute-start = (bf16[140,8,128]{2,1,0:T(8,128)(2,1)S(1)}, bf16[140,8,128]{2,1,0:T(8,128)(2,1)S(1)}, u32[]{:S(2)}, u32[]{:S(2)}) collective-permute-start(bf16[140,8,128]{2,1,0:T(8,128)(2,1)S(1)} %get-tuple-element.29.after_ref), channel_id=1, source_target_pairs={{1,2},{2,1},{3,4},{4,3},{5,6},{6,5},{7,8},{8,7},{9,10},{10,9},{11,... | collective-permute-start | bytes 860168 | tf_op jit(solution)/shard_map/ppermute | solution.py:415
  2.6 7.1 %collective-permute-start.1 = (bf16[76,8,128]{2,1,0:T(8,128)(2,1)S(1)}, bf16[76,8,128]{2,1,0:T(8,128)(2,1)S(1)}, u32[]{:S(2)}, u32[]{:S(2)}) collective-permute-start(bf16[76,8,128]{2,1,0:T(8,128)(2,1)S(1)} %get-tuple-element.37), channel_id=1, source_target_pairs={{0,1},{1,0},{2,3},{3,2},{4,5},{5,4},{6,7},{7,6},{8,9},{9,8},{10,11... | collective-permute-start | bytes 466952 | tf_op jit(solution)/shard_map/ppermute | solution.py:413
  7.0 2.7 %collective-permute-start.2 = (bf16[64,8,128]{2,1,0:T(8,128)(2,1)S(1)}, bf16[64,8,128]{2,1,0:T(8,128)(2,1)S(1)}, u32[]{:S(2)}, u32[]{:S(2)}) collective-permute-start(bf16[64,8,128]{2,1,0:T(8,128)(2,1)S(1)} %get-tuple-element.38), channel_id=1, source_target_pairs={{0,1},{1,0},{2,3},{3,2},{4,5},{5,4},{6,7},{7,6},{8,9},{9,8},{10,11... | collective-permute-start | bytes 393224 | tf_op jit(solution)/shard_map/ppermute | solution.py:414
  7.3 0.8 %copy-start.2 = (f32[2,3,2,8,128]{4,3,2,1,0:T(8,128)S(1)}, f32[2,3,2,8,128]{4,3,2,1,0:T(8,128)}, u32[]{:S(2)}) copy-start(f32[2,3,2,8,128]{4,3,2,1,0:T(8,128)} %speed_ref.3) | copy-start | bytes 147460
  7.3 0.8 %copy-start.3 = (f32[2,3,2,8,128]{4,3,2,1,0:T(8,128)S(1)}, f32[2,3,2,8,128]{4,3,2,1,0:T(8,128)}, u32[]{:S(2)}) copy-start(f32[2,3,2,8,128]{4,3,2,1,0:T(8,128)} %diff_ref.3) | copy-start | bytes 147460
  7.3 0.8 %copy-start.4 = (s32[2,3,2,8,128]{4,3,2,1,0:T(8,128)S(1)}, s32[2,3,2,8,128]{4,3,2,1,0:T(8,128)}, u32[]{:S(2)}) copy-start(s32[2,3,2,8,128]{4,3,2,1,0:T(8,128)} %flag_ref.3) | copy-start | bytes 147460
  7.3 0.8 %copy-start.5 = (f32[2,2,8,128]{3,2,1,0:T(8,128)S(1)}, f32[2,2,8,128]{3,2,1,0:T(8,128)}, u32[]{:S(2)}) copy-start(f32[2,2,8,128]{3,2,1,0:T(8,128)} %react_ref.1) | copy-start | bytes 49156
  9.7 1.0 %copy-start.1 = (s32[320,8]{1,0:T(8,128)S(1)}, s32[320,8]{1,0:T(8,128)}, u32[]{:S(2)}) copy-start(s32[320,8]{1,0:T(8,128)} %constant.2.clone.table_ref.refs_3_) | copy-start | bytes 30724
  11.7 4.2 %collective-permute-start.3 = (bf16[1168,128]{1,0:T(8,128)(2,1)S(1)}, bf16[1168,128]{1,0:T(8,128)(2,1)S(1)}, u32[]{:S(2)}, u32[]{:S(2)}) collective-permute-start(bf16[1168,128]{1,0:T(8,128)(2,1)S(1)} %get-tuple-element.45), channel_id=1, source_target_pairs={{0,1},{1,0},{2,3},{3,2},{4,5},{5,4},{6,7},{7,6},{8,9},{9,8},{10,11... | collective-permute-start | bytes 897032 | tf_op jit(solution)/shard_map/ppermute | solution.py:523
  16.2 6.0 %collective-permute-start.4 = (bf16[400,128]{1,0:T(8,128)(2,1)S(1)}, bf16[400,128]{1,0:T(8,128)(2,1)S(1)}, u32[]{:S(2)}, u32[]{:S(2)}) collective-permute-start(bf16[400,128]{1,0:T(8,128)(2,1)S(1)} %get-tuple-element.48), channel_id=1, source_target_pairs={{0,2},{1,3},{2,0},{3,1},{4,6},{5,7},{6,4},{7,5},{8,10},{9,11},{10,... | collective-permute-start | bytes 307208 | tf_op jit(solution)/shard_map/ppermute | solution.py:523
  22.4 5.8 %collective-permute-start.5 = (bf16[144,128]{1,0:T(8,128)(2,1)S(1)}, bf16[144,128]{1,0:T(8,128)(2,1)S(1)}, u32[]{:S(2)}, u32[]{:S(2)}) collective-permute-start(bf16[144,128]{1,0:T(8,128)(2,1)S(1)} %get-tuple-element.51), channel_id=1, source_target_pairs={{0,12},{1,13},{2,14},{3,15},{4,8},{5,9},{6,10},{7,11},{8,4},{9,5},... | collective-permute-start | bytes 110600 | tf_op jit(solution)/shard_map/ppermute | solution.py:553
  26.1 4.0 %collective-permute-start.6 = (bf16[144,128]{1,0:T(8,128)(2,1)S(1)}, bf16[144,128]{1,0:T(8,128)(2,1)S(1)}, u32[]{:S(2)}, u32[]{:S(2)}) collective-permute-start(bf16[144,128]{1,0:T(8,128)(2,1)S(1)} %get-tuple-element.52), channel_id=1, source_target_pairs={{0,4},{1,5},{2,6},{3,7},{4,0},{5,1},{6,2},{7,3},{8,12},{9,13},{10,... | collective-permute-start | bytes 110600 | tf_op jit(solution)/shard_map/ppermute | solution.py:553
  26.1 4.9 %collective-permute-start.7 = (bf16[144,128]{1,0:T(8,128)(2,1)S(1)}, bf16[144,128]{1,0:T(8,128)(2,1)S(1)}, u32[]{:S(2)}, u32[]{:S(2)}) collective-permute-start(bf16[144,128]{1,0:T(8,128)(2,1)S(1)} %get-tuple-element.53), channel_id=1, source_target_pairs={{0,8},{1,9},{2,10},{3,11},{4,12},{5,13},{6,14},{7,15},{8,0},{9,1},... | collective-permute-start | bytes 110600 | tf_op jit(solution)/shard_map/ppermute | solution.py:553

commit v8 on v7

--- a/solution.py
+++ b/solution.py
@@ -299,14 +299,21 @@
     pieces += [in_ref[:samples], got_below, got_above, in_ref[3 * samples :]]
     gathered = jnp.concatenate(pieces, axis=0)
     total_rows = gathered.shape[0]
-    order = picked((table_ref[:total_rows, 1:2] ^ me) + table_ref[:total_rows, 2:3], 0, gathered.shape[0])
+    order = picked((table_ref[:, 0:1] ^ me) + table_ref[:, 1:2], 0, gathered.shape[0])
     ordered = jnp.dot(order, gathered, preferred_element_type=F32).astype(BF16)
     count = ordered.shape[0] // 2
     keep_rows_ref[...] = ordered[:count]
     packet_ref[2 * half * size :] = ordered[count:]
 
 
-def merge_kernel(wide_in, wide_out, keep_ref, keep_rows_ref, got_ref, table_ref, keep_out, rows_out, packet_out):
+def move_rows(rows, moves, from_ref, to_ref):
+    block, pairs = moves
+    from_ref[...] = rows.astype(F32)
+    for new, old in pairs:
+        to_ref[pl.ds(new, block), :] = from_ref[pl.ds(old, block), :]
+
+
+def merge_kernel(wide_in, wide_out, moves, keep_ref, keep_rows_ref, got_ref, keep_out, rows_out, packet_out, from_ref, to_ref):
     size = keep_ref.shape[0]
     half = size // 2
     total = keep_ref[...] + got_ref[:size].astype(F32)
@@ -321,13 +328,13 @@
         packet_out[:half] = total[half:].astype(BF16)
     count = keep_rows_ref.shape[0]
     rows = jnp.concatenate([keep_rows_ref[...], got_ref[got_ref.shape[0] - count :]], axis=0)
-    order = picked(table_ref[: 2 * count, 0:1], 0, 2 * count)
-    ordered = jnp.dot(order, rows, preferred_element_type=F32).astype(BF16)
+    move_rows(rows, moves, from_ref, to_ref)
+    ordered = to_ref[...].astype(BF16)
     rows_out[...] = ordered[:count]
     packet_out[packet_out.shape[0] - count :] = ordered[count:]
 
 
-def spread_kernel(wide_in, room, keep_ref, keep_rows_ref, got_ref, table_ref, keep_out, rows_out, *packets_out):
+def spread_kernel(wide_in, room, moves, keep_ref, keep_rows_ref, got_ref, keep_out, rows_out, *refs):
     size = keep_ref.shape[0]
     total = keep_ref[...] + got_ref[:size].astype(F32)
     if wide_in:
@@ -335,8 +342,10 @@
     part = size // DIRECT
     count = keep_rows_ref.shape[0]
     rows = jnp.concatenate([keep_rows_ref[...], got_ref[got_ref.shape[0] - count :]], axis=0)
-    order = picked(table_ref[: DIRECT * room, 5:6], 0, 2 * count)
-    ordered = jnp.dot(order, rows, preferred_element_type=F32).astype(BF16)
+    packets_out, from_ref, to_ref = refs[:-2], refs[-2], refs[-1]
+    to_ref[...] = jnp.zeros(to_ref.shape, F32)
+    move_rows(rows, moves, from_ref, to_ref)
+    ordered = to_ref[...].astype(BF16)
     keep_out[...] = total[:part]
     rows_out[...] = ordered[:room]
     for at, packet_out in enumerate(packets_out, 1):
@@ -344,10 +353,10 @@
         packet_out[part:] = ordered[at * room : (at + 1) * room]
 
 
-def final_kernel(volume, steps, block, keep_ref, keep_rows_ref, *refs):
-    got_refs, table_ref, sum_out, rows_out = refs[: DIRECT - 1], refs[-3], refs[-2], refs[-1]
+def final_kernel(volume, block, olds, keep_ref, keep_rows_ref, *refs):
+    got_refs = refs[: DIRECT - 1]
+    sum_out, rows_out, from_ref, to_ref = refs[DIRECT - 1 :]
     size = keep_ref.shape[0]
-    room = keep_rows_ref.shape[0]
     total = keep_ref[...]
     rows = [keep_rows_ref[...]] + [None] * (DIRECT - 1)
     for at, got_ref in zip(ORDER, got_refs):
@@ -355,14 +364,9 @@
         rows[at] = got_ref[size:]
     sum_out[...] = volume * total
     me = lax.axis_index("cells")
-    mine = 0
-    for step, place in enumerate(places(steps)):
-        mine = mine + (((me >> step) & 1) << place)
-    came = table_ref[: rows_out.shape[0], 3:4] ^ mine
-    low = steps - 2
-    start = (came >> low) * room + (came & ((1 << low) - 1)) * block
-    order = picked(start + table_ref[: rows_out.shape[0], 4:5], 0, DIRECT * room)
-    rows_out[...] = jnp.dot(order, jnp.concatenate(rows, axis=0), preferred_element_type=F32).astype(BF16)
+    pairs = [((me ^ at) * block, old) for at, old in enumerate(olds)]
+    move_rows(jnp.concatenate(rows, axis=0), (block, pairs), from_ref, to_ref)
+    rows_out[...] = to_ref[...].astype(BF16)
 
 
 def places(steps):
@@ -422,7 +426,7 @@
         scratch_shapes=[pltpu.SemaphoreType.DMA((3,))],
         compiler_params=LIMIT,
         name="load",
-    )(basis, sample_cell[0].T, sample_count, to_outer)
+    )(pltpu.with_memory_space_constraint(basis, pltpu.HBM), sample_cell[0].T, sample_count, to_outer)
     flat = loaded.reshape(modes, cells)
 
     block = slots * rows
@@ -430,19 +434,18 @@
     block = slots * rows
     share = devices // DIRECT * block
     room = round_up(share, 16)
-    table = np.full((DIRECT * room, 8), -1, np.int32)
     in_block = np.arange(block)
+    table = np.zeros((devices, block, 8), np.int32)
+    turns, spreads, olds = [], [], []
     for place in range(devices):
-        turned = (((place & 1) << (steps - 1)) + (place >> 1)) * block + in_block
-        at = slice(place * block, (place + 1) * block)
-        table[at, 0] = turned
-        table[at, 1] = relative[place]
-        table[at, 2] = (in_block // slots) * samples + (in_block % slots) * devices
-        table[at, 3] = sum(((place >> step) & 1) << to for step, to in enumerate(places(steps)))
-        table[at, 4] = in_block
-        start = place * block // share * room + place * block % share
-        table[start : start + block, 5] = turned
-    table = jnp.asarray(table)
+        old = (((place & 1) << (steps - 1)) + (place >> 1)) * block
+        turns.append((place * block, old))
+        spreads.append((place * block // share * room + place * block % share, old))
+        came = sum(((place >> step) & 1) << to for step, to in enumerate(places(steps)))
+        olds.append(came * block // share * room + came * block % share)
+        table[place, :, 0] = relative[place]
+        table[place, :, 1] = (in_block // slots) * samples + (in_block % slots) * devices
+    table = jnp.asarray(table.reshape(devices * block, 8))
 
     acc, edge, got_in, center, cell = pl.pallas_call(
         functools.partial(local_kernel, (params, layers, width_y, width_z, plane, samples)),
@@ -526,40 +529,43 @@
             half //= 2
             packet_rows = (2 if next_wide else 1) * half * size + count
             keep, keep_rows, packet = pl.pallas_call(
-                functools.partial(merge_kernel, wide, next_wide),
+                functools.partial(merge_kernel, wide, next_wide, (block, turns)),
                 out_shape=(
                     shape((half * size, MB), F32),
                     shape((count, MB), BF16),
                     shape((packet_rows, MB), BF16),
                 ),
-                in_specs=[VMEM] * 4,
+                in_specs=[VMEM] * 3,
                 out_specs=(VMEM,) * 3,
+                scratch_shapes=[pltpu.VMEM((2 * count, MB), F32), pltpu.VMEM((2 * count, MB), F32)],
                 compiler_params=LIMIT,
                 name="merge",
-            )(keep, keep_rows, got, table)
+            )(keep, keep_rows, got)
             wide = next_wide
     sent = shape((size + room, MB), BF16)
     keep, keep_rows, *packets = pl.pallas_call(
-        functools.partial(spread_kernel, wide, room),
+        functools.partial(spread_kernel, wide, room, (block, spreads)),
         out_shape=(shape((size, MB), F32), shape((room, MB), BF16)) + (sent,) * (DIRECT - 1),
-        in_specs=[VMEM] * 4,
+        in_specs=[VMEM] * 3,
         out_specs=(VMEM,) * (DIRECT + 1),
+        scratch_shapes=[pltpu.VMEM((2 * count, MB), F32), pltpu.VMEM((DIRECT * room, MB), F32)],
         compiler_params=LIMIT,
         name="spread",
-    )(keep, keep_rows, got, table)
+    )(keep, keep_rows, got)
     got = [None] * DIRECT
     for at in ORDER:
         mask = ((at >> 1) << (steps - 2)) | ((at & 1) << (steps - 1))
         got[at] = lax.ppermute(packets[at - 1], "cells", [(i, i ^ mask) for i in range(devices)])
     volume = 1.0 / (layers * devices * width_y * width_z)
     summed, sampled = pl.pallas_call(
-        functools.partial(final_kernel, volume, steps, block),
+        functools.partial(final_kernel, volume, block, olds),
         out_shape=(shape((size, MB), F32), shape((2 * count, MB), BF16)),
-        in_specs=[VMEM] * (DIRECT + 2),
+        in_specs=[VMEM] * (DIRECT + 1),
         out_specs=(VMEM,) * 2,
+        scratch_shapes=[pltpu.VMEM((DIRECT * room, MB), F32), pltpu.VMEM((2 * count, MB), F32)],
         compiler_params=LIMIT,
         name="finish",
-    )(keep, keep_rows, *[got[at] for at in ORDER], table)
+    )(keep, keep_rows, *[got[at] for at in ORDER])
     galerkin = summed.reshape(own, params, MB)
     sampled = sampled.reshape(devices, rows, slots, MB)
     return (galerkin, jnp.transpose(sampled, (0, 2, 1, 3))[None])

time: 32.2 us -> 31.3 us (0.972)
  starting transfers between devices: 15.4 us -> 13.9 us
  Pallas kernels: 6.47 us -> 7.12 us
    ppermute x2, starting transfers between devices: 5.77 us -> 4.32 us  [shards(): lax.ppermute(packet, 'cells', [(i, i ^ 1 << step) for i in range(devices)])]
    pallas_call x1, Pallas kernels: 0.17 us -> 1.62 us  [shards(): pl.pallas_call(load_kernel, out_shape=(shape(basis.shape, BF16), shape((s...]
    pallas_call x3, Pallas kernels: 1.5 us -> 0.81 us  [the longest x1 0.68 us: shards(): pl.pallas_call(functools.partial(final_kernel, volume, block, olds), out_...]
    unnamed x17 -> x15, local copies, waits for them, and re-layouts: 0.84 us -> 0.83 us
  transfers between devices with their start and end apart: 8 -> 8, of which waited for: 5 -> 5; matrix products, arithmetic and copies ran while one was open for 2% -> 2% of each run, Pallas kernels for 8% -> 13%
where the time goes in v8:
time: 31.3 us; the launch traced here: 31.1 us
  starting transfers between devices  13.9 us (44%)
  waiting for transfers between devices  8.47 us (27%)
  Pallas kernels  7.12 us (23%)
  local copies, waits for them, and re-layouts  0.83 us (3%)
  between operations  0.78 us (2%)
    ppermute x3, starting transfers between devices, shards(): lax.ppermute(packets[at - 1], 'cells', [(i, i ^ mask) for i in range(devi...  4.45 us
    ppermute x2, waiting for transfers between devices, shards(): lax.ppermute(packet, 'cells', [(i, i ^ 1 << step) for i in range(devices)])  4.4 us
    ppermute x1, starting transfers between devices, shards(): low = lax.ppermute(to_low, 'cells', inner_pairs)  4.38 us
    ppermute x2, starting transfers between devices, shards(): lax.ppermute(packet, 'cells', [(i, i ^ 1 << step) for i in range(devices)])  4.32 us
    ppermute x3, waiting for transfers between devices, shards(): lax.ppermute(packets[at - 1], 'cells', [(i, i ^ mask) for i in range(devi...  4.06 us
    pallas_call x1, Pallas kernels, shards(): pl.pallas_call(load_kernel, out_shape=(shape(basis.shape, BF16), shape((s...  1.62 us
    pallas_call x1, Pallas kernels, shards(): pl.pallas_call(functools.partial(local_kernel, (params, layers, width_y,...  1.55 us
    pallas_call x1, Pallas kernels, shards(): pl.pallas_call(functools.partial(pack_kernel, (params, layers)), out_shap...  1.16 us
  transfers between devices with their start and end apart: 8, of which 5 were waited for; matrix products, arithmetic and copies ran while one was open for 2% of the time, Pallas kernels for 13%

profile of v8, /device:TPU:0, one launch (start us, length us, event | category | flops | bytes accessed | tf_op | source)
XLA Modules:
  0.0 31.1 jit_solution(6357369078518645317)
XLA Ops:
  0.6 0.0 copy-start.6
  0.6 0.0 copy-start.5
  0.6 1.2 %pack_halo.1 = (bf16[76,8,128]{2,1,0:T(8,128)(2,1)S(1)}, bf16[64,8,128]{2,1,0:T(8,128)(2,1)S(1)}, bf16[140,8,128]{2,1,0:T(8,128)(2,1)S(1)}) custom-call(bf16[512,2,8,128]{3,2,1,0:T(8,128)(2,1)} %basis_ref.3, f32[2,3,2,8,128]{4,3,2,1,0:T(8,128)} %speed_ref.3, f32[2,3,2,8,128]{4,3,2,1,0:T(8,128)} %diff_ref.3, s32[2,3,2,8,128]{4,3,2,1,0:T(8,128)} %flag_ref.3), custom_call_target="tpu_custom_call" | custom-call | tf_op jit(solution)/shard_map/pack_halo/pallas_call | solution.py:395
  1.8 0.7 %collective-permute-start = (bf16[140,8,128]{2,1,0:T(8,128)(2,1)S(1)}, bf16[140,8,128]{2,1,0:T(8,128)(2,1)S(1)}, u32[]{:S(2)}, u32[]{:S(2)}) collective-permute-start(bf16[140,8,128]{2,1,0:T(8,128)(2,1)S(1)} %get-tuple-element.29.after_ref), channel_id=1, source_target_pairs={{1,2},{2,1},{3,4},{4,3},{5,6},{6,5},{7,8},{8,7},{9,10},{10,9},{11,... | collective-permute-start | bytes 860168 | tf_op jit(solution)/shard_map/ppermute | solution.py:419
  2.5 4.4 %collective-permute-start.1 = (bf16[76,8,128]{2,1,0:T(8,128)(2,1)S(1)}, bf16[76,8,128]{2,1,0:T(8,128)(2,1)S(1)}, u32[]{:S(2)}, u32[]{:S(2)}) collective-permute-start(bf16[76,8,128]{2,1,0:T(8,128)(2,1)S(1)} %get-tuple-element.37), channel_id=1, source_target_pairs={{0,1},{1,0},{2,3},{3,2},{4,5},{5,4},{6,7},{7,6},{8,9},{9,8},{10,11... | collective-permute-start | bytes 466952 | tf_op jit(solution)/shard_map/ppermute | solution.py:417
  6.9 0.1 collective-permute-start.2
  7.0 0.0 copy-done.6
  7.0 0.0 copy-done.5
  7.0 1.6 %load.1 = (bf16[512,2,8,128]{3,2,1,0:T(8,128)(2,1)S(1)}, s32[2,16]{1,0:T(2,128)S(1)}, s32[1,16]{1,0:T(1,128)S(1)}) custom-call(bf16[512,2,8,128]{3,2,1,0:T(8,128)(2,1)} %basis_ref.3, s32[2,16]{1,0:T(2,128)S(1)} %bitcast.18, s32[1,16]{1,0:T(1,128)S(1)} %copy-done.6, bf16[140,8,128]{2,1,0:T(8,128)(2,1)S(1)} %get-tuple-element.29.after_ref), custom_call_target="tpu_custom_call" | custom-call | tf_op jit(solution)/shard_map/load/pallas_call | solution.py:421
  8.6 0.0 copy-start
  8.6 0.0 copy-start.1
  8.6 0.0 copy-start.2
  8.6 0.0 copy-start.4
  8.6 0.5 %copy.12 = bf16[64,8,16,128]{3,1,2,0:T(8,128)(2,1)S(1)} copy(bf16[64,8,16,128]{3,2,1,0:T(8,128)(2,1)S(1)} %bitcast.17) | data formatting | bytes 4194304
  9.2 0.2 copy-done
  9.4 0.0 copy-done.1
  9.4 0.0 copy-done.2
  9.4 0.0 copy-done.4
  9.5 1.6 %local_stencil.1 = (f32[256,2048]{1,0:T(8,128)S(1)}, f32[2,8,128]{2,1,0:T(8,128)S(1)}, bf16[224,128]{1,0:T(8,128)(2,1)S(1)}, bf16[32,2048]{1,0:T(8,128)(2,1)S(1)}, s32[32,1]{1,0:T(8,128)S(1)}) custom-call(bf16[512,2048]{1,0:T(8,128)(2,1)S(1)} %bitcast.14, f32[2,3,2,8,128]{4,3,2,1,0:T(8,128)S(1)} %copy-done, f32[2,3,2,8,128]{4,3,2,1,0:T(8,128)S(1)} %copy-done.1, ...), custom_call_target="tpu_custom_call" | custom-call | flops 1 | bytes 1 | tf_op jit(solution)/shard_map/local_stencil/pallas_call | solution.py:450
  11.0 0.0 collective-permute-done.2.high_ref
  11.0 0.0 collective-permute-done.1.low_ref
  11.0 0.0 copy-start.3
  11.0 0.9 %near_layer.1 = (f32[512,256]{1,0:T(8,128)S(1)}, f32[32,256]{1,0:T(8,128)S(1)}, bf16[32,128]{1,0:T(8,128)(2,1)S(1)}) custom-call(bf16[512,2048]{1,0:T(8,128)(2,1)S(1)} %bitcast.15, bf16[76,8,128]{2,1,0:T(8,128)(2,1)S(1)} %collective-permute-done.1.low_ref, bf16[64,8,128]{2,1,0:T(8,128)(2,1)S(1)} %collective-permute-done.2.high_ref, ...), custom_call_target="tpu_custom_call" | custom-call | flops 1 | bytes 1 | tf_op jit(solution)/shard_map/near_layer/pallas_call | solution.py:476
  12.0 0.0 collective-permute-done.outer_ref
  12.0 0.0 copy-done.3
  12.0 1.0 %project.1 = (f32[512,128]{1,0:T(8,128)S(1)}, bf16[144,128]{1,0:T(8,128)(2,1)S(1)}, bf16[1168,128]{1,0:T(8,128)(2,1)S(1)}) custom-call(bf16[512,2048]{1,0:T(8,128)(2,1)S(1)} %bitcast.16, bf16[140,8,128]{2,1,0:T(8,128)(2,1)S(1)} %collective-permute-done.outer_ref, f32[256,2048]{1,0:T(8,128)S(1)} %get-tuple-element.33.acc_ref, ...), custom_call_target="tpu_custom_call" | custom-call | tf_op jit(solution)/shard_map/project/pallas_call | solution.py:494
  13.1 1.5 %collective-permute-start.3 = (bf16[1168,128]{1,0:T(8,128)(2,1)S(1)}, bf16[1168,128]{1,0:T(8,128)(2,1)S(1)}, u32[]{:S(2)}, u32[]{:S(2)}) collective-permute-start(bf16[1168,128]{1,0:T(8,128)(2,1)S(1)} %get-tuple-element.45), channel_id=1, source_target_pairs={{0,1},{1,0},{2,3},{3,2},{4,5},{5,4},{6,7},{7,6},{8,9},{9,8},{10,11... | collective-permute-start | bytes 897032 | tf_op jit(solution)/shard_map/ppermute | solution.py:526
  14.6 1.2 %collective-permute-done.3.got_ref = bf16[1168,128]{1,0:T(8,128)(2,1)S(1)} collective-permute-done((bf16[1168,128]{1,0:T(8,128)(2,1)S(1)}, bf16[1168,128]{1,0:T(8,128)(2,1)S(1)}, u32[]{:S(2)}, u32[]{:S(2)}) %collective-permute-start.3) | collective-permute-done | bytes 299040 | tf_op jit(solution)/shard_map/ppermute | solution.py:526
  15.8 0.1 merge.1
  15.9 2.8 %collective-permute-start.4 = (bf16[400,128]{1,0:T(8,128)(2,1)S(1)}, bf16[400,128]{1,0:T(8,128)(2,1)S(1)}, u32[]{:S(2)}, u32[]{:S(2)}) collective-permute-start(bf16[400,128]{1,0:T(8,128)(2,1)S(1)} %get-tuple-element.48), channel_id=1, source_target_pairs={{0,2},{1,3},{2,0},{3,1},{4,6},{5,7},{6,4},{7,5},{8,10},{9,11},{10,... | collective-permute-start | bytes 307208 | tf_op jit(solution)/shard_map/ppermute | solution.py:526
  18.7 3.2 %collective-permute-done.4.got_ref = bf16[400,128]{1,0:T(8,128)(2,1)S(1)} collective-permute-done((bf16[400,128]{1,0:T(8,128)(2,1)S(1)}, bf16[400,128]{1,0:T(8,128)(2,1)S(1)}, u32[]{:S(2)}, u32[]{:S(2)}) %collective-permute-start.4) | collective-permute-done | bytes 102432 | tf_op jit(solution)/shard_map/ppermute | solution.py:526
  21.9 3.7 %collective-permute-start.5 = (bf16[144,128]{1,0:T(8,128)(2,1)S(1)}, bf16[144,128]{1,0:T(8,128)(2,1)S(1)}, u32[]{:S(2)}, u32[]{:S(2)}) collective-permute-start(bf16[144,128]{1,0:T(8,128)(2,1)S(1)} %get-tuple-element.51), channel_id=1, source_target_pairs={{0,12},{1,13},{2,14},{3,15},{4,8},{5,9},{6,10},{7,11},{8,4},{9,5},... | collective-permute-start | bytes 110600 | tf_op jit(solution)/shard_map/ppermute | solution.py:558
  25.6 0.0 collective-permute-start.6
  25.6 0.8 %collective-permute-start.7 = (bf16[144,128]{1,0:T(8,128)(2,1)S(1)}, bf16[144,128]{1,0:T(8,128)(2,1)S(1)}, u32[]{:S(2)}, u32[]{:S(2)}) collective-permute-start(bf16[144,128]{1,0:T(8,128)(2,1)S(1)} %get-tuple-element.53), channel_id=1, source_target_pairs={{0,8},{1,9},{2,10},{3,11},{4,12},{5,13},{6,14},{7,15},{8,0},{9,1},... | collective-permute-start | bytes 110600 | tf_op jit(solution)/shard_map/ppermute | solution.py:558
  26.4 1.4 %collective-permute-done.5.refs_0_ = bf16[144,128]{1,0:T(8,128)(2,1)S(1)} collective-permute-done((bf16[144,128]{1,0:T(8,128)(2,1)S(1)}, bf16[144,128]{1,0:T(8,128)(2,1)S(1)}, u32[]{:S(2)}, u32[]{:S(2)}) %collective-permute-start.5) | collective-permute-done | bytes 36896 | tf_op jit(solution)/shard_map/ppermute | solution.py:558
  27.8 1.8 %collective-permute-done.6.refs_1_ = bf16[144,128]{1,0:T(8,128)(2,1)S(1)} collective-permute-done((bf16[144,128]{1,0:T(8,128)(2,1)S(1)}, bf16[144,128]{1,0:T(8,128)(2,1)S(1)}, u32[]{:S(2)}, u32[]{:S(2)}) %collective-permute-start.6) | collective-permute-done | bytes 36896 | tf_op jit(solution)/shard_map/ppermute | solution.py:558
  29.5 0.9 %collective-permute-done.7.refs_2_ = bf16[144,128]{1,0:T(8,128)(2,1)S(1)} collective-permute-done((bf16[144,128]{1,0:T(8,128)(2,1)S(1)}, bf16[144,128]{1,0:T(8,128)(2,1)S(1)}, u32[]{:S(2)}, u32[]{:S(2)}) %collective-permute-start.7) | collective-permute-done | bytes 36896 | tf_op jit(solution)/shard_map/ppermute | solution.py:558
  30.4 0.7 %finish.1 = (f32[64,128]{1,0:T(8,128)}, bf16[288,128]{1,0:T(8,128)(2,1)}) custom-call(f32[64,128]{1,0:T(8,128)S(1)} %get-tuple-element.49.keep_ref, bf16[80,128]{1,0:T(8,128)(2,1)S(1)} %get-tuple-element.50.keep_rows_ref, bf16[144,128]{1,0:T(8,128)(2,1)S(1)} %collective-permute-done.5.refs_0_, bf16[144,128]{1,0:T(8,128)(2,1)S(1)} %collective-permute-done.6.refs_1_, ...), custom_call_target="tpu_custom_call" | custom-call | tf_op jit(solution)/shard_map/finish/pallas_call | solution.py:560
  (1 shorter events, 0.0 us)
Async XLA Ops:
  0.6 6.3 %copy-start.6 = (s32[1,16]{1,0:T(1,128)S(1)}, s32[1,16]{1,0:T(1,128)}, u32[]{:S(2)}) copy-start(s32[1,16]{1,0:T(1,128)} %count_ref.1) | copy-start | bytes 196
  0.6 6.3 %copy-start.5 = (s32[1,16,2]{1,2,0:T(2,128)S(1)}, s32[1,16,2]{1,2,0:T(2,128)}, u32[]{:S(2)}) copy-start(s32[1,16,2]{1,2,0:T(2,128)} %param.13) | copy-start | bytes 388
  1.8 10.2 %collective-permute-start = (bf16[140,8,128]{2,1,0:T(8,128)(2,1)S(1)}, bf16[140,8,128]{2,1,0:T(8,128)(2,1)S(1)}, u32[]{:S(2)}, u32[]{:S(2)}) collective-permute-start(bf16[140,8,128]{2,1,0:T(8,128)(2,1)S(1)} %get-tuple-element.29.after_ref), channel_id=1, source_target_pairs={{1,2},{2,1},{3,4},{4,3},{5,6},{6,5},{7,8},{8,7},{9,10},{10,9},{11,... | collective-permute-start | bytes 860168 | tf_op jit(solution)/shard_map/ppermute | solution.py:419
  2.5 8.5 %collective-permute-start.1 = (bf16[76,8,128]{2,1,0:T(8,128)(2,1)S(1)}, bf16[76,8,128]{2,1,0:T(8,128)(2,1)S(1)}, u32[]{:S(2)}, u32[]{:S(2)}) collective-permute-start(bf16[76,8,128]{2,1,0:T(8,128)(2,1)S(1)} %get-tuple-element.37), channel_id=1, source_target_pairs={{0,1},{1,0},{2,3},{3,2},{4,5},{5,4},{6,7},{7,6},{8,9},{9,8},{10,11... | collective-permute-start | bytes 466952 | tf_op jit(solution)/shard_map/ppermute | solution.py:417
  6.9 4.1 %collective-permute-start.2 = (bf16[64,8,128]{2,1,0:T(8,128)(2,1)S(1)}, bf16[64,8,128]{2,1,0:T(8,128)(2,1)S(1)}, u32[]{:S(2)}, u32[]{:S(2)}) collective-permute-start(bf16[64,8,128]{2,1,0:T(8,128)(2,1)S(1)} %get-tuple-element.38), channel_id=1, source_target_pairs={{0,1},{1,0},{2,3},{3,2},{4,5},{5,4},{6,7},{7,6},{8,9},{9,8},{10,11... | collective-permute-start | bytes 393224 | tf_op jit(solution)/shard_map/ppermute | solution.py:418
  8.6 0.8 %copy-start = (f32[2,3,2,8,128]{4,3,2,1,0:T(8,128)S(1)}, f32[2,3,2,8,128]{4,3,2,1,0:T(8,128)}, u32[]{:S(2)}) copy-start(f32[2,3,2,8,128]{4,3,2,1,0:T(8,128)} %speed_ref.3) | copy-start | bytes 147460
  8.6 0.8 %copy-start.1 = (f32[2,3,2,8,128]{4,3,2,1,0:T(8,128)S(1)}, f32[2,3,2,8,128]{4,3,2,1,0:T(8,128)}, u32[]{:S(2)}) copy-start(f32[2,3,2,8,128]{4,3,2,1,0:T(8,128)} %diff_ref.3) | copy-start | bytes 147460
  8.6 0.8 %copy-start.2 = (s32[2,3,2,8,128]{4,3,2,1,0:T(8,128)S(1)}, s32[2,3,2,8,128]{4,3,2,1,0:T(8,128)}, u32[]{:S(2)}) copy-start(s32[2,3,2,8,128]{4,3,2,1,0:T(8,128)} %flag_ref.3) | copy-start | bytes 147460
  8.6 0.8 %copy-start.4 = (f32[2,2,8,128]{3,2,1,0:T(8,128)S(1)}, f32[2,2,8,128]{3,2,1,0:T(8,128)}, u32[]{:S(2)}) copy-start(f32[2,2,8,128]{3,2,1,0:T(8,128)} %react_ref.1) | copy-start | bytes 49156
  11.0 1.0 %copy-start.3 = (s32[288,8]{1,0:T(8,128)S(1)}, s32[288,8]{1,0:T(8,128)}, u32[]{:S(2)}) copy-start(s32[288,8]{1,0:T(8,128)} %constant.2.clone.table_ref) | copy-start | bytes 27652
  13.1 2.7 %collective-permute-start.3 = (bf16[1168,128]{1,0:T(8,128)(2,1)S(1)}, bf16[1168,128]{1,0:T(8,128)(2,1)S(1)}, u32[]{:S(2)}, u32[]{:S(2)}) collective-permute-start(bf16[1168,128]{1,0:T(8,128)(2,1)S(1)} %get-tuple-element.45), channel_id=1, source_target_pairs={{0,1},{1,0},{2,3},{3,2},{4,5},{5,4},{6,7},{7,6},{8,9},{9,8},{10,11... | collective-permute-start | bytes 897032 | tf_op jit(solution)/shard_map/ppermute | solution.py:526
  15.9 6.0 %collective-permute-start.4 = (bf16[400,128]{1,0:T(8,128)(2,1)S(1)}, bf16[400,128]{1,0:T(8,128)(2,1)S(1)}, u32[]{:S(2)}, u32[]{:S(2)}) collective-permute-start(bf16[400,128]{1,0:T(8,128)(2,1)S(1)} %get-tuple-element.48), channel_id=1, source_target_pairs={{0,2},{1,3},{2,0},{3,1},{4,6},{5,7},{6,4},{7,5},{8,10},{9,11},{10,... | collective-permute-start | bytes 307208 | tf_op jit(solution)/shard_map/ppermute | solution.py:526
  21.9 5.8 %collective-permute-start.5 = (bf16[144,128]{1,0:T(8,128)(2,1)S(1)}, bf16[144,128]{1,0:T(8,128)(2,1)S(1)}, u32[]{:S(2)}, u32[]{:S(2)}) collective-permute-start(bf16[144,128]{1,0:T(8,128)(2,1)S(1)} %get-tuple-element.51), channel_id=1, source_target_pairs={{0,12},{1,13},{2,14},{3,15},{4,8},{5,9},{6,10},{7,11},{8,4},{9,5},... | collective-permute-start | bytes 110600 | tf_op jit(solution)/shard_map/ppermute | solution.py:558
  25.6 4.0 %collective-permute-start.6 = (bf16[144,128]{1,0:T(8,128)(2,1)S(1)}, bf16[144,128]{1,0:T(8,128)(2,1)S(1)}, u32[]{:S(2)}, u32[]{:S(2)}) collective-permute-start(bf16[144,128]{1,0:T(8,128)(2,1)S(1)} %get-tuple-element.52), channel_id=1, source_target_pairs={{0,4},{1,5},{2,6},{3,7},{4,0},{5,1},{6,2},{7,3},{8,12},{9,13},{10,... | collective-permute-start | bytes 110600 | tf_op jit(solution)/shard_map/ppermute | solution.py:558
  25.6 4.9 %collective-permute-start.7 = (bf16[144,128]{1,0:T(8,128)(2,1)S(1)}, bf16[144,128]{1,0:T(8,128)(2,1)S(1)}, u32[]{:S(2)}, u32[]{:S(2)}) collective-permute-start(bf16[144,128]{1,0:T(8,128)(2,1)S(1)} %get-tuple-element.53), channel_id=1, source_target_pairs={{0,8},{1,9},{2,10},{3,11},{4,12},{5,13},{6,14},{7,15},{8,0},{9,1},... | collective-permute-start | bytes 110600 | tf_op jit(solution)/shard_map/ppermute | solution.py:558

commit v9 on v8

--- a/solution.py
+++ b/solution.py
@@ -282,10 +282,8 @@
         if place < half:
             keep_ref[place * size : (place + 1) * size] = terms
         else:
-            head, rest = halves(terms)
             at = (place - half) * size
-            packet_ref[at : at + size] = head
-            packet_ref[half * size + at : half * size + at + size] = rest
+            packet_ref[at : at + size] = terms.astype(BF16)
 
     picks = nt_dot(center_ref[:, pl.ds(lane, plane)], applied_ref[...])
     got_applied = (near_picks_ref[...] + picks).astype(BF16)
@@ -303,7 +301,7 @@
     ordered = jnp.dot(order, gathered, preferred_element_type=F32).astype(BF16)
     count = ordered.shape[0] // 2
     keep_rows_ref[...] = ordered[:count]
-    packet_ref[2 * half * size :] = ordered[count:]
+    packet_ref[half * size :] = ordered[count:]
 
 
 def move_rows(rows, moves, from_ref, to_ref):
@@ -500,7 +498,7 @@
         out_shape=(
             shape((half * size, MB), F32),
             shape((count, MB), BF16),
-            shape((2 * half * size + count, MB), BF16),
+            shape((half * size + count, MB), BF16),
         ),
         in_specs=[VMEM] * 11,
         out_specs=(VMEM,) * 3,
@@ -521,7 +519,7 @@
         table,
     )
 
-    wide = True
+    wide = False
     for step in range(steps - 2):
         got = lax.ppermute(packet, "cells", [(i, i ^ (1 << step)) for i in range(devices)])
         if step < steps - 3:

time: 31.3 us -> 31.1 us (level)
  no operation moved by 1% of the time
where the time goes in v9:
time: 31.1 us; the launch traced here: 30.9 us
  starting transfers between devices  13.9 us (45%)
  waiting for transfers between devices  8.28 us (27%)
  Pallas kernels  7.09 us (23%)
  local copies, waits for them, and re-layouts  0.83 us (3%)
  between operations  0.78 us (3%)
    ppermute x3, starting transfers between devices, shards(): lax.ppermute(packets[at - 1], 'cells', [(i, i ^ mask) for i in range(devi...  4.45 us
    ppermute x1, starting transfers between devices, shards(): low = lax.ppermute(to_low, 'cells', inner_pairs)  4.38 us
    ppermute x2, starting transfers between devices, shards(): lax.ppermute(packet, 'cells', [(i, i ^ 1 << step) for i in range(devices)])  4.31 us
    ppermute x2, waiting for transfers between devices, shards(): lax.ppermute(packet, 'cells', [(i, i ^ 1 << step) for i in range(devices)])  4.22 us
    ppermute x3, waiting for transfers between devices, shards(): lax.ppermute(packets[at - 1], 'cells', [(i, i ^ mask) for i in range(devi...  4.05 us
    pallas_call x1, Pallas kernels, shards(): pl.pallas_call(load_kernel, out_shape=(shape(basis.shape, BF16), shape((s...  1.62 us
    pallas_call x1, Pallas kernels, shards(): pl.pallas_call(functools.partial(local_kernel, (params, layers, width_y,...  1.55 us
    pallas_call x1, Pallas kernels, shards(): pl.pallas_call(functools.partial(pack_kernel, (params, layers)), out_shap...  1.16 us
  transfers between devices with their start and end apart: 8, of which 5 were waited for; matrix products, arithmetic and copies ran while one was open for 2% of the time, Pallas kernels for 13%

profile of v9, /device:TPU:0, one launch (start us, length us, event | category | flops | bytes accessed | tf_op | source)
XLA Modules:
  0.0 30.9 jit_solution(9608253407898566374)
XLA Ops:
  0.6 0.0 copy-start.6
  0.6 0.0 copy-start.5
  0.6 1.2 %pack_halo.1 = (bf16[76,8,128]{2,1,0:T(8,128)(2,1)S(1)}, bf16[64,8,128]{2,1,0:T(8,128)(2,1)S(1)}, bf16[140,8,128]{2,1,0:T(8,128)(2,1)S(1)}) custom-call(bf16[512,2,8,128]{3,2,1,0:T(8,128)(2,1)} %basis_ref.3, f32[2,3,2,8,128]{4,3,2,1,0:T(8,128)} %speed_ref.3, f32[2,3,2,8,128]{4,3,2,1,0:T(8,128)} %diff_ref.3, s32[2,3,2,8,128]{4,3,2,1,0:T(8,128)} %flag_ref.3), custom_call_target="tpu_custom_call" | custom-call | tf_op jit(solution)/shard_map/pack_halo/pallas_call | solution.py:393
  1.8 0.7 %collective-permute-start = (bf16[140,8,128]{2,1,0:T(8,128)(2,1)S(1)}, bf16[140,8,128]{2,1,0:T(8,128)(2,1)S(1)}, u32[]{:S(2)}, u32[]{:S(2)}) collective-permute-start(bf16[140,8,128]{2,1,0:T(8,128)(2,1)S(1)} %get-tuple-element.29.after_ref), channel_id=1, source_target_pairs={{1,2},{2,1},{3,4},{4,3},{5,6},{6,5},{7,8},{8,7},{9,10},{10,9},{11,... | collective-permute-start | bytes 860168 | tf_op jit(solution)/shard_map/ppermute | solution.py:417
  2.5 4.4 %collective-permute-start.1 = (bf16[76,8,128]{2,1,0:T(8,128)(2,1)S(1)}, bf16[76,8,128]{2,1,0:T(8,128)(2,1)S(1)}, u32[]{:S(2)}, u32[]{:S(2)}) collective-permute-start(bf16[76,8,128]{2,1,0:T(8,128)(2,1)S(1)} %get-tuple-element.37), channel_id=1, source_target_pairs={{0,1},{1,0},{2,3},{3,2},{4,5},{5,4},{6,7},{7,6},{8,9},{9,8},{10,11... | collective-permute-start | bytes 466952 | tf_op jit(solution)/shard_map/ppermute | solution.py:415
  6.9 0.1 collective-permute-start.2
  7.0 0.0 copy-done.6
  7.0 0.0 copy-done.5
  7.0 1.6 %load.1 = (bf16[512,2,8,128]{3,2,1,0:T(8,128)(2,1)S(1)}, s32[2,16]{1,0:T(2,128)S(1)}, s32[1,16]{1,0:T(1,128)S(1)}) custom-call(bf16[512,2,8,128]{3,2,1,0:T(8,128)(2,1)} %basis_ref.3, s32[2,16]{1,0:T(2,128)S(1)} %bitcast.18, s32[1,16]{1,0:T(1,128)S(1)} %copy-done.6, bf16[140,8,128]{2,1,0:T(8,128)(2,1)S(1)} %get-tuple-element.29.after_ref), custom_call_target="tpu_custom_call" | custom-call | tf_op jit(solution)/shard_map/load/pallas_call | solution.py:419
  8.6 0.0 copy-start
  8.6 0.0 copy-start.1
  8.6 0.0 copy-start.2
  8.6 0.0 copy-start.4
  8.6 0.5 %copy.12 = bf16[64,8,16,128]{3,1,2,0:T(8,128)(2,1)S(1)} copy(bf16[64,8,16,128]{3,2,1,0:T(8,128)(2,1)S(1)} %bitcast.17) | data formatting | bytes 4194304
  9.2 0.2 copy-done
  9.4 0.0 copy-done.1
  9.4 0.0 copy-done.2
  9.4 0.0 copy-done.4
  9.5 1.6 %local_stencil.1 = (f32[256,2048]{1,0:T(8,128)S(1)}, f32[2,8,128]{2,1,0:T(8,128)S(1)}, bf16[224,128]{1,0:T(8,128)(2,1)S(1)}, bf16[32,2048]{1,0:T(8,128)(2,1)S(1)}, s32[32,1]{1,0:T(8,128)S(1)}) custom-call(bf16[512,2048]{1,0:T(8,128)(2,1)S(1)} %bitcast.14, f32[2,3,2,8,128]{4,3,2,1,0:T(8,128)S(1)} %copy-done, f32[2,3,2,8,128]{4,3,2,1,0:T(8,128)S(1)} %copy-done.1, ...), custom_call_target="tpu_custom_call" | custom-call | flops 1 | bytes 1 | tf_op jit(solution)/shard_map/local_stencil/pallas_call | solution.py:448
  11.0 0.0 collective-permute-done.2.high_ref
  11.0 0.0 collective-permute-done.1.low_ref
  11.0 0.0 copy-start.3
  11.0 0.9 %near_layer.1 = (f32[512,256]{1,0:T(8,128)S(1)}, f32[32,256]{1,0:T(8,128)S(1)}, bf16[32,128]{1,0:T(8,128)(2,1)S(1)}) custom-call(bf16[512,2048]{1,0:T(8,128)(2,1)S(1)} %bitcast.15, bf16[76,8,128]{2,1,0:T(8,128)(2,1)S(1)} %collective-permute-done.1.low_ref, bf16[64,8,128]{2,1,0:T(8,128)(2,1)S(1)} %collective-permute-done.2.high_ref, ...), custom_call_target="tpu_custom_call" | custom-call | flops 1 | bytes 1 | tf_op jit(solution)/shard_map/near_layer/pallas_call | solution.py:474
  12.0 0.0 collective-permute-done.outer_ref
  12.0 0.0 copy-done.3
  12.0 1.0 %project.1 = (f32[512,128]{1,0:T(8,128)S(1)}, bf16[144,128]{1,0:T(8,128)(2,1)S(1)}, bf16[656,128]{1,0:T(8,128)(2,1)S(1)}) custom-call(bf16[512,2048]{1,0:T(8,128)(2,1)S(1)} %bitcast.16, bf16[140,8,128]{2,1,0:T(8,128)(2,1)S(1)} %collective-permute-done.outer_ref, f32[256,2048]{1,0:T(8,128)S(1)} %get-tuple-element.33.acc_ref, ...), custom_call_target="tpu_custom_call" | custom-call | tf_op jit(solution)/shard_map/project/pallas_call | solution.py:492
  13.0 1.5 %collective-permute-start.3 = (bf16[656,128]{1,0:T(8,128)(2,1)S(1)}, bf16[656,128]{1,0:T(8,128)(2,1)S(1)}, u32[]{:S(2)}, u32[]{:S(2)}) collective-permute-start(bf16[656,128]{1,0:T(8,128)(2,1)S(1)} %get-tuple-element.45), channel_id=1, source_target_pairs={{0,1},{1,0},{2,3},{3,2},{4,5},{5,4},{6,7},{7,6},{8,9},{9,8},{10,11... | collective-permute-start | bytes 503816 | tf_op jit(solution)/shard_map/ppermute | solution.py:524
  14.6 1.0 %collective-permute-done.3.got_ref = bf16[656,128]{1,0:T(8,128)(2,1)S(1)} collective-permute-done((bf16[656,128]{1,0:T(8,128)(2,1)S(1)}, bf16[656,128]{1,0:T(8,128)(2,1)S(1)}, u32[]{:S(2)}, u32[]{:S(2)}) %collective-permute-start.3) | collective-permute-done | bytes 167968 | tf_op jit(solution)/shard_map/ppermute | solution.py:524
  15.6 0.1 merge.1
  15.6 2.8 %collective-permute-start.4 = (bf16[400,128]{1,0:T(8,128)(2,1)S(1)}, bf16[400,128]{1,0:T(8,128)(2,1)S(1)}, u32[]{:S(2)}, u32[]{:S(2)}) collective-permute-start(bf16[400,128]{1,0:T(8,128)(2,1)S(1)} %get-tuple-element.48), channel_id=1, source_target_pairs={{0,2},{1,3},{2,0},{3,1},{4,6},{5,7},{6,4},{7,5},{8,10},{9,11},{10,... | collective-permute-start | bytes 307208 | tf_op jit(solution)/shard_map/ppermute | solution.py:524
  18.4 3.2 %collective-permute-done.4.got_ref = bf16[400,128]{1,0:T(8,128)(2,1)S(1)} collective-permute-done((bf16[400,128]{1,0:T(8,128)(2,1)S(1)}, bf16[400,128]{1,0:T(8,128)(2,1)S(1)}, u32[]{:S(2)}, u32[]{:S(2)}) %collective-permute-start.4) | collective-permute-done | bytes 102432 | tf_op jit(solution)/shard_map/ppermute | solution.py:524
  21.7 3.6 %collective-permute-start.5 = (bf16[144,128]{1,0:T(8,128)(2,1)S(1)}, bf16[144,128]{1,0:T(8,128)(2,1)S(1)}, u32[]{:S(2)}, u32[]{:S(2)}) collective-permute-start(bf16[144,128]{1,0:T(8,128)(2,1)S(1)} %get-tuple-element.51), channel_id=1, source_target_pairs={{0,12},{1,13},{2,14},{3,15},{4,8},{5,9},{6,10},{7,11},{8,4},{9,5},... | collective-permute-start | bytes 110600 | tf_op jit(solution)/shard_map/ppermute | solution.py:556
  25.3 0.0 collective-permute-start.6
  25.3 0.8 %collective-permute-start.7 = (bf16[144,128]{1,0:T(8,128)(2,1)S(1)}, bf16[144,128]{1,0:T(8,128)(2,1)S(1)}, u32[]{:S(2)}, u32[]{:S(2)}) collective-permute-start(bf16[144,128]{1,0:T(8,128)(2,1)S(1)} %get-tuple-element.53), channel_id=1, source_target_pairs={{0,8},{1,9},{2,10},{3,11},{4,12},{5,13},{6,14},{7,15},{8,0},{9,1},... | collective-permute-start | bytes 110600 | tf_op jit(solution)/shard_map/ppermute | solution.py:556
  26.1 1.4 %collective-permute-done.5.refs_0_ = bf16[144,128]{1,0:T(8,128)(2,1)S(1)} collective-permute-done((bf16[144,128]{1,0:T(8,128)(2,1)S(1)}, bf16[144,128]{1,0:T(8,128)(2,1)S(1)}, u32[]{:S(2)}, u32[]{:S(2)}) %collective-permute-start.5) | collective-permute-done | bytes 36896 | tf_op jit(solution)/shard_map/ppermute | solution.py:556
  27.5 1.7 %collective-permute-done.6.refs_1_ = bf16[144,128]{1,0:T(8,128)(2,1)S(1)} collective-permute-done((bf16[144,128]{1,0:T(8,128)(2,1)S(1)}, bf16[144,128]{1,0:T(8,128)(2,1)S(1)}, u32[]{:S(2)}, u32[]{:S(2)}) %collective-permute-start.6) | collective-permute-done | bytes 36896 | tf_op jit(solution)/shard_map/ppermute | solution.py:556
  29.3 0.9 %collective-permute-done.7.refs_2_ = bf16[144,128]{1,0:T(8,128)(2,1)S(1)} collective-permute-done((bf16[144,128]{1,0:T(8,128)(2,1)S(1)}, bf16[144,128]{1,0:T(8,128)(2,1)S(1)}, u32[]{:S(2)}, u32[]{:S(2)}) %collective-permute-start.7) | collective-permute-done | bytes 36896 | tf_op jit(solution)/shard_map/ppermute | solution.py:556
  30.2 0.7 %finish.1 = (f32[64,128]{1,0:T(8,128)}, bf16[288,128]{1,0:T(8,128)(2,1)}) custom-call(f32[64,128]{1,0:T(8,128)S(1)} %get-tuple-element.49.keep_ref, bf16[80,128]{1,0:T(8,128)(2,1)S(1)} %get-tuple-element.50.keep_rows_ref, bf16[144,128]{1,0:T(8,128)(2,1)S(1)} %collective-permute-done.5.refs_0_, bf16[144,128]{1,0:T(8,128)(2,1)S(1)} %collective-permute-done.6.refs_1_, ...), custom_call_target="tpu_custom_call" | custom-call | tf_op jit(solution)/shard_map/finish/pallas_call | solution.py:558
  (1 shorter events, 0.0 us)
Async XLA Ops:
  0.6 6.3 %copy-start.6 = (s32[1,16]{1,0:T(1,128)S(1)}, s32[1,16]{1,0:T(1,128)}, u32[]{:S(2)}) copy-start(s32[1,16]{1,0:T(1,128)} %count_ref.1) | copy-start | bytes 196
  0.6 6.3 %copy-start.5 = (s32[1,16,2]{1,2,0:T(2,128)S(1)}, s32[1,16,2]{1,2,0:T(2,128)}, u32[]{:S(2)}) copy-start(s32[1,16,2]{1,2,0:T(2,128)} %param.13) | copy-start | bytes 388
  1.8 10.2 %collective-permute-start = (bf16[140,8,128]{2,1,0:T(8,128)(2,1)S(1)}, bf16[140,8,128]{2,1,0:T(8,128)(2,1)S(1)}, u32[]{:S(2)}, u32[]{:S(2)}) collective-permute-start(bf16[140,8,128]{2,1,0:T(8,128)(2,1)S(1)} %get-tuple-element.29.after_ref), channel_id=1, source_target_pairs={{1,2},{2,1},{3,4},{4,3},{5,6},{6,5},{7,8},{8,7},{9,10},{10,9},{11,... | collective-permute-start | bytes 860168 | tf_op jit(solution)/shard_map/ppermute | solution.py:417
  2.5 8.5 %collective-permute-start.1 = (bf16[76,8,128]{2,1,0:T(8,128)(2,1)S(1)}, bf16[76,8,128]{2,1,0:T(8,128)(2,1)S(1)}, u32[]{:S(2)}, u32[]{:S(2)}) collective-permute-start(bf16[76,8,128]{2,1,0:T(8,128)(2,1)S(1)} %get-tuple-element.37), channel_id=1, source_target_pairs={{0,1},{1,0},{2,3},{3,2},{4,5},{5,4},{6,7},{7,6},{8,9},{9,8},{10,11... | collective-permute-start | bytes 466952 | tf_op jit(solution)/shard_map/ppermute | solution.py:415
  6.9 4.1 %collective-permute-start.2 = (bf16[64,8,128]{2,1,0:T(8,128)(2,1)S(1)}, bf16[64,8,128]{2,1,0:T(8,128)(2,1)S(1)}, u32[]{:S(2)}, u32[]{:S(2)}) collective-permute-start(bf16[64,8,128]{2,1,0:T(8,128)(2,1)S(1)} %get-tuple-element.38), channel_id=1, source_target_pairs={{0,1},{1,0},{2,3},{3,2},{4,5},{5,4},{6,7},{7,6},{8,9},{9,8},{10,11... | collective-permute-start | bytes 393224 | tf_op jit(solution)/shard_map/ppermute | solution.py:416
  8.6 0.8 %copy-start = (f32[2,3,2,8,128]{4,3,2,1,0:T(8,128)S(1)}, f32[2,3,2,8,128]{4,3,2,1,0:T(8,128)}, u32[]{:S(2)}) copy-start(f32[2,3,2,8,128]{4,3,2,1,0:T(8,128)} %speed_ref.3) | copy-start | bytes 147460
  8.6 0.8 %copy-start.1 = (f32[2,3,2,8,128]{4,3,2,1,0:T(8,128)S(1)}, f32[2,3,2,8,128]{4,3,2,1,0:T(8,128)}, u32[]{:S(2)}) copy-start(f32[2,3,2,8,128]{4,3,2,1,0:T(8,128)} %diff_ref.3) | copy-start | bytes 147460
  8.6 0.8 %copy-start.2 = (s32[2,3,2,8,128]{4,3,2,1,0:T(8,128)S(1)}, s32[2,3,2,8,128]{4,3,2,1,0:T(8,128)}, u32[]{:S(2)}) copy-start(s32[2,3,2,8,128]{4,3,2,1,0:T(8,128)} %flag_ref.3) | copy-start | bytes 147460
  8.6 0.8 %copy-start.4 = (f32[2,2,8,128]{3,2,1,0:T(8,128)S(1)}, f32[2,2,8,128]{3,2,1,0:T(8,128)}, u32[]{:S(2)}) copy-start(f32[2,2,8,128]{3,2,1,0:T(8,128)} %react_ref.1) | copy-start | bytes 49156
  11.0 1.0 %copy-start.3 = (s32[288,8]{1,0:T(8,128)S(1)}, s32[288,8]{1,0:T(8,128)}, u32[]{:S(2)}) copy-start(s32[288,8]{1,0:T(8,128)} %constant.2.clone.table_ref) | copy-start | bytes 27652
  13.0 2.5 %collective-permute-start.3 = (bf16[656,128]{1,0:T(8,128)(2,1)S(1)}, bf16[656,128]{1,0:T(8,128)(2,1)S(1)}, u32[]{:S(2)}, u32[]{:S(2)}) collective-permute-start(bf16[656,128]{1,0:T(8,128)(2,1)S(1)} %get-tuple-element.45), channel_id=1, source_target_pairs={{0,1},{1,0},{2,3},{3,2},{4,5},{5,4},{6,7},{7,6},{8,9},{9,8},{10,11... | collective-permute-start | bytes 503816 | tf_op jit(solution)/shard_map/ppermute | solution.py:524
  15.6 6.0 %collective-permute-start.4 = (bf16[400,128]{1,0:T(8,128)(2,1)S(1)}, bf16[400,128]{1,0:T(8,128)(2,1)S(1)}, u32[]{:S(2)}, u32[]{:S(2)}) collective-permute-start(bf16[400,128]{1,0:T(8,128)(2,1)S(1)} %get-tuple-element.48), channel_id=1, source_target_pairs={{0,2},{1,3},{2,0},{3,1},{4,6},{5,7},{6,4},{7,5},{8,10},{9,11},{10,... | collective-permute-start | bytes 307208 | tf_op jit(solution)/shard_map/ppermute | solution.py:524
  21.7 5.9 %collective-permute-start.5 = (bf16[144,128]{1,0:T(8,128)(2,1)S(1)}, bf16[144,128]{1,0:T(8,128)(2,1)S(1)}, u32[]{:S(2)}, u32[]{:S(2)}) collective-permute-start(bf16[144,128]{1,0:T(8,128)(2,1)S(1)} %get-tuple-element.51), channel_id=1, source_target_pairs={{0,12},{1,13},{2,14},{3,15},{4,8},{5,9},{6,10},{7,11},{8,4},{9,5},... | collective-permute-start | bytes 110600 | tf_op jit(solution)/shard_map/ppermute | solution.py:556
  25.3 4.0 %collective-permute-start.6 = (bf16[144,128]{1,0:T(8,128)(2,1)S(1)}, bf16[144,128]{1,0:T(8,128)(2,1)S(1)}, u32[]{:S(2)}, u32[]{:S(2)}) collective-permute-start(bf16[144,128]{1,0:T(8,128)(2,1)S(1)} %get-tuple-element.52), channel_id=1, source_target_pairs={{0,4},{1,5},{2,6},{3,7},{4,0},{5,1},{6,2},{7,3},{8,12},{9,13},{10,... | collective-permute-start | bytes 110600 | tf_op jit(solution)/shard_map/ppermute | solution.py:556
  25.3 4.9 %collective-permute-start.7 = (bf16[144,128]{1,0:T(8,128)(2,1)S(1)}, bf16[144,128]{1,0:T(8,128)(2,1)S(1)}, u32[]{:S(2)}, u32[]{:S(2)}) collective-permute-start(bf16[144,128]{1,0:T(8,128)(2,1)S(1)} %get-tuple-element.53), channel_id=1, source_target_pairs={{0,8},{1,9},{2,10},{3,11},{4,12},{5,13},{6,14},{7,15},{8,0},{9,1},... | collective-permute-start | bytes 110600 | tf_op jit(solution)/shard_map/ppermute | solution.py:556

commit v10 on v9

--- a/solution.py
+++ b/solution.py
@@ -9,7 +9,7 @@
 from jax.sharding import PartitionSpec as P
 
 MB = 128
-SPLITS = 3
+SPLITS = 2
 NARROW_STEPS = 1
 DIRECT = 4
 ORDER = (3, 2, 1)
@@ -206,8 +206,8 @@
     for at in range(2 * SPLITS):
         part = halo_refs[0][held + at * params : held + (at + 1) * params].astype(F32)
         faces.append(part.reshape(params * width_y, width_z))
-    signed = faces[0] + faces[1] + faces[2]
-    diff = faces[3] + faces[4] + faces[5]
+    signed = faces[0] + faces[1]
+    diff = faces[2] + faces[3]
     edge = edge_ref[...].reshape(params * width_y, width_z)
     coef_ref[0] = jnp.where(from_next, edge, -(jnp.maximum(signed, 0.0) + diff))
     coef_ref[1] = jnp.where(from_next, 0.0, diff - jnp.minimum(signed, 0.0))

time: 31.1 us -> 30.9 us (level)
  no operation moved by 1% of the time
where the time goes in v10:
time: 30.9 us; the launch traced here: 30.7 us
  starting transfers between devices  13.8 us (45%)
  waiting for transfers between devices  8.28 us (27%)
  Pallas kernels  7.02 us (23%)
  local copies, waits for them, and re-layouts  0.83 us (3%)
  between operations  0.78 us (3%)
    ppermute x3, starting transfers between devices, shards(): lax.ppermute(packets[at - 1], 'cells', [(i, i ^ mask) for i in range(devi...  4.45 us
    ppermute x1, starting transfers between devices, shards(): low = lax.ppermute(to_low, 'cells', inner_pairs)  4.38 us
    ppermute x2, waiting for transfers between devices, shards(): lax.ppermute(packet, 'cells', [(i, i ^ 1 << step) for i in range(devices)])  4.22 us
    ppermute x2, starting transfers between devices, shards(): lax.ppermute(packet, 'cells', [(i, i ^ 1 << step) for i in range(devices)])  4.18 us
    ppermute x3, waiting for transfers between devices, shards(): lax.ppermute(packets[at - 1], 'cells', [(i, i ^ mask) for i in range(devi...  4.05 us
    pallas_call x1, Pallas kernels, shards(): pl.pallas_call(load_kernel, out_shape=(shape(basis.shape, BF16), shape((s...  1.62 us
    pallas_call x1, Pallas kernels, shards(): pl.pallas_call(functools.partial(local_kernel, (params, layers, width_y,...  1.52 us
    pallas_call x1, Pallas kernels, shards(): pl.pallas_call(functools.partial(pack_kernel, (params, layers)), out_shap...  1.16 us
  transfers between devices with their start and end apart: 8, of which 5 were waited for; matrix products, arithmetic and copies ran while one was open for 2% of the time, Pallas kernels for 13%

profile of v10, /device:TPU:0, one launch (start us, length us, event | category | flops | bytes accessed | tf_op | source)
XLA Modules:
  0.0 30.7 jit_solution(9892645152322410802)
XLA Ops:
  0.6 0.0 copy-start.6
  0.6 0.0 copy-start.5
  0.6 1.2 %pack_halo.1 = (bf16[72,8,128]{2,1,0:T(8,128)(2,1)S(1)}, bf16[64,8,128]{2,1,0:T(8,128)(2,1)S(1)}, bf16[136,8,128]{2,1,0:T(8,128)(2,1)S(1)}) custom-call(bf16[512,2,8,128]{3,2,1,0:T(8,128)(2,1)} %basis_ref.3, f32[2,3,2,8,128]{4,3,2,1,0:T(8,128)} %speed_ref.3, f32[2,3,2,8,128]{4,3,2,1,0:T(8,128)} %diff_ref.3, s32[2,3,2,8,128]{4,3,2,1,0:T(8,128)} %flag_ref.3), custom_call_target="tpu_custom_call" | custom-call | tf_op jit(solution)/shard_map/pack_halo/pallas_call | solution.py:393
  1.8 0.7 %collective-permute-start = (bf16[136,8,128]{2,1,0:T(8,128)(2,1)S(1)}, bf16[136,8,128]{2,1,0:T(8,128)(2,1)S(1)}, u32[]{:S(2)}, u32[]{:S(2)}) collective-permute-start(bf16[136,8,128]{2,1,0:T(8,128)(2,1)S(1)} %get-tuple-element.29.after_ref), channel_id=1, source_target_pairs={{1,2},{2,1},{3,4},{4,3},{5,6},{6,5},{7,8},{8,7},{9,10},{10,9},{11,... | collective-permute-start | bytes 835592 | tf_op jit(solution)/shard_map/ppermute | solution.py:417
  2.5 4.4 %collective-permute-start.1 = (bf16[72,8,128]{2,1,0:T(8,128)(2,1)S(1)}, bf16[72,8,128]{2,1,0:T(8,128)(2,1)S(1)}, u32[]{:S(2)}, u32[]{:S(2)}) collective-permute-start(bf16[72,8,128]{2,1,0:T(8,128)(2,1)S(1)} %get-tuple-element.37), channel_id=1, source_target_pairs={{0,1},{1,0},{2,3},{3,2},{4,5},{5,4},{6,7},{7,6},{8,9},{9,8},{10,11... | collective-permute-start | bytes 442376 | tf_op jit(solution)/shard_map/ppermute | solution.py:415
  6.9 0.1 collective-permute-start.2
  7.0 0.0 copy-done.6
  7.0 0.0 copy-done.5
  7.0 1.6 %load.1 = (bf16[512,2,8,128]{3,2,1,0:T(8,128)(2,1)S(1)}, s32[2,16]{1,0:T(2,128)S(1)}, s32[1,16]{1,0:T(1,128)S(1)}) custom-call(bf16[512,2,8,128]{3,2,1,0:T(8,128)(2,1)} %basis_ref.3, s32[2,16]{1,0:T(2,128)S(1)} %bitcast.18, s32[1,16]{1,0:T(1,128)S(1)} %copy-done.6, bf16[136,8,128]{2,1,0:T(8,128)(2,1)S(1)} %get-tuple-element.29.after_ref), custom_call_target="tpu_custom_call" | custom-call | tf_op jit(solution)/shard_map/load/pallas_call | solution.py:419
  8.6 0.0 copy-start
  8.6 0.0 copy-start.1
  8.6 0.0 copy-start.2
  8.6 0.0 copy-start.4
  8.6 0.5 %copy.12 = bf16[64,8,16,128]{3,1,2,0:T(8,128)(2,1)S(1)} copy(bf16[64,8,16,128]{3,2,1,0:T(8,128)(2,1)S(1)} %bitcast.17) | data formatting | bytes 4194304
  9.2 0.2 copy-done
  9.4 0.0 copy-done.1
  9.4 0.0 copy-done.2
  9.4 0.0 copy-done.4
  9.5 1.5 %local_stencil.1 = (f32[256,2048]{1,0:T(8,128)S(1)}, f32[2,8,128]{2,1,0:T(8,128)S(1)}, bf16[224,128]{1,0:T(8,128)(2,1)S(1)}, bf16[32,2048]{1,0:T(8,128)(2,1)S(1)}, s32[32,1]{1,0:T(8,128)S(1)}) custom-call(bf16[512,2048]{1,0:T(8,128)(2,1)S(1)} %bitcast.14, f32[2,3,2,8,128]{4,3,2,1,0:T(8,128)S(1)} %copy-done, f32[2,3,2,8,128]{4,3,2,1,0:T(8,128)S(1)} %copy-done.1, ...), custom_call_target="tpu_custom_call" | custom-call | flops 1 | bytes 1 | tf_op jit(solution)/shard_map/local_stencil/pallas_call | solution.py:448
  11.0 0.0 collective-permute-done.2.high_ref
  11.0 0.0 collective-permute-done.1.low_ref
  11.0 0.0 copy-start.3
  11.0 0.9 %near_layer.1 = (f32[512,256]{1,0:T(8,128)S(1)}, f32[32,256]{1,0:T(8,128)S(1)}, bf16[32,128]{1,0:T(8,128)(2,1)S(1)}) custom-call(bf16[512,2048]{1,0:T(8,128)(2,1)S(1)} %bitcast.15, bf16[72,8,128]{2,1,0:T(8,128)(2,1)S(1)} %collective-permute-done.1.low_ref, bf16[64,8,128]{2,1,0:T(8,128)(2,1)S(1)} %collective-permute-done.2.high_ref, ...), custom_call_target="tpu_custom_call" | custom-call | flops 1 | bytes 1 | tf_op jit(solution)/shard_map/near_layer/pallas_call | solution.py:474
  11.9 0.0 collective-permute-done.outer_ref
  11.9 0.0 copy-done.3
  12.0 1.0 %project.1 = (f32[512,128]{1,0:T(8,128)S(1)}, bf16[144,128]{1,0:T(8,128)(2,1)S(1)}, bf16[656,128]{1,0:T(8,128)(2,1)S(1)}) custom-call(bf16[512,2048]{1,0:T(8,128)(2,1)S(1)} %bitcast.16, bf16[136,8,128]{2,1,0:T(8,128)(2,1)S(1)} %collective-permute-done.outer_ref, f32[256,2048]{1,0:T(8,128)S(1)} %get-tuple-element.33.acc_ref, ...), custom_call_target="tpu_custom_call" | custom-call | tf_op jit(solution)/shard_map/project/pallas_call | solution.py:492
  13.0 1.4 %collective-permute-start.3 = (bf16[656,128]{1,0:T(8,128)(2,1)S(1)}, bf16[656,128]{1,0:T(8,128)(2,1)S(1)}, u32[]{:S(2)}, u32[]{:S(2)}) collective-permute-start(bf16[656,128]{1,0:T(8,128)(2,1)S(1)} %get-tuple-element.45), channel_id=1, source_target_pairs={{0,1},{1,0},{2,3},{3,2},{4,5},{5,4},{6,7},{7,6},{8,9},{9,8},{10,11... | collective-permute-start | bytes 503816 | tf_op jit(solution)/shard_map/ppermute | solution.py:524
  14.4 1.0 %collective-permute-done.3.got_ref = bf16[656,128]{1,0:T(8,128)(2,1)S(1)} collective-permute-done((bf16[656,128]{1,0:T(8,128)(2,1)S(1)}, bf16[656,128]{1,0:T(8,128)(2,1)S(1)}, u32[]{:S(2)}, u32[]{:S(2)}) %collective-permute-start.3) | collective-permute-done | bytes 167968 | tf_op jit(solution)/shard_map/ppermute | solution.py:524
  15.4 0.1 merge.1
  15.5 2.8 %collective-permute-start.4 = (bf16[400,128]{1,0:T(8,128)(2,1)S(1)}, bf16[400,128]{1,0:T(8,128)(2,1)S(1)}, u32[]{:S(2)}, u32[]{:S(2)}) collective-permute-start(bf16[400,128]{1,0:T(8,128)(2,1)S(1)} %get-tuple-element.48), channel_id=1, source_target_pairs={{0,2},{1,3},{2,0},{3,1},{4,6},{5,7},{6,4},{7,5},{8,10},{9,11},{10,... | collective-permute-start | bytes 307208 | tf_op jit(solution)/shard_map/ppermute | solution.py:524
  18.3 3.2 %collective-permute-done.4.got_ref = bf16[400,128]{1,0:T(8,128)(2,1)S(1)} collective-permute-done((bf16[400,128]{1,0:T(8,128)(2,1)S(1)}, bf16[400,128]{1,0:T(8,128)(2,1)S(1)}, u32[]{:S(2)}, u32[]{:S(2)}) %collective-permute-start.4) | collective-permute-done | bytes 102432 | tf_op jit(solution)/shard_map/ppermute | solution.py:524
  21.5 3.6 %collective-permute-start.5 = (bf16[144,128]{1,0:T(8,128)(2,1)S(1)}, bf16[144,128]{1,0:T(8,128)(2,1)S(1)}, u32[]{:S(2)}, u32[]{:S(2)}) collective-permute-start(bf16[144,128]{1,0:T(8,128)(2,1)S(1)} %get-tuple-element.51), channel_id=1, source_target_pairs={{0,12},{1,13},{2,14},{3,15},{4,8},{5,9},{6,10},{7,11},{8,4},{9,5},... | collective-permute-start | bytes 110600 | tf_op jit(solution)/shard_map/ppermute | solution.py:556
  25.1 0.0 collective-permute-start.6
  25.1 0.8 %collective-permute-start.7 = (bf16[144,128]{1,0:T(8,128)(2,1)S(1)}, bf16[144,128]{1,0:T(8,128)(2,1)S(1)}, u32[]{:S(2)}, u32[]{:S(2)}) collective-permute-start(bf16[144,128]{1,0:T(8,128)(2,1)S(1)} %get-tuple-element.53), channel_id=1, source_target_pairs={{0,8},{1,9},{2,10},{3,11},{4,12},{5,13},{6,14},{7,15},{8,0},{9,1},... | collective-permute-start | bytes 110600 | tf_op jit(solution)/shard_map/ppermute | solution.py:556
  25.9 1.4 %collective-permute-done.5.refs_0_ = bf16[144,128]{1,0:T(8,128)(2,1)S(1)} collective-permute-done((bf16[144,128]{1,0:T(8,128)(2,1)S(1)}, bf16[144,128]{1,0:T(8,128)(2,1)S(1)}, u32[]{:S(2)}, u32[]{:S(2)}) %collective-permute-start.5) | collective-permute-done | bytes 36896 | tf_op jit(solution)/shard_map/ppermute | solution.py:556
  27.3 1.7 %collective-permute-done.6.refs_1_ = bf16[144,128]{1,0:T(8,128)(2,1)S(1)} collective-permute-done((bf16[144,128]{1,0:T(8,128)(2,1)S(1)}, bf16[144,128]{1,0:T(8,128)(2,1)S(1)}, u32[]{:S(2)}, u32[]{:S(2)}) %collective-permute-start.6) | collective-permute-done | bytes 36896 | tf_op jit(solution)/shard_map/ppermute | solution.py:556
  29.1 0.9 %collective-permute-done.7.refs_2_ = bf16[144,128]{1,0:T(8,128)(2,1)S(1)} collective-permute-done((bf16[144,128]{1,0:T(8,128)(2,1)S(1)}, bf16[144,128]{1,0:T(8,128)(2,1)S(1)}, u32[]{:S(2)}, u32[]{:S(2)}) %collective-permute-start.7) | collective-permute-done | bytes 36896 | tf_op jit(solution)/shard_map/ppermute | solution.py:556
  30.0 0.7 %finish.1 = (f32[64,128]{1,0:T(8,128)}, bf16[288,128]{1,0:T(8,128)(2,1)}) custom-call(f32[64,128]{1,0:T(8,128)S(1)} %get-tuple-element.49.keep_ref, bf16[80,128]{1,0:T(8,128)(2,1)S(1)} %get-tuple-element.50.keep_rows_ref, bf16[144,128]{1,0:T(8,128)(2,1)S(1)} %collective-permute-done.5.refs_0_, bf16[144,128]{1,0:T(8,128)(2,1)S(1)} %collective-permute-done.6.refs_1_, ...), custom_call_target="tpu_custom_call" | custom-call | tf_op jit(solution)/shard_map/finish/pallas_call | solution.py:558
  (1 shorter events, 0.0 us)
Async XLA Ops:
  0.6 6.3 %copy-start.6 = (s32[1,16]{1,0:T(1,128)S(1)}, s32[1,16]{1,0:T(1,128)}, u32[]{:S(2)}) copy-start(s32[1,16]{1,0:T(1,128)} %count_ref.1) | copy-start | bytes 196
  0.6 6.3 %copy-start.5 = (s32[1,16,2]{1,2,0:T(2,128)S(1)}, s32[1,16,2]{1,2,0:T(2,128)}, u32[]{:S(2)}) copy-start(s32[1,16,2]{1,2,0:T(2,128)} %param.13) | copy-start | bytes 388
  1.8 10.1 %collective-permute-start = (bf16[136,8,128]{2,1,0:T(8,128)(2,1)S(1)}, bf16[136,8,128]{2,1,0:T(8,128)(2,1)S(1)}, u32[]{:S(2)}, u32[]{:S(2)}) collective-permute-start(bf16[136,8,128]{2,1,0:T(8,128)(2,1)S(1)} %get-tuple-element.29.after_ref), channel_id=1, source_target_pairs={{1,2},{2,1},{3,4},{4,3},{5,6},{6,5},{7,8},{8,7},{9,10},{10,9},{11,... | collective-permute-start | bytes 835592 | tf_op jit(solution)/shard_map/ppermute | solution.py:417
  2.5 8.5 %collective-permute-start.1 = (bf16[72,8,128]{2,1,0:T(8,128)(2,1)S(1)}, bf16[72,8,128]{2,1,0:T(8,128)(2,1)S(1)}, u32[]{:S(2)}, u32[]{:S(2)}) collective-permute-start(bf16[72,8,128]{2,1,0:T(8,128)(2,1)S(1)} %get-tuple-element.37), channel_id=1, source_target_pairs={{0,1},{1,0},{2,3},{3,2},{4,5},{5,4},{6,7},{7,6},{8,9},{9,8},{10,11... | collective-permute-start | bytes 442376 | tf_op jit(solution)/shard_map/ppermute | solution.py:415
  6.9 4.1 %collective-permute-start.2 = (bf16[64,8,128]{2,1,0:T(8,128)(2,1)S(1)}, bf16[64,8,128]{2,1,0:T(8,128)(2,1)S(1)}, u32[]{:S(2)}, u32[]{:S(2)}) collective-permute-start(bf16[64,8,128]{2,1,0:T(8,128)(2,1)S(1)} %get-tuple-element.38), channel_id=1, source_target_pairs={{0,1},{1,0},{2,3},{3,2},{4,5},{5,4},{6,7},{7,6},{8,9},{9,8},{10,11... | collective-permute-start | bytes 393224 | tf_op jit(solution)/shard_map/ppermute | solution.py:416
  8.6 0.8 %copy-start = (f32[2,3,2,8,128]{4,3,2,1,0:T(8,128)S(1)}, f32[2,3,2,8,128]{4,3,2,1,0:T(8,128)}, u32[]{:S(2)}) copy-start(f32[2,3,2,8,128]{4,3,2,1,0:T(8,128)} %speed_ref.3) | copy-start | bytes 147460
  8.6 0.8 %copy-start.1 = (f32[2,3,2,8,128]{4,3,2,1,0:T(8,128)S(1)}, f32[2,3,2,8,128]{4,3,2,1,0:T(8,128)}, u32[]{:S(2)}) copy-start(f32[2,3,2,8,128]{4,3,2,1,0:T(8,128)} %diff_ref.3) | copy-start | bytes 147460
  8.6 0.8 %copy-start.2 = (s32[2,3,2,8,128]{4,3,2,1,0:T(8,128)S(1)}, s32[2,3,2,8,128]{4,3,2,1,0:T(8,128)}, u32[]{:S(2)}) copy-start(s32[2,3,2,8,128]{4,3,2,1,0:T(8,128)} %flag_ref.3) | copy-start | bytes 147460
  8.6 0.8 %copy-start.4 = (f32[2,2,8,128]{3,2,1,0:T(8,128)S(1)}, f32[2,2,8,128]{3,2,1,0:T(8,128)}, u32[]{:S(2)}) copy-start(f32[2,2,8,128]{3,2,1,0:T(8,128)} %react_ref.1) | copy-start | bytes 49156
  11.0 0.9 %copy-start.3 = (s32[288,8]{1,0:T(8,128)S(1)}, s32[288,8]{1,0:T(8,128)}, u32[]{:S(2)}) copy-start(s32[288,8]{1,0:T(8,128)} %constant.2.clone.table_ref) | copy-start | bytes 27652
  13.0 2.4 %collective-permute-start.3 = (bf16[656,128]{1,0:T(8,128)(2,1)S(1)}, bf16[656,128]{1,0:T(8,128)(2,1)S(1)}, u32[]{:S(2)}, u32[]{:S(2)}) collective-permute-start(bf16[656,128]{1,0:T(8,128)(2,1)S(1)} %get-tuple-element.45), channel_id=1, source_target_pairs={{0,1},{1,0},{2,3},{3,2},{4,5},{5,4},{6,7},{7,6},{8,9},{9,8},{10,11... | collective-permute-start | bytes 503816 | tf_op jit(solution)/shard_map/ppermute | solution.py:524
  15.5 6.0 %collective-permute-start.4 = (bf16[400,128]{1,0:T(8,128)(2,1)S(1)}, bf16[400,128]{1,0:T(8,128)(2,1)S(1)}, u32[]{:S(2)}, u32[]{:S(2)}) collective-permute-start(bf16[400,128]{1,0:T(8,128)(2,1)S(1)} %get-tuple-element.48), channel_id=1, source_target_pairs={{0,2},{1,3},{2,0},{3,1},{4,6},{5,7},{6,4},{7,5},{8,10},{9,11},{10,... | collective-permute-start | bytes 307208 | tf_op jit(solution)/shard_map/ppermute | solution.py:524
  21.5 5.9 %collective-permute-start.5 = (bf16[144,128]{1,0:T(8,128)(2,1)S(1)}, bf16[144,128]{1,0:T(8,128)(2,1)S(1)}, u32[]{:S(2)}, u32[]{:S(2)}) collective-permute-start(bf16[144,128]{1,0:T(8,128)(2,1)S(1)} %get-tuple-element.51), channel_id=1, source_target_pairs={{0,12},{1,13},{2,14},{3,15},{4,8},{5,9},{6,10},{7,11},{8,4},{9,5},... | collective-permute-start | bytes 110600 | tf_op jit(solution)/shard_map/ppermute | solution.py:556
  25.1 4.0 %collective-permute-start.6 = (bf16[144,128]{1,0:T(8,128)(2,1)S(1)}, bf16[144,128]{1,0:T(8,128)(2,1)S(1)}, u32[]{:S(2)}, u32[]{:S(2)}) collective-permute-start(bf16[144,128]{1,0:T(8,128)(2,1)S(1)} %get-tuple-element.52), channel_id=1, source_target_pairs={{0,4},{1,5},{2,6},{3,7},{4,0},{5,1},{6,2},{7,3},{8,12},{9,13},{10,... | collective-permute-start | bytes 110600 | tf_op jit(solution)/shard_map/ppermute | solution.py:556
  25.1 4.9 %collective-permute-start.7 = (bf16[144,128]{1,0:T(8,128)(2,1)S(1)}, bf16[144,128]{1,0:T(8,128)(2,1)S(1)}, u32[]{:S(2)}, u32[]{:S(2)}) collective-permute-start(bf16[144,128]{1,0:T(8,128)(2,1)S(1)} %get-tuple-element.53), channel_id=1, source_target_pairs={{0,8},{1,9},{2,10},{3,11},{4,12},{5,13},{6,14},{7,15},{8,0},{9,1},... | collective-permute-start | bytes 110600 | tf_op jit(solution)/shard_map/ppermute | solution.py:556

commit v11 on v10

--- a/solution.py
+++ b/solution.py
@@ -62,40 +62,40 @@
     return parts
 
 
-def pack_kernel(dims, basis_ref, speed_ref, diff_ref, flag_ref, low_ref, high_ref, outer_ref, speed_buf, diff_buf, flag_buf, sems):
+def pack_kernel(dims, basis_ref, speed_ref, diff_ref, flag_ref, outer_ref, speed_buf, diff_buf, flag_buf, sems):
     params, layers = dims
     last = layers - 1
-    half = MB // 2
     block = pl.ds(0, MB)
-    low, high = pl.ds(0, half), pl.ds(half, half)
-    beside = (1 - core()) * last
-    layers_out = [
-        pltpu.make_async_copy(basis_ref.at[block, core() * last], outer_ref.at[block], sems.at[0]),
-        pltpu.make_async_copy(basis_ref.at[low, beside], low_ref.at[low], sems.at[1]),
-        pltpu.make_async_copy(basis_ref.at[high, beside], high_ref, sems.at[5]),
+    outer = pltpu.make_async_copy(basis_ref.at[block, core() * last], outer_ref.at[block], sems.at[0])
+    copies = [
+        pltpu.make_async_copy(speed_ref.at[:, 0, last], speed_buf, sems.at[1]),
+        pltpu.make_async_copy(diff_ref.at[:, 0, last], diff_buf, sems.at[2]),
+        pltpu.make_async_copy(flag_ref.at[:, 0, last], flag_buf, sems.at[3]),
     ]
-    copies = [
-        pltpu.make_async_copy(speed_ref.at[:, 0, last], speed_buf, sems.at[2]),
-        pltpu.make_async_copy(diff_ref.at[:, 0, last], diff_buf, sems.at[3]),
-        pltpu.make_async_copy(flag_ref.at[:, 0, last], flag_buf, sems.at[4]),
-    ]
-    for copy in copies + layers_out:
+    for copy in copies + [outer]:
         copy.start()
     for copy in copies:
         copy.wait()
     for at, part in enumerate(face_parts(speed_buf[...], diff_buf[...], flag_buf[...])):
-        low_ref[half + at * params : half + (at + 1) * params] = part
         outer_ref[MB + at * params : MB + (at + 1) * params] = part
-    for copy in layers_out:
-        copy.wait()
-
-
-def load_kernel(basis_ref, cell_ref, count_ref, after_ref, basis_out, cell_out, count_out, sems):
-    del after_ref
-    pairs = ((basis_ref, basis_out), (cell_ref, cell_out), (count_ref, count_out))
+    outer.wait()
+
+
+def load_kernel(last, basis_ref, cell_ref, count_ref, outer_ref, basis_out, cell_out, count_out, low_ref, high_ref, sems):
+    half = MB // 2
+    low, high = pl.ds(0, half), pl.ds(half, half)
+    beside = (1 - core()) * last
+    pairs = (
+        (basis_ref.at[low, beside], low_ref.at[low]),
+        (basis_ref.at[high, beside], high_ref),
+        (basis_ref, basis_out),
+        (cell_ref, cell_out),
+        (count_ref, count_out),
+    )
     copies = [pltpu.make_async_copy(source, out, sems.at[at]) for at, (source, out) in enumerate(pairs)]
     for copy in copies:
         copy.start()
+    low_ref[half:] = outer_ref[MB:]
     for copy in copies:
         copy.wait()
 
@@ -390,20 +390,16 @@
     tail = params * width_y
     hbm = pl.BlockSpec(memory_space=pltpu.HBM)
     planes = 2 * SPLITS * params
-    to_low, to_high, to_outer = pl.pallas_call(
+    to_outer = pl.pallas_call(
         functools.partial(pack_kernel, (params, layers)),
-        out_shape=(
-            shape((MB // 2 + planes, width_y, width_z), BF16),
-            shape((MB // 2, width_y, width_z), BF16),
-            shape((MB + planes, width_y, width_z), BF16),
-        ),
+        out_shape=shape((MB + planes, width_y, width_z), BF16),
         in_specs=[hbm] * 4,
-        out_specs=(VMEM,) * 3,
+        out_specs=VMEM,
         scratch_shapes=[
             pltpu.VMEM((params, width_y, width_z), F32),
             pltpu.VMEM((params, width_y, width_z), F32),
             pltpu.VMEM((params, width_y, width_z), I32),
-            pltpu.SemaphoreType.DMA((6,)),
+            pltpu.SemaphoreType.DMA((4,)),
         ],
         compiler_params=LIMIT,
         name="pack_halo",
@@ -412,20 +408,26 @@
     outer_pairs = []
     for i in range(1, devices - 1, 2):
         outer_pairs += [(i, i + 1), (i + 1, i)]
-    low = lax.ppermute(to_low, "cells", inner_pairs)
-    high = lax.ppermute(to_high, "cells", inner_pairs)
     outer = lax.ppermute(to_outer, "cells", outer_pairs)
 
-    loaded, cells_in, counts_in = pl.pallas_call(
-        load_kernel,
-        out_shape=(shape(basis.shape, BF16), shape((slots, devices), I32), shape((1, devices), I32)),
+    loaded, cells_in, counts_in, to_low, to_high = pl.pallas_call(
+        functools.partial(load_kernel, layers - 1),
+        out_shape=(
+            shape(basis.shape, BF16),
+            shape((slots, devices), I32),
+            shape((1, devices), I32),
+            shape((MB // 2 + planes, width_y, width_z), BF16),
+            shape((MB // 2, width_y, width_z), BF16),
+        ),
         in_specs=[hbm] * 3 + [VMEM],
-        out_specs=(VMEM,) * 3,
-        scratch_shapes=[pltpu.SemaphoreType.DMA((3,))],
+        out_specs=(VMEM,) * 5,
+        scratch_shapes=[pltpu.SemaphoreType.DMA((5,))],
         compiler_params=LIMIT,
         name="load",
     )(pltpu.with_memory_space_constraint(basis, pltpu.HBM), sample_cell[0].T, sample_count, to_outer)
     flat = loaded.reshape(modes, cells)
+    low = lax.ppermute(to_low, "cells", inner_pairs)
+    high = lax.ppermute(to_high, "cells", inner_pairs)
 
     block = slots * rows
     relative = [sum(((place >> (steps - 1 - step)) & 1) << step for step in range(steps)) for place in range(devices)]

time: 30.9 us -> 30.8 us (level)
  transfers between devices with their start and end apart: 8 -> 8, of which waited for: 5 -> 5; matrix products, arithmetic and copies ran while one was open for 2% -> 2% of each run, Pallas kernels for 13% -> 14%
where the time goes in v11:
time: 30.8 us; the launch traced here: 30.6 us
  starting transfers between devices  13.6 us (44%)
  waiting for transfers between devices  8.28 us (27%)
  Pallas kernels  7.1 us (23%)
  local copies, waits for them, and re-layouts  0.85 us (3%)
  between operations  0.77 us (2%)
    ppermute x3, starting transfers between devices, shards(): lax.ppermute(packets[at - 1], 'cells', [(i, i ^ mask) for i in range(devi...  4.45 us
    ppermute x1, starting transfers between devices, shards(): low = lax.ppermute(to_low, 'cells', inner_pairs)  4.38 us
    ppermute x2, waiting for transfers between devices, shards(): lax.ppermute(packet, 'cells', [(i, i ^ 1 << step) for i in range(devices)])  4.22 us
    ppermute x3, waiting for transfers between devices, shards(): lax.ppermute(packets[at - 1], 'cells', [(i, i ^ mask) for i in range(devi...  4.05 us
    ppermute x2, starting transfers between devices, shards(): lax.ppermute(packet, 'cells', [(i, i ^ 1 << step) for i in range(devices)])  3.99 us
    pallas_call x1, Pallas kernels, shards(): pl.pallas_call(functools.partial(load_kernel, layers - 1), out_shape=(sha...  1.81 us
    pallas_call x1, Pallas kernels, shards(): pl.pallas_call(functools.partial(local_kernel, (params, layers, width_y,...  1.52 us
    pallas_call x1, Pallas kernels, shards(): pl.pallas_call(functools.partial(pack_kernel, (params, layers)), out_shap...  1.05 us
  transfers between devices with their start and end apart: 8, of which 5 were waited for; matrix products, arithmetic and copies ran while one was open for 2% of the time, Pallas kernels for 14%

profile of v11, /device:TPU:0, one launch (start us, length us, event | category | flops | bytes accessed | tf_op | source)
XLA Modules:
  0.0 30.6 jit_solution(11376516968698418339)
XLA Ops:
  0.6 0.0 copy-start.6
  0.6 0.0 copy-start.5
  0.6 1.0 %pack_halo.1.outer_ref = bf16[136,8,128]{2,1,0:T(8,128)(2,1)S(1)} custom-call(bf16[512,2,8,128]{3,2,1,0:T(8,128)(2,1)} %basis_ref.3, f32[2,3,2,8,128]{4,3,2,1,0:T(8,128)} %speed_ref.3, f32[2,3,2,8,128]{4,3,2,1,0:T(8,128)} %diff_ref.3, s32[2,3,2,8,128]{4,3,2,1,0:T(8,128)} %flag_ref.3), custom_call_target="tpu_custom_call" | custom-call | tf_op jit(solution)/shard_map/pack_halo/pallas_call | solution.py:393
  1.7 0.7 %collective-permute-start = (bf16[136,8,128]{2,1,0:T(8,128)(2,1)S(1)}, bf16[136,8,128]{2,1,0:T(8,128)(2,1)S(1)}, u32[]{:S(2)}, u32[]{:S(2)}) collective-permute-start(bf16[136,8,128]{2,1,0:T(8,128)(2,1)S(1)} %pack_halo.1.outer_ref), channel_id=1, source_target_pairs={{1,2},{2,1},{3,4},{4,3},{5,6},{6,5},{7,8},{8,7},{9,10},{10,9},{11,... | collective-permute-start | bytes 835592 | tf_op jit(solution)/shard_map/ppermute | solution.py:411
  2.4 0.0 copy-done.6
  2.4 0.0 copy-done.5
  2.4 1.8 %load.1 = (bf16[512,2,8,128]{3,2,1,0:T(8,128)(2,1)S(1)}, s32[2,16]{1,0:T(2,128)S(1)}, s32[1,16]{1,0:T(1,128)S(1)}, bf16[72,8,128]{2,1,0:T(8,128)(2,1)S(1)}, bf16[64,8,128]{2,1,0:T(8,128)(2,1)S(1)}) custom-call(bf16[512,2,8,128]{3,2,1,0:T(8,128)(2,1)} %basis_ref.3, s32[2,16]{1,0:T(2,128)S(1)} %bitcast.18, s32[1,16]{1,0:T(1,128)S(1)} %copy-done.6, ...), custom_call_target="tpu_custom_call" | custom-call | tf_op jit(solution)/shard_map/load/pallas_call | solution.py:413
  4.2 4.4 %collective-permute-start.1 = (bf16[72,8,128]{2,1,0:T(8,128)(2,1)S(1)}, bf16[72,8,128]{2,1,0:T(8,128)(2,1)S(1)}, u32[]{:S(2)}, u32[]{:S(2)}) collective-permute-start(bf16[72,8,128]{2,1,0:T(8,128)(2,1)S(1)} %get-tuple-element.35), channel_id=1, source_target_pairs={{0,1},{1,0},{2,3},{3,2},{4,5},{5,4},{6,7},{7,6},{8,9},{9,8},{10,11... | collective-permute-start | bytes 442376 | tf_op jit(solution)/shard_map/ppermute | solution.py:429
  8.6 0.1 collective-permute-start.2
  8.7 0.0 copy-start
  8.7 0.0 copy-start.1
  8.7 0.0 copy-start.2
  8.7 0.0 copy-start.4
  8.7 0.6 %copy.12 = bf16[64,8,16,128]{3,1,2,0:T(8,128)(2,1)S(1)} copy(bf16[64,8,16,128]{3,2,1,0:T(8,128)(2,1)S(1)} %bitcast.17) | data formatting | bytes 4194304
  9.3 0.2 copy-done
  9.5 0.0 copy-done.1
  9.5 0.0 copy-done.2
  9.5 0.0 copy-done.4
  9.5 1.5 %local_stencil.1 = (f32[256,2048]{1,0:T(8,128)S(1)}, f32[2,8,128]{2,1,0:T(8,128)S(1)}, bf16[224,128]{1,0:T(8,128)(2,1)S(1)}, bf16[32,2048]{1,0:T(8,128)(2,1)S(1)}, s32[32,1]{1,0:T(8,128)S(1)}) custom-call(bf16[512,2048]{1,0:T(8,128)(2,1)S(1)} %bitcast.14, f32[2,3,2,8,128]{4,3,2,1,0:T(8,128)S(1)} %copy-done, f32[2,3,2,8,128]{4,3,2,1,0:T(8,128)S(1)} %copy-done.1, ...), custom_call_target="tpu_custom_call" | custom-call | flops 1 | bytes 1 | tf_op jit(solution)/shard_map/local_stencil/pallas_call | solution.py:450
  11.1 0.0 collective-permute-done.2.high_ref
  11.1 0.0 collective-permute-done.1.low_ref
  11.1 0.0 copy-start.3
  11.1 0.9 %near_layer.1 = (f32[512,256]{1,0:T(8,128)S(1)}, f32[32,256]{1,0:T(8,128)S(1)}, bf16[32,128]{1,0:T(8,128)(2,1)S(1)}) custom-call(bf16[512,2048]{1,0:T(8,128)(2,1)S(1)} %bitcast.15, bf16[72,8,128]{2,1,0:T(8,128)(2,1)S(1)} %collective-permute-done.1.low_ref, bf16[64,8,128]{2,1,0:T(8,128)(2,1)S(1)} %collective-permute-done.2.high_ref, ...), custom_call_target="tpu_custom_call" | custom-call | flops 1 | bytes 1 | tf_op jit(solution)/shard_map/near_layer/pallas_call | solution.py:476
  12.0 0.0 collective-permute-done.outer_ref
  12.0 0.0 copy-done.3
  12.0 1.0 %project.1 = (f32[512,128]{1,0:T(8,128)S(1)}, bf16[144,128]{1,0:T(8,128)(2,1)S(1)}, bf16[656,128]{1,0:T(8,128)(2,1)S(1)}) custom-call(bf16[512,2048]{1,0:T(8,128)(2,1)S(1)} %bitcast.16, bf16[136,8,128]{2,1,0:T(8,128)(2,1)S(1)} %collective-permute-done.outer_ref, f32[256,2048]{1,0:T(8,128)S(1)} %get-tuple-element.31.acc_ref, ...), custom_call_target="tpu_custom_call" | custom-call | tf_op jit(solution)/shard_map/project/pallas_call | solution.py:494
  13.1 1.2 %collective-permute-start.3 = (bf16[656,128]{1,0:T(8,128)(2,1)S(1)}, bf16[656,128]{1,0:T(8,128)(2,1)S(1)}, u32[]{:S(2)}, u32[]{:S(2)}) collective-permute-start(bf16[656,128]{1,0:T(8,128)(2,1)S(1)} %get-tuple-element.43), channel_id=1, source_target_pairs={{0,1},{1,0},{2,3},{3,2},{4,5},{5,4},{6,7},{7,6},{8,9},{9,8},{10,11... | collective-permute-start | bytes 503816 | tf_op jit(solution)/shard_map/ppermute | solution.py:526
  14.3 1.0 %collective-permute-done.3.got_ref = bf16[656,128]{1,0:T(8,128)(2,1)S(1)} collective-permute-done((bf16[656,128]{1,0:T(8,128)(2,1)S(1)}, bf16[656,128]{1,0:T(8,128)(2,1)S(1)}, u32[]{:S(2)}, u32[]{:S(2)}) %collective-permute-start.3) | collective-permute-done | bytes 167968 | tf_op jit(solution)/shard_map/ppermute | solution.py:526
  15.3 0.1 merge.1
  15.4 2.8 %collective-permute-start.4 = (bf16[400,128]{1,0:T(8,128)(2,1)S(1)}, bf16[400,128]{1,0:T(8,128)(2,1)S(1)}, u32[]{:S(2)}, u32[]{:S(2)}) collective-permute-start(bf16[400,128]{1,0:T(8,128)(2,1)S(1)} %get-tuple-element.46), channel_id=1, source_target_pairs={{0,2},{1,3},{2,0},{3,1},{4,6},{5,7},{6,4},{7,5},{8,10},{9,11},{10,... | collective-permute-start | bytes 307208 | tf_op jit(solution)/shard_map/ppermute | solution.py:526
  18.1 3.2 %collective-permute-done.4.got_ref = bf16[400,128]{1,0:T(8,128)(2,1)S(1)} collective-permute-done((bf16[400,128]{1,0:T(8,128)(2,1)S(1)}, bf16[400,128]{1,0:T(8,128)(2,1)S(1)}, u32[]{:S(2)}, u32[]{:S(2)}) %collective-permute-start.4) | collective-permute-done | bytes 102432 | tf_op jit(solution)/shard_map/ppermute | solution.py:526
  21.4 3.6 %collective-permute-start.5 = (bf16[144,128]{1,0:T(8,128)(2,1)S(1)}, bf16[144,128]{1,0:T(8,128)(2,1)S(1)}, u32[]{:S(2)}, u32[]{:S(2)}) collective-permute-start(bf16[144,128]{1,0:T(8,128)(2,1)S(1)} %get-tuple-element.49), channel_id=1, source_target_pairs={{0,12},{1,13},{2,14},{3,15},{4,8},{5,9},{6,10},{7,11},{8,4},{9,5},... | collective-permute-start | bytes 110600 | tf_op jit(solution)/shard_map/ppermute | solution.py:558
  25.0 0.0 collective-permute-start.6
  25.0 0.8 %collective-permute-start.7 = (bf16[144,128]{1,0:T(8,128)(2,1)S(1)}, bf16[144,128]{1,0:T(8,128)(2,1)S(1)}, u32[]{:S(2)}, u32[]{:S(2)}) collective-permute-start(bf16[144,128]{1,0:T(8,128)(2,1)S(1)} %get-tuple-element.51), channel_id=1, source_target_pairs={{0,8},{1,9},{2,10},{3,11},{4,12},{5,13},{6,14},{7,15},{8,0},{9,1},... | collective-permute-start | bytes 110600 | tf_op jit(solution)/shard_map/ppermute | solution.py:558
  25.8 1.4 %collective-permute-done.5.refs_0_ = bf16[144,128]{1,0:T(8,128)(2,1)S(1)} collective-permute-done((bf16[144,128]{1,0:T(8,128)(2,1)S(1)}, bf16[144,128]{1,0:T(8,128)(2,1)S(1)}, u32[]{:S(2)}, u32[]{:S(2)}) %collective-permute-start.5) | collective-permute-done | bytes 36896 | tf_op jit(solution)/shard_map/ppermute | solution.py:558
  27.2 1.7 %collective-permute-done.6.refs_1_ = bf16[144,128]{1,0:T(8,128)(2,1)S(1)} collective-permute-done((bf16[144,128]{1,0:T(8,128)(2,1)S(1)}, bf16[144,128]{1,0:T(8,128)(2,1)S(1)}, u32[]{:S(2)}, u32[]{:S(2)}) %collective-permute-start.6) | collective-permute-done | bytes 36896 | tf_op jit(solution)/shard_map/ppermute | solution.py:558
  29.0 0.9 %collective-permute-done.7.refs_2_ = bf16[144,128]{1,0:T(8,128)(2,1)S(1)} collective-permute-done((bf16[144,128]{1,0:T(8,128)(2,1)S(1)}, bf16[144,128]{1,0:T(8,128)(2,1)S(1)}, u32[]{:S(2)}, u32[]{:S(2)}) %collective-permute-start.7) | collective-permute-done | bytes 36896 | tf_op jit(solution)/shard_map/ppermute | solution.py:558
  29.9 0.7 %finish.1 = (f32[64,128]{1,0:T(8,128)}, bf16[288,128]{1,0:T(8,128)(2,1)}) custom-call(f32[64,128]{1,0:T(8,128)S(1)} %get-tuple-element.47.keep_ref, bf16[80,128]{1,0:T(8,128)(2,1)S(1)} %get-tuple-element.48.keep_rows_ref, bf16[144,128]{1,0:T(8,128)(2,1)S(1)} %collective-permute-done.5.refs_0_, bf16[144,128]{1,0:T(8,128)(2,1)S(1)} %collective-permute-done.6.refs_1_, ...), custom_call_target="tpu_custom_call" | custom-call | tf_op jit(solution)/shard_map/finish/pallas_call | solution.py:560
  (1 shorter events, 0.0 us)
Async XLA Ops:
  0.6 1.8 %copy-start.6 = (s32[1,16]{1,0:T(1,128)S(1)}, s32[1,16]{1,0:T(1,128)}, u32[]{:S(2)}) copy-start(s32[1,16]{1,0:T(1,128)} %count_ref.1) | copy-start | bytes 196
  0.6 1.8 %copy-start.5 = (s32[1,16,2]{1,2,0:T(2,128)S(1)}, s32[1,16,2]{1,2,0:T(2,128)}, u32[]{:S(2)}) copy-start(s32[1,16,2]{1,2,0:T(2,128)} %param.13) | copy-start | bytes 388
  1.7 10.3 %collective-permute-start = (bf16[136,8,128]{2,1,0:T(8,128)(2,1)S(1)}, bf16[136,8,128]{2,1,0:T(8,128)(2,1)S(1)}, u32[]{:S(2)}, u32[]{:S(2)}) collective-permute-start(bf16[136,8,128]{2,1,0:T(8,128)(2,1)S(1)} %pack_halo.1.outer_ref), channel_id=1, source_target_pairs={{1,2},{2,1},{3,4},{4,3},{5,6},{6,5},{7,8},{8,7},{9,10},{10,9},{11,... | collective-permute-start | bytes 835592 | tf_op jit(solution)/shard_map/ppermute | solution.py:411
  4.2 6.8 %collective-permute-start.1 = (bf16[72,8,128]{2,1,0:T(8,128)(2,1)S(1)}, bf16[72,8,128]{2,1,0:T(8,128)(2,1)S(1)}, u32[]{:S(2)}, u32[]{:S(2)}) collective-permute-start(bf16[72,8,128]{2,1,0:T(8,128)(2,1)S(1)} %get-tuple-element.35), channel_id=1, source_target_pairs={{0,1},{1,0},{2,3},{3,2},{4,5},{5,4},{6,7},{7,6},{8,9},{9,8},{10,11... | collective-permute-start | bytes 442376 | tf_op jit(solution)/shard_map/ppermute | solution.py:429
  8.6 2.5 %collective-permute-start.2 = (bf16[64,8,128]{2,1,0:T(8,128)(2,1)S(1)}, bf16[64,8,128]{2,1,0:T(8,128)(2,1)S(1)}, u32[]{:S(2)}, u32[]{:S(2)}) collective-permute-start(bf16[64,8,128]{2,1,0:T(8,128)(2,1)S(1)} %get-tuple-element.36), channel_id=1, source_target_pairs={{0,1},{1,0},{2,3},{3,2},{4,5},{5,4},{6,7},{7,6},{8,9},{9,8},{10,11... | collective-permute-start | bytes 393224 | tf_op jit(solution)/shard_map/ppermute | solution.py:430
  8.7 0.8 %copy-start = (f32[2,3,2,8,128]{4,3,2,1,0:T(8,128)S(1)}, f32[2,3,2,8,128]{4,3,2,1,0:T(8,128)}, u32[]{:S(2)}) copy-start(f32[2,3,2,8,128]{4,3,2,1,0:T(8,128)} %speed_ref.3) | copy-start | bytes 147460
  8.7 0.8 %copy-start.1 = (f32[2,3,2,8,128]{4,3,2,1,0:T(8,128)S(1)}, f32[2,3,2,8,128]{4,3,2,1,0:T(8,128)}, u32[]{:S(2)}) copy-start(f32[2,3,2,8,128]{4,3,2,1,0:T(8,128)} %diff_ref.3) | copy-start | bytes 147460
  8.7 0.8 %copy-start.2 = (s32[2,3,2,8,128]{4,3,2,1,0:T(8,128)S(1)}, s32[2,3,2,8,128]{4,3,2,1,0:T(8,128)}, u32[]{:S(2)}) copy-start(s32[2,3,2,8,128]{4,3,2,1,0:T(8,128)} %flag_ref.3) | copy-start | bytes 147460
  8.7 0.8 %copy-start.4 = (f32[2,2,8,128]{3,2,1,0:T(8,128)S(1)}, f32[2,2,8,128]{3,2,1,0:T(8,128)}, u32[]{:S(2)}) copy-start(f32[2,2,8,128]{3,2,1,0:T(8,128)} %react_ref.1) | copy-start | bytes 49156
  11.1 0.9 %copy-start.3 = (s32[288,8]{1,0:T(8,128)S(1)}, s32[288,8]{1,0:T(8,128)}, u32[]{:S(2)}) copy-start(s32[288,8]{1,0:T(8,128)} %constant.2.clone.table_ref) | copy-start | bytes 27652
  13.1 2.2 %collective-permute-start.3 = (bf16[656,128]{1,0:T(8,128)(2,1)S(1)}, bf16[656,128]{1,0:T(8,128)(2,1)S(1)}, u32[]{:S(2)}, u32[]{:S(2)}) collective-permute-start(bf16[656,128]{1,0:T(8,128)(2,1)S(1)} %get-tuple-element.43), channel_id=1, source_target_pairs={{0,1},{1,0},{2,3},{3,2},{4,5},{5,4},{6,7},{7,6},{8,9},{9,8},{10,11... | collective-permute-start | bytes 503816 | tf_op jit(solution)/shard_map/ppermute | solution.py:526
  15.4 6.0 %collective-permute-start.4 = (bf16[400,128]{1,0:T(8,128)(2,1)S(1)}, bf16[400,128]{1,0:T(8,128)(2,1)S(1)}, u32[]{:S(2)}, u32[]{:S(2)}) collective-permute-start(bf16[400,128]{1,0:T(8,128)(2,1)S(1)} %get-tuple-element.46), channel_id=1, source_target_pairs={{0,2},{1,3},{2,0},{3,1},{4,6},{5,7},{6,4},{7,5},{8,10},{9,11},{10,... | collective-permute-start | bytes 307208 | tf_op jit(solution)/shard_map/ppermute | solution.py:526
  21.4 5.9 %collective-permute-start.5 = (bf16[144,128]{1,0:T(8,128)(2,1)S(1)}, bf16[144,128]{1,0:T(8,128)(2,1)S(1)}, u32[]{:S(2)}, u32[]{:S(2)}) collective-permute-start(bf16[144,128]{1,0:T(8,128)(2,1)S(1)} %get-tuple-element.49), channel_id=1, source_target_pairs={{0,12},{1,13},{2,14},{3,15},{4,8},{5,9},{6,10},{7,11},{8,4},{9,5},... | collective-permute-start | bytes 110600 | tf_op jit(solution)/shard_map/ppermute | solution.py:558
  25.0 4.0 %collective-permute-start.6 = (bf16[144,128]{1,0:T(8,128)(2,1)S(1)}, bf16[144,128]{1,0:T(8,128)(2,1)S(1)}, u32[]{:S(2)}, u32[]{:S(2)}) collective-permute-start(bf16[144,128]{1,0:T(8,128)(2,1)S(1)} %get-tuple-element.50), channel_id=1, source_target_pairs={{0,4},{1,5},{2,6},{3,7},{4,0},{5,1},{6,2},{7,3},{8,12},{9,13},{10,... | collective-permute-start | bytes 110600 | tf_op jit(solution)/shard_map/ppermute | solution.py:558
  25.0 4.9 %collective-permute-start.7 = (bf16[144,128]{1,0:T(8,128)(2,1)S(1)}, bf16[144,128]{1,0:T(8,128)(2,1)S(1)}, u32[]{:S(2)}, u32[]{:S(2)}) collective-permute-start(bf16[144,128]{1,0:T(8,128)(2,1)S(1)} %get-tuple-element.51), channel_id=1, source_target_pairs={{0,8},{1,9},{2,10},{3,11},{4,12},{5,13},{6,14},{7,15},{8,0},{9,1},... | collective-permute-start | bytes 110600 | tf_op jit(solution)/shard_map/ppermute | solution.py:558
